TPU v7x, 256 devices: a whole 4x4x8 slice. The times are simulated.
256 devices in a mesh: space: 16 (over z_hi, x, core), tm: 16 (over z_lo, y).
Axes of the slice: x: 4, y: 4, z: 8 (z_hi: 2, z_lo: 4; z = z_hi * 4 + z_lo), core: 2. Of those that a mesh axis runs over, the one named last changes fastest.
Arguments:
- query_space: bfloat16 [2, 16, 1024, 2048], P(None, 'tm', 'space'), may hold values from -10 to 10
- key_space: bfloat16 [2, 16, 1024, 2048], P(None, 'tm', 'space'), may hold values from -10 to 10
- value_space: bfloat16 [2, 16, 1024, 2048], P(None, 'tm', 'space'), may hold values from -6 to 6
- query_time: bfloat16 [2, 16, 1024, 2048], P(None, 'tm', 'space'), may hold values from -10 to 10
- key_time: bfloat16 [2, 16, 1024, 2048], P(None, 'tm', 'space'), may hold values from -10 to 10
- value_time: bfloat16 [2, 16, 1024, 2048], P(None, 'tm', 'space'), may hold values from -6 to 6
- block_grad: bfloat16 [2, 16, 1024, 2048], P(None, 'tm', 'space'), may hold values from -6 to 6
- branch_grad: bfloat16 [2, 16, 1024, 2048], P(None, 'tm', 'space'), may hold values from -6 to 6
- proj_space: bfloat16 [2048, 2048], P('space'), may hold values from -0.5 to 0.5
- proj_time: bfloat16 [2048, 2048], P('tm'), may hold values from -0.5 to 0.5
Outputs:
- grad_query_space: bfloat16 [2, 16, 1024, 2048], P(None, 'tm', 'space')
- grad_key_space: bfloat16 [2, 16, 1024, 2048], P(None, 'tm', 'space')
- grad_value_space: bfloat16 [2, 16, 1024, 2048], P(None, 'tm', 'space')
- grad_query_time: bfloat16 [2, 16, 1024, 2048], P(None, 'tm', 'space')
- grad_key_time: bfloat16 [2, 16, 1024, 2048], P(None, 'tm', 'space')
- grad_value_time: bfloat16 [2, 16, 1024, 2048], P(None, 'tm', 'space')
All inputs are finite; a program needn't handle non-finite values.
Results may differ from a plain program's by a relative error of at most 0.011.
Values may be sent and summed in bfloat16 or wider, within the bound.
No kernel may reach another device: no remote copies, remote signals or barrier semaphores. Data moves between devices by JAX's collectives and lax.ppermute only.
A program may use at most 128 MiB of HBM per device.

v0:
```python
import math

import jax
import jax.numpy as jnp
from jax import lax
from jax.experimental import pallas as pl
from jax.experimental.pallas import tpu as pltpu
from jax.sharding import PartitionSpec as P

HEAD_DIM = 128
SCALE = 1.0 / math.sqrt(HEAD_DIM)
LOG2E = math.log2(math.e)
VMEM = 48 * 1024 * 1024
BF16 = jnp.bfloat16
F32 = jnp.float32


def permutation(move):
    pairs = []
    for s in range(16):
        for t in range(16):
            z, x, y, c = (s // 8) * 4 + t // 4, (s // 2) % 4, t % 4, s % 2
            z2, x2, y2, c2 = move(z, x, y, c)
            z2, x2, y2, c2 = z2 % 8, x2 % 4, y2 % 4, c2 % 2
            pairs.append((s * 16 + t, ((z2 // 4) * 8 + x2 * 2 + c2) * 16 + (z2 % 4) * 4 + y2))
    return pairs


def send(array, move):
    return lax.ppermute(array, ("space", "tm"), permutation(move))


def nt(a, b):
    return lax.dot_general(a, b, (((1,), (1,)), ((), ())), preferred_element_type=F32)


def nn(a, b):
    return lax.dot_general(a, b, (((1,), (0,)), ((), ())), preferred_element_type=F32)


def call(kernel, out_shape, flops, size, **kw):
    return pl.pallas_call(
        kernel,
        out_shape=out_shape,
        compiler_params=pltpu.CompilerParams(vmem_limit_bytes=VMEM),
        cost_estimate=pl.CostEstimate(flops=flops, bytes_accessed=size, transcendentals=0),
        **kw,
    )


def pack_kernel(a_ref, b_ref, c_ref, out_ref):
    for t, ref in enumerate((a_ref, b_ref, c_ref)):
        for h in range(16):
            out_ref[h, t] = ref[:, h * 128 : (h + 1) * 128]


def pack(a, b, c):
    flat = [v.reshape(128, 2048) for v in (a, b, c)]
    out = call(pack_kernel, jax.ShapeDtypeStruct((16, 3, 128, 128), BF16), 0, 3 << 20)(*flat)
    return out.reshape(16, 3, 2, 64, 128)


def unpack_kernel(in_ref, a_ref, b_ref, c_ref):
    for t, ref in enumerate((a_ref, b_ref, c_ref)):
        for h in range(16):
            ref[:, h * 128 : (h + 1) * 128] = in_ref[h, t]


def unpack(array):
    shape = jax.ShapeDtypeStruct((128, 2048), BF16)
    outs = call(unpack_kernel, (shape,) * 3, 0, 3 << 20)(array.reshape(16, 3, 128, 128))
    return tuple(v.reshape(2, 1, 64, 2048) for v in outs)


def space_proj_kernel(pos_ref, *refs):
    shards, w_own, w_other, keep, other = refs[:8], refs[8], refs[9], refs[10], refs[11]
    weight = jnp.concatenate([w_own[...], w_other[...]], axis=0)
    for i in range(8):
        at = pos_ref[0] ^ i
        out = nt(shards[i][...], weight).astype(BF16)
        keep[at] = out[:, :128]
        other[at] = out[:, 128:]


def space_proj(pos, shards, w_own, w_other):
    shape = jax.ShapeDtypeStruct((8, 128, 128), BF16)
    vmem = pl.BlockSpec(memory_space=pltpu.VMEM)
    return call(
        space_proj_kernel,
        (shape, shape),
        1 << 30,
        6 << 20,
        in_specs=[pl.BlockSpec(memory_space=pltpu.SMEM)] + [vmem] * 10,
    )(pos, *shards, w_own, w_other)


def time_proj_kernel(pos_ref, *refs):
    shards, own, pieces, outs, weight_ref = refs[:4], refs[4], refs[5:13], refs[13:17], refs[17]
    weight_ref[:128] = own[...]
    for i in range(8):
        for k in range(3):
            row = 128 * (k + 1) + (pos_ref[1] ^ i) * 16
            weight_ref[pl.ds(pl.multiple_of(row, 16), 16)] = pieces[i][k]
    for i in range(4):
        out = nt(shards[i][...], weight_ref[...]).astype(BF16)
        for k in range(4):
            outs[k][pos_ref[0] ^ i] = out[:, k * 128 : (k + 1) * 128]


def time_proj(pos, shards, own, pieces):
    shape = jax.ShapeDtypeStruct((4, 128, 128), BF16)
    vmem = pl.BlockSpec(memory_space=pltpu.VMEM)
    return call(
        time_proj_kernel,
        (shape,) * 4,
        1 << 30,
        5 << 20,
        in_specs=[pl.BlockSpec(memory_space=pltpu.SMEM)] + [vmem] * 13,
        scratch_shapes=[pltpu.VMEM((512, 2048), BF16)],
    )(pos, *shards, own, *pieces)


def attend(q, k, v, o, k_t, mask):
    s = nt(k, q)
    if mask is not None:
        s = jnp.where(mask, s, -1e30)
    e = jnp.exp2((s - jnp.max(s, axis=0, keepdims=True)) * (SCALE * LOG2E))
    p = e * (1.0 / jnp.sum(e, axis=0, keepdims=True))
    dv = nn(p.astype(BF16), o)
    dp = nt(v, o)
    delta = jnp.sum(p * dp, axis=0, keepdims=True)
    ds = (p * (dp - delta)).astype(BF16)
    dk = nn(ds, q)
    dq_t = nn(k_t, ds)
    return dq_t, dk, dv


def space_kernel(pos_ref, qkv_ref, keep_ref, got_ref, out_ref, o_ref, dk_ref, dv_ref):
    z_hi = pos_ref[0]
    o_ref[pl.ds(pl.multiple_of(z_hi * 512, 512), 512), :] = keep_ref[...].reshape(512, 128)
    o_ref[pl.ds(pl.multiple_of((1 - z_hi) * 512, 512), 512), :] = got_ref[...].reshape(512, 128)
    k = qkv_ref[:, 1].reshape(1024, 128)
    v = qkv_ref[:, 2].reshape(1024, 128)
    k_t = k.T
    chunk = 256
    for j in range(1024 // chunk):
        n = chunk // 64
        q = qkv_ref[j * n : (j + 1) * n, 0].reshape(chunk, 128)
        o = o_ref[j * chunk : (j + 1) * chunk, :]
        dq_t, dk, dv = attend(q, k, v, o, k_t, None)
        out_ref[j * n : (j + 1) * n, 0] = (dq_t * SCALE).T.astype(BF16).reshape(n, 1, 64, 128)
        if j:
            dk_ref[...] += dk
            dv_ref[...] += dv
        else:
            dk_ref[...] = dk
            dv_ref[...] = dv
    out_ref[:, 1] = (dk_ref[...] * SCALE).astype(BF16).reshape(16, 1, 64, 128)
    out_ref[:, 2] = dv_ref[...].astype(BF16).reshape(16, 1, 64, 128)


def space_attention(z_hi, qkv, keep, got):
    whole = pl.BlockSpec((16, 3, 1, 64, 128), lambda b: (0, 0, b, 0, 0))
    half = pl.BlockSpec((8, 1, 64, 128), lambda b: (0, b, 0, 0))
    return call(
        space_kernel,
        jax.ShapeDtypeStruct((16, 3, 2, 64, 128), BF16),
        5 * (1 << 29),
        4 << 20,
        grid=(2,),
        in_specs=[pl.BlockSpec(memory_space=pltpu.SMEM), whole, half, half],
        out_specs=whole,
        scratch_shapes=[
            pltpu.VMEM((1024, 128), BF16),
            pltpu.VMEM((1024, 128), F32),
            pltpu.VMEM((1024, 128), F32),
        ],
    )(z_hi, qkv, keep, got)


def time_kernel(pos_ref, qkv_ref, *refs):
    parts, out_ref, o_ref = refs[:4], refs[4], refs[5]
    for i in range(4):
        o_ref[pl.ds(((pos_ref[0] - i) & 3) * 4, 4)] = parts[i][:, 0]
    rows = lax.broadcasted_iota(jnp.int32, (256, 256), 0)
    columns = lax.broadcasted_iota(jnp.int32, (256, 256), 1)
    mask = ((rows ^ columns) & 15) == 0
    for i in range(4):
        at = slice(16 * i, 16 * (i + 1))
        q = qkv_ref[:, 0, 0, at].reshape(256, 128)
        k = qkv_ref[:, 1, 0, at].reshape(256, 128)
        v = qkv_ref[:, 2, 0, at].reshape(256, 128)
        o = o_ref[:, at].reshape(256, 128)
        dq_t, dk, dv = attend(q, k, v, o, k.T, mask)
        out_ref[:, 0, 0, at] = (dq_t * SCALE).T.astype(BF16).reshape(16, 16, 128)
        out_ref[:, 1, 0, at] = (dk * SCALE).astype(BF16).reshape(16, 16, 128)
        out_ref[:, 2, 0, at] = dv.astype(BF16).reshape(16, 16, 128)


def time_attention(z_lo, qkv, parts):
    whole = pl.BlockSpec((16, 3, 1, 64, 128), lambda b: (0, 0, b, 0, 0))
    quarter = pl.BlockSpec((4, 1, 64, 128), lambda b: (0, b, 0, 0))
    return call(
        time_kernel,
        jax.ShapeDtypeStruct((16, 3, 2, 64, 128), BF16),
        5 * (1 << 27),
        4 << 20,
        grid=(2,),
        in_specs=[pl.BlockSpec(memory_space=pltpu.SMEM), whole] + [quarter] * 4,
        out_specs=whole,
        scratch_shapes=[pltpu.VMEM((16, 64, 128), BF16)],
    )(z_lo, qkv, *parts)


def exchange(array, axis):
    return lax.all_to_all(array, axis, split_axis=0, concat_axis=0, tiled=True)


def on_device(
    query_space,
    key_space,
    value_space,
    query_time,
    key_time,
    value_time,
    block_grad,
    branch_grad,
    proj_space,
    proj_time,
):
    place_s, place_t = lax.axis_index("space"), lax.axis_index("tm")
    z_hi, xc = place_s // 8, place_s % 8
    z_lo, y = place_t // 4, place_t % 4

    time_in = exchange(pack(query_time, key_time, value_time), "tm")

    rows = lax.dynamic_slice_in_dim(proj_time, xc * 16, 16, 0)
    piece = jnp.stack(
        [
            send(rows, lambda z, x, y, c: (z - 1, x, y, c)),
            send(rows, lambda z, x, y, c: (z + 2 - 4 * c, x, y, c)),
            send(rows, lambda z, x, y, c: (z + 1, x, y, c)),
        ]
    )
    along_x = [piece] + [send(piece, lambda z, x, y, c, k=k: (z, x ^ k, y, c)) for k in (1, 2, 3)]
    twins = [send(p, lambda z, x, y, c: (z, x, y, 1 - c)) for p in along_x]
    pieces = [(along_x, twins)[i % 2][i // 2] for i in range(8)]

    cotangent = (block_grad.astype(F32) + branch_grad.astype(F32)).astype(BF16).reshape(128, 2048)
    along_y = [cotangent] + [
        send(cotangent, lambda z, x, y, c, k=k: (z, x, y ^ k, c)) for k in (1, 2, 3)
    ]

    grad = block_grad.reshape(128, 2048)
    along_x = [grad] + [send(grad, lambda z, x, y, c, k=k: (z, x ^ k, y, c)) for k in (1, 2, 3)]
    twins = [send(g, lambda z, x, y, c: (z, x, y, 1 - c)) for g in along_x]
    shards = [(along_x, twins)[i % 2][i // 2] for i in range(8)]
    w_other = send(proj_space, lambda z, x, y, c: (z + (-2 if z % 4 < 2 else 2), x, y, c))

    space_packed = pack(query_space, key_space, value_space)
    time_in, pieces, along_y, shards, w_other, space_packed = lax.optimization_barrier(
        (time_in, pieces, along_y, shards, w_other, space_packed)
    )

    space_in = exchange(space_packed, "space")
    outs = time_proj(jnp.stack([y, xc]), along_y, proj_time, pieces)
    parts = [outs[0]] + [
        lax.ppermute(
            outs[k], "tm", [(t, (t // 4 + k) % 4 * 4 + t % 4) for t in range(16)]
        )
        for k in (1, 2, 3)
    ]
    keep, other = space_proj(xc.reshape(1), shards, proj_space, w_other)
    got = send(other, lambda z, x, y, c: (z + 4, x, y, c))
    time_grads = time_attention(
        z_lo.reshape(1), time_in, [p.reshape(4, 2, 64, 128) for p in parts]
    )
    space_in, keep, got, time_grads = lax.optimization_barrier((space_in, keep, got, time_grads))

    time_out = exchange(time_grads, "tm")
    space_grads = space_attention(
        z_hi.reshape(1), space_in, keep.reshape(8, 2, 64, 128), got.reshape(8, 2, 64, 128)
    )
    time_out, space_grads = lax.optimization_barrier((time_out, space_grads))
    space_out = exchange(space_grads, "space")
    return unpack(space_out) + unpack(time_out)


def solution(mesh):
    tokens = P(None, "tm", "space", None)
    in_specs = (tokens,) * 8 + (P("space", None), P("tm", None))
    return jax.shard_map(
        on_device, mesh=mesh, in_specs=in_specs, out_specs=(tokens,) * 6, check_vma=False
    )
```

profile of v0, /device:TPU:38, one launch (start us, length us, event | category | flops | bytes accessed | tf_op | source)
XLA Modules:
  0.0 291.4 jit_solution(14501729014069223993)
XLA Ops:
  0.6 1.0 copy-done.9
  1.7 1.0 copy-done.10
  2.7 1.0 copy-done.11
  3.8 1.4 shard_map.145
  5.2 8.8 %all-to-all-start = ((bf16[16,3,2,64,128]{4,3,2,1,0:T(8,128)(2,1)}), bf16[16,3,2,64,128]{4,3,2,1,0:T(8,128)(2,1)S(1)}, u32[]{:S(2)}, u32[]{:S(2)}) async-start(bf16[16,3,2,64,128]{4,3,2,1,0:T(8,128)(2,1)} %bitcast.3), calls=%async_computation | async-start | bytes 3145728 | tf_op jit(solution)/shard_map/all_to_all | solution.py:216
  14.2 2.8 collective-permute-start.1
  17.0 2.7 collective-permute-start.2
  19.7 32.6 %collective-permute-done = bf16[16,2048]{1,0:T(8,128)(2,1)S(1)} collective-permute-done((bf16[16,2048]{1,0:T(8,128)(2,1)S(1)}, bf16[16,2048]{1,0:T(8,128)(2,1)S(1)}, u32[]{:S(2)}, u32[]{:S(2)}) %collective-permute-start) | collective-permute-done | bytes 65568 | tf_op jit(solution)/shard_map/ppermute | solution.py:30
  52.4 0.9 collective-permute-start.4
  53.3 1.1 collective-permute-start.6
  54.4 2.8 collective-permute-start.8
  57.2 3.1 %collective-permute-done.4.refs_7_ = bf16[3,16,2048]{2,1,0:T(8,128)(2,1)S(1)} collective-permute-done((bf16[3,16,2048]{2,1,0:T(8,128)(2,1)S(1)}, bf16[3,16,2048]{2,1,0:T(8,128)(2,1)S(1)}, u32[]{:S(2)}, u32[]{:S(2)}) %collective-permute-start.4) | collective-permute-done | bytes 196640 | tf_op jit(solution)/shard_map/ppermute | solution.py:30
  60.3 4.0 %collective-permute-done.6.refs_9_ = bf16[3,16,2048]{2,1,0:T(8,128)(2,1)S(1)} collective-permute-done((bf16[3,16,2048]{2,1,0:T(8,128)(2,1)S(1)}, bf16[3,16,2048]{2,1,0:T(8,128)(2,1)S(1)}, u32[]{:S(2)}, u32[]{:S(2)}) %collective-permute-start.6) | collective-permute-done | bytes 196640 | tf_op jit(solution)/shard_map/ppermute | solution.py:30
  64.8 1.2 add_convert_fusion
  66.7 2.6 collective-permute-start.16
  69.9 1.1 collective-permute-start.18
  72.4 1.4 collective-permute-start.10
  73.8 1.2 collective-permute-done.14.refs_2_
  75.0 3.1 %collective-permute-start.11 = (bf16[128,2048]{1,0:T(8,128)(2,1)S(1)}, bf16[128,2048]{1,0:T(8,128)(2,1)S(1)}, u32[]{:S(2)}, u32[]{:S(2)}) collective-permute-start(bf16[128,2048]{1,0:T(8,128)(2,1)S(1)} %bitcast.46), channel_id=1, source_target_pairs={{0,2},{1,3},{2,0},{3,1},{4,6},{5,7},{6,4},{7,5},{8,10},{9,11},{10,... | collective-permute-start | bytes 1572872 | tf_op jit(solution)/shard_map/ppermute | solution.py:30
  78.0 6.3 %collective-permute-done.16.refs_4_ = bf16[128,2048]{1,0:T(8,128)(2,1)S(1)} collective-permute-done((bf16[128,2048]{1,0:T(8,128)(2,1)S(1)}, bf16[128,2048]{1,0:T(8,128)(2,1)S(1)}, u32[]{:S(2)}, u32[]{:S(2)}) %collective-permute-start.16) | collective-permute-done | bytes 524320 | tf_op jit(solution)/shard_map/ppermute | solution.py:30
  84.4 2.8 collective-permute-start.12
  87.1 7.6 %collective-permute-done.18.refs_6_ = bf16[128,2048]{1,0:T(8,128)(2,1)S(1)} collective-permute-done((bf16[128,2048]{1,0:T(8,128)(2,1)S(1)}, bf16[128,2048]{1,0:T(8,128)(2,1)S(1)}, u32[]{:S(2)}, u32[]{:S(2)}) %collective-permute-start.18) | collective-permute-done | bytes 524320 | tf_op jit(solution)/shard_map/ppermute | solution.py:30
  95.5 0.8 copy-done.16
  96.3 0.8 copy-done.3
  98.4 1.8 collective-permute-done.11.refs_2_
  100.3 0.8 copy-done.5
  101.9 1.0 copy-done.12
  102.9 1.0 copy-done.13
  104.0 1.0 copy-done.14
  105.0 1.4 shard_map.146
  106.4 2.2 collective-permute-done.12.refs_3_
  108.6 0.8 copy-done.7
  109.5 12.0 %collective-permute-done.20.refs_9_ = bf16[128,2048]{1,0:T(8,128)(2,1)S(1)} collective-permute-done((bf16[128,2048]{1,0:T(8,128)(2,1)}, bf16[128,2048]{1,0:T(8,128)(2,1)S(1)}, u32[]{:S(2)}, u32[]{:S(2)}) %collective-permute-start.20) | collective-permute-done | bytes 524320 | tf_op jit(solution)/shard_map/ppermute | solution.py:30
  121.5 0.8 copy-done.24
  122.3 0.8 copy-done.26
  123.1 0.8 copy-done.28
  123.9 0.8 copy-done.30
  124.7 5.9 %all-to-all-start.1 = ((bf16[16,3,2,64,128]{4,3,2,1,0:T(8,128)(2,1)}), bf16[16,3,2,64,128]{4,3,2,1,0:T(8,128)(2,1)}, u32[]{:S(2)}, u32[]{:S(2)}) async-start(bf16[16,3,2,64,128]{4,3,2,1,0:T(8,128)(2,1)} %bitcast.12), calls=%async_computation.1 | async-start | bytes 3145728 | tf_op jit(solution)/shard_map/all_to_all | solution.py:216
  130.7 1.0 copy-done.15
  131.7 1.0 copy-done.17
  132.8 1.0 copy-done.19
  133.8 1.0 copy-done.21
  134.9 1.0 copy-done.23
  135.9 1.0 copy-done.25
  136.9 1.0 copy-done.27
  138.0 1.0 copy-done.29
  139.0 1.0 copy-done.31
  140.1 3.5 %shard_map.147 = (bf16[8,128,128]{2,1,0:T(8,128)(2,1)S(1)}, bf16[8,128,128]{2,1,0:T(8,128)(2,1)}) custom-call(s32[1]{0:T(128)} %bitcast.13.pos_ref, bf16[128,2048]{1,0:T(8,128)(2,1)S(1)} %bitcast.53, bf16[128,2048]{1,0:T(8,128)(2,1)S(1)} %copy-done.23, bf16[128,2048]{1,0:T(8,128)(2,1)S(1)} %copy-done.17, bf16[128,2048]{1,0:T(8,128)(2,1)S(1)} %copy-done.27, ...), custom_call_target="tpu_custom_call" | custom-call | flops 1073741824 | bytes 6291456 | tf_op jit(solution)/shard_map/pallas_call | solution.py:88
  143.6 5.4 %collective-permute-start.21 = (bf16[8,128,128]{2,1,0:T(8,128)(2,1)}, bf16[8,128,128]{2,1,0:T(8,128)(2,1)S(1)}, u32[]{:S(2)}, u32[]{:S(2)}) collective-permute-start(bf16[8,128,128]{2,1,0:T(8,128)(2,1)} %get-tuple-element.58), channel_id=1, source_target_pairs={{0,128},{1,129},{2,130},{3,131},{4,132},{5,133},{6,134},{7,135},{8... | collective-permute-start | bytes 786440 | tf_op jit(solution)/shard_map/ppermute | solution.py:30
  149.1 4.3 %shard_map.148 = (bf16[4,128,128]{2,1,0:T(8,128)(2,1)S(1)}, bf16[4,128,128]{2,1,0:T(8,128)(2,1)}, bf16[4,128,128]{2,1,0:T(8,128)(2,1)}, bf16[4,128,128]{2,1,0:T(8,128)(2,1)S(1)}) custom-call(s32[2]{0:T(128)S(1)} %pad_add_fusion.pos_ref, bf16[128,2048]{1,0:T(8,128)(2,1)S(1)} %bitcast.48, bf16[128,2048]{1,0:T(8,128)(2,1)S(1)} %copy-done.4, ...), custom_call_target="tpu_custom_call" | custom-call | flops 1073741824 | bytes 5242880 | tf_op jit(solution)/shard_map/pallas_call | solution.py:113
  153.5 0.8 collective-permute-start.22
  154.3 1.0 collective-permute-start.23
  155.8 25.2 %collective-permute-done.22 = bf16[4,128,128]{2,1,0:T(8,128)(2,1)S(1)} collective-permute-done((bf16[4,128,128]{2,1,0:T(8,128)(2,1)}, bf16[4,128,128]{2,1,0:T(8,128)(2,1)S(1)}, u32[]{:S(2)}, u32[]{:S(2)}) %collective-permute-start.22) | collective-permute-done | bytes 131104 | tf_op jit(solution)/shard_map/ppermute | solution.py:268
  181.0 6.7 %collective-permute-done.23 = bf16[4,128,128]{2,1,0:T(8,128)(2,1)S(1)} collective-permute-done((bf16[4,128,128]{2,1,0:T(8,128)(2,1)}, bf16[4,128,128]{2,1,0:T(8,128)(2,1)S(1)}, u32[]{:S(2)}, u32[]{:S(2)}) %collective-permute-start.23) | collective-permute-done | bytes 131104 | tf_op jit(solution)/shard_map/ppermute | solution.py:268
  187.7 1.5 collective-permute-done.24
  189.3 5.3 %shard_map.149 = bf16[16,3,2,64,128]{4,3,2,1,0:T(8,128)(2,1)} custom-call(s32[1]{0:T(128)} %bitcast.14.pos_ref, bf16[16,3,2,64,128]{4,3,2,1,0:T(8,128)(2,1)S(1)} %all-to-all-done.qkv_ref, bf16[4,2,64,128]{3,2,1,0:T(8,128)(2,1)S(1)} %bitcast.60, bf16[4,2,64,128]{3,2,1,0:T(8,128)(2,1)S(1)} %bitcast.61, bf16[4,2,64,128]{3,2,1,0:T(8,128)(2,1)S(1)} %bitcast.62, ...), custom_call_target="tpu_custom_call" | custom-call | flops 671088640 | bytes 4194304 | tf_op jit(solution)/shard_map/pallas_call | solution.py:203
  194.6 7.2 %all-to-all-start.2 = ((bf16[16,3,2,64,128]{4,3,2,1,0:T(8,128)(2,1)}), bf16[16,3,2,64,128]{4,3,2,1,0:T(8,128)(2,1)S(1)}, u32[]{:S(2)}, u32[]{:S(2)}) async-start(bf16[16,3,2,64,128]{4,3,2,1,0:T(8,128)(2,1)} %shard_map.149), calls=%async_computation.2 | async-start | bytes 3145728 | tf_op jit(solution)/shard_map/all_to_all | solution.py:216
  201.7 10.9 %shard_map.150 = bf16[16,3,2,64,128]{4,3,2,1,0:T(8,128)(2,1)S(1)} custom-call(s32[1]{0:T(128)} %bitcast.20.pos_ref, bf16[16,3,2,64,128]{4,3,2,1,0:T(8,128)(2,1)} %all-to-all-done.1.qkv_ref, bf16[8,2,64,128]{3,2,1,0:T(8,128)(2,1)S(1)} %bitcast.64, bf16[8,2,64,128]{3,2,1,0:T(8,128)(2,1)S(1)} %bitcast.65), custom_call_target="tpu_custom_call" | custom-call | flops 2684354560 | bytes 4194304 | tf_op jit(solution)/shard_map/pallas_call | solution.py:165
  212.7 1.1 copy-done.1
  213.8 24.7 %all-to-all-done.2 = bf16[16,3,2,64,128]{4,3,2,1,0:T(8,128)(2,1)S(1)} async-done(((bf16[16,3,2,64,128]{4,3,2,1,0:T(8,128)(2,1)}), bf16[16,3,2,64,128]{4,3,2,1,0:T(8,128)(2,1)S(1)}, u32[]{:S(2)}, u32[]{:S(2)}) %all-to-all-start.2) | async-done | bytes 1572896 | tf_op jit(solution)/shard_map/all_to_all | solution.py:216
  238.6 8.5 %all-to-all-start.3 = ((bf16[16,3,2,64,128]{4,3,2,1,0:T(8,128)(2,1)}), bf16[16,3,2,64,128]{4,3,2,1,0:T(8,128)(2,1)S(1)}, u32[]{:S(2)}, u32[]{:S(2)}) async-start(bf16[16,3,2,64,128]{4,3,2,1,0:T(8,128)(2,1)} %copy-done.1), calls=%async_computation.3 | async-start | bytes 3145728 | tf_op jit(solution)/shard_map/all_to_all | solution.py:216
  247.1 1.5 shard_map.152
  248.6 41.3 %all-to-all-done.3 = bf16[16,3,2,64,128]{4,3,2,1,0:T(8,128)(2,1)S(1)} async-done(((bf16[16,3,2,64,128]{4,3,2,1,0:T(8,128)(2,1)}), bf16[16,3,2,64,128]{4,3,2,1,0:T(8,128)(2,1)S(1)}, u32[]{:S(2)}, u32[]{:S(2)}) %all-to-all-start.3) | async-done | bytes 1572896 | tf_op jit(solution)/shard_map/all_to_all | solution.py:216
  289.9 1.5 shard_map.151
  (98 shorter events, 7.1 us)
Async XLA Ops:
  0.6 1.0 copy-start.9
  1.7 1.0 copy-start.10
  2.7 1.0 copy-start.11
  5.2 8.8 %copy-start.2 = (bf16[128,2048]{1,0:T(8,128)(2,1)S(1)}, bf16[128,2048]{1,0:T(8,128)(2,1)}, u32[]{:S(2)}) copy-start(bf16[128,2048]{1,0:T(8,128)(2,1)} %refs_4_.1) | copy-start | bytes 1572868
  5.2 52.0 %copy-start = (bf16[2,1,64,2048]{3,2,1,0:T(8,128)(2,1)S(1)}, bf16[2,1,64,2048]{3,2,1,0:T(8,128)(2,1)}, u32[]{:S(2)}) copy-start(bf16[2,1,64,2048]{3,2,1,0:T(8,128)(2,1)} %param.16) | copy-start | bytes 1572868
  5.2 119.5 %all-to-all-start = ((bf16[16,3,2,64,128]{4,3,2,1,0:T(8,128)(2,1)}), bf16[16,3,2,64,128]{4,3,2,1,0:T(8,128)(2,1)S(1)}, u32[]{:S(2)}, u32[]{:S(2)}) async-start(bf16[16,3,2,64,128]{4,3,2,1,0:T(8,128)(2,1)} %bitcast.3), calls=%async_computation | async-start | bytes 3145728 | tf_op jit(solution)/shard_map/all_to_all | solution.py:216
  14.0 38.3 %collective-permute-start = (bf16[16,2048]{1,0:T(8,128)(2,1)S(1)}, bf16[16,2048]{1,0:T(8,128)(2,1)S(1)}, u32[]{:S(2)}, u32[]{:S(2)}) collective-permute-start(bf16[16,2048]{1,0:T(8,128)(2,1)S(1)} %constant_dynamic-slice_fusion), channel_id=1, source_target_pairs={{0,140},{1,141},{2,142},{3,143},{4,0},{5,1},{6,2},{7,3},{8,4},{9,5... | collective-permute-start | bytes 196616 | tf_op jit(solution)/shard_map/ppermute | solution.py:30
  14.2 38.1 %collective-permute-start.1 = (bf16[16,2048]{1,0:T(8,128)(2,1)S(1)}, bf16[16,2048]{1,0:T(8,128)(2,1)S(1)}, u32[]{:S(2)}, u32[]{:S(2)}) collective-permute-start(bf16[16,2048]{1,0:T(8,128)(2,1)S(1)} %constant_dynamic-slice_fusion), channel_id=1, source_target_pairs={{0,8},{1,9},{2,10},{3,11},{4,12},{5,13},{6,14},{7,15},{8,128},{9,1... | collective-permute-start | bytes 196616 | tf_op jit(solution)/shard_map/ppermute | solution.py:30
  17.0 35.3 %collective-permute-start.2 = (bf16[16,2048]{1,0:T(8,128)(2,1)S(1)}, bf16[16,2048]{1,0:T(8,128)(2,1)S(1)}, u32[]{:S(2)}, u32[]{:S(2)}) collective-permute-start(bf16[16,2048]{1,0:T(8,128)(2,1)S(1)} %constant_dynamic-slice_fusion), channel_id=1, source_target_pairs={{0,4},{1,5},{2,6},{3,7},{4,8},{5,9},{6,10},{7,11},{8,12},{9,13},{1... | collective-permute-start | bytes 196616 | tf_op jit(solution)/shard_map/ppermute | solution.py:30
  52.4 7.9 %collective-permute-start.4 = (bf16[3,16,2048]{2,1,0:T(8,128)(2,1)S(1)}, bf16[3,16,2048]{2,1,0:T(8,128)(2,1)S(1)}, u32[]{:S(2)}, u32[]{:S(2)}) collective-permute-start(bf16[3,16,2048]{2,1,0:T(8,128)(2,1)S(1)} %pad_maximum_fusion.refs_5_), channel_id=1, source_target_pairs={{0,32},{1,33},{2,34},{3,35},{4,36},{5,37},{6,38},{7,39},{8,40},{9,... | collective-permute-start | bytes 589832 | tf_op jit(solution)/shard_map/ppermute | solution.py:30
  53.3 11.0 %collective-permute-start.6 = (bf16[3,16,2048]{2,1,0:T(8,128)(2,1)S(1)}, bf16[3,16,2048]{2,1,0:T(8,128)(2,1)S(1)}, u32[]{:S(2)}, u32[]{:S(2)}) collective-permute-start(bf16[3,16,2048]{2,1,0:T(8,128)(2,1)S(1)} %pad_maximum_fusion.refs_5_), channel_id=1, source_target_pairs={{0,64},{1,65},{2,66},{3,67},{4,68},{5,69},{6,70},{7,71},{8,72},{9,... | collective-permute-start | bytes 589832 | tf_op jit(solution)/shard_map/ppermute | solution.py:30
  54.4 9.9 %collective-permute-start.8 = (bf16[3,16,2048]{2,1,0:T(8,128)(2,1)S(1)}, bf16[3,16,2048]{2,1,0:T(8,128)(2,1)S(1)}, u32[]{:S(2)}, u32[]{:S(2)}) collective-permute-start(bf16[3,16,2048]{2,1,0:T(8,128)(2,1)S(1)} %pad_maximum_fusion.refs_5_), channel_id=1, source_target_pairs={{0,96},{1,97},{2,98},{3,99},{4,100},{5,101},{6,102},{7,103},{8,104... | collective-permute-start | bytes 589832 | tf_op jit(solution)/shard_map/ppermute | solution.py:30
  57.2 17.8 %collective-permute-start.14 = (bf16[128,2048]{1,0:T(8,128)(2,1)S(1)}, bf16[128,2048]{1,0:T(8,128)(2,1)S(1)}, u32[]{:S(2)}, u32[]{:S(2)}) collective-permute-start(bf16[128,2048]{1,0:T(8,128)(2,1)S(1)} %bitcast.49), channel_id=1, source_target_pairs={{0,32},{1,33},{2,34},{3,35},{4,36},{5,37},{6,38},{7,39},{8,40},{9,... | collective-permute-start | bytes 1572872 | tf_op jit(solution)/shard_map/ppermute | solution.py:30
  57.2 8.8 %collective-permute-start.3 = (bf16[3,16,2048]{2,1,0:T(8,128)(2,1)S(1)}, bf16[3,16,2048]{2,1,0:T(8,128)(2,1)S(1)}, u32[]{:S(2)}, u32[]{:S(2)}) collective-permute-start(bf16[3,16,2048]{2,1,0:T(8,128)(2,1)S(1)} %pad_maximum_fusion.refs_5_), channel_id=1, source_target_pairs={{0,16},{1,17},{2,18},{3,19},{4,20},{5,21},{6,22},{7,23},{8,24},{9,... | collective-permute-start | bytes 589832 | tf_op jit(solution)/shard_map/ppermute | solution.py:30
  60.3 9.0 %collective-permute-start.5 = (bf16[3,16,2048]{2,1,0:T(8,128)(2,1)S(1)}, bf16[3,16,2048]{2,1,0:T(8,128)(2,1)S(1)}, u32[]{:S(2)}, u32[]{:S(2)}) collective-permute-start(bf16[3,16,2048]{2,1,0:T(8,128)(2,1)S(1)} %collective-permute-done.4.refs_7_), channel_id=1, source_target_pairs={{0,16},{1,17},{2,18},{3,19},{4,20},{5,21},{6,22},{7,23},{8,24},{9,... | collective-permute-start | bytes 589832 | tf_op jit(solution)/shard_map/ppermute | solution.py:30
  64.3 22.8 %copy-start.32 = (bf16[3,16,2048]{2,1,0:T(8,128)(2,1)}, bf16[3,16,2048]{2,1,0:T(8,128)(2,1)S(1)}, u32[]{:S(2)}) copy-start(bf16[3,16,2048]{2,1,0:T(8,128)(2,1)S(1)} %collective-permute-done.6.refs_9_) | copy-start | bytes 589828
  64.3 6.7 %collective-permute-start.7 = (bf16[3,16,2048]{2,1,0:T(8,128)(2,1)S(1)}, bf16[3,16,2048]{2,1,0:T(8,128)(2,1)S(1)}, u32[]{:S(2)}, u32[]{:S(2)}) collective-permute-start(bf16[3,16,2048]{2,1,0:T(8,128)(2,1)S(1)} %collective-permute-done.6.refs_9_), channel_id=1, source_target_pairs={{0,16},{1,17},{2,18},{3,19},{4,20},{5,21},{6,22},{7,23},{8,24},{9,... | collective-permute-start | bytes 589832 | tf_op jit(solution)/shard_map/ppermute | solution.py:30
  64.3 37.6 %copy-start.34 = (bf16[3,16,2048]{2,1,0:T(8,128)(2,1)}, bf16[3,16,2048]{2,1,0:T(8,128)(2,1)S(1)}, u32[]{:S(2)}) copy-start(bf16[3,16,2048]{2,1,0:T(8,128)(2,1)S(1)} %collective-permute-done.8.refs_11_) | copy-start | bytes 589828
  64.3 7.4 %collective-permute-start.9 = (bf16[3,16,2048]{2,1,0:T(8,128)(2,1)S(1)}, bf16[3,16,2048]{2,1,0:T(8,128)(2,1)S(1)}, u32[]{:S(2)}, u32[]{:S(2)}) collective-permute-start(bf16[3,16,2048]{2,1,0:T(8,128)(2,1)S(1)} %collective-permute-done.8.refs_11_), channel_id=1, source_target_pairs={{0,16},{1,17},{2,18},{3,19},{4,20},{5,21},{6,22},{7,23},{8,24},{9,... | collective-permute-start | bytes 589832 | tf_op jit(solution)/shard_map/ppermute | solution.py:30
  66.7 17.7 %collective-permute-start.16 = (bf16[128,2048]{1,0:T(8,128)(2,1)S(1)}, bf16[128,2048]{1,0:T(8,128)(2,1)S(1)}, u32[]{:S(2)}, u32[]{:S(2)}) collective-permute-start(bf16[128,2048]{1,0:T(8,128)(2,1)S(1)} %bitcast.50), channel_id=1, source_target_pairs={{0,64},{1,65},{2,66},{3,67},{4,68},{5,69},{6,70},{7,71},{8,72},{9,... | collective-permute-start | bytes 1572872 | tf_op jit(solution)/shard_map/ppermute | solution.py:30
  69.9 24.8 %collective-permute-start.18 = (bf16[128,2048]{1,0:T(8,128)(2,1)S(1)}, bf16[128,2048]{1,0:T(8,128)(2,1)S(1)}, u32[]{:S(2)}, u32[]{:S(2)}) collective-permute-start(bf16[128,2048]{1,0:T(8,128)(2,1)S(1)} %bitcast.51), channel_id=1, source_target_pairs={{0,96},{1,97},{2,98},{3,99},{4,100},{5,101},{6,102},{7,103},{8,104... | collective-permute-start | bytes 1572872 | tf_op jit(solution)/shard_map/ppermute | solution.py:30
  71.7 23.0 %collective-permute-start.13 = (bf16[128,2048]{1,0:T(8,128)(2,1)S(1)}, bf16[128,2048]{1,0:T(8,128)(2,1)S(1)}, u32[]{:S(2)}, u32[]{:S(2)}) collective-permute-start(bf16[128,2048]{1,0:T(8,128)(2,1)S(1)} %bitcast.52), channel_id=1, source_target_pairs={{0,16},{1,17},{2,18},{3,19},{4,20},{5,21},{6,22},{7,23},{8,24},{9,... | collective-permute-start | bytes 1572872 | tf_op jit(solution)/shard_map/ppermute | solution.py:30
  72.4 23.9 %collective-permute-start.10 = (bf16[128,2048]{1,0:T(8,128)(2,1)S(1)}, bf16[128,2048]{1,0:T(8,128)(2,1)S(1)}, u32[]{:S(2)}, u32[]{:S(2)}) collective-permute-start(bf16[128,2048]{1,0:T(8,128)(2,1)S(1)} %bitcast.45), channel_id=1, source_target_pairs={{0,1},{1,0},{2,3},{3,2},{4,5},{5,4},{6,7},{7,6},{8,9},{9,8},{10,11... | collective-permute-start | bytes 1572872 | tf_op jit(solution)/shard_map/ppermute | solution.py:30
  75.0 25.3 %collective-permute-start.11 = (bf16[128,2048]{1,0:T(8,128)(2,1)S(1)}, bf16[128,2048]{1,0:T(8,128)(2,1)S(1)}, u32[]{:S(2)}, u32[]{:S(2)}) collective-permute-start(bf16[128,2048]{1,0:T(8,128)(2,1)S(1)} %bitcast.46), channel_id=1, source_target_pairs={{0,2},{1,3},{2,0},{3,1},{4,6},{5,7},{6,4},{7,5},{8,10},{9,11},{10,... | collective-permute-start | bytes 1572872 | tf_op jit(solution)/shard_map/ppermute | solution.py:30
  84.4 24.3 %collective-permute-start.12 = (bf16[128,2048]{1,0:T(8,128)(2,1)S(1)}, bf16[128,2048]{1,0:T(8,128)(2,1)S(1)}, u32[]{:S(2)}, u32[]{:S(2)}) collective-permute-start(bf16[128,2048]{1,0:T(8,128)(2,1)S(1)} %bitcast.47), channel_id=1, source_target_pairs={{0,3},{1,2},{2,1},{3,0},{4,7},{5,6},{6,5},{7,4},{8,11},{9,10},{10,... | collective-permute-start | bytes 1572872 | tf_op jit(solution)/shard_map/ppermute | solution.py:30
  94.7 26.8 %collective-permute-start.20 = (bf16[128,2048]{1,0:T(8,128)(2,1)}, bf16[128,2048]{1,0:T(8,128)(2,1)S(1)}, u32[]{:S(2)}, u32[]{:S(2)}) collective-permute-start(bf16[128,2048]{1,0:T(8,128)(2,1)} %refs_8_.1), channel_id=1, source_target_pairs={{0,136},{1,137},{2,138},{3,139},{4,140},{5,141},{6,142},{7,143},{8... | collective-permute-start | bytes 1572872 | tf_op jit(solution)/shard_map/ppermute | solution.py:30
  95.5 26.8 %collective-permute-start.15 = (bf16[128,2048]{1,0:T(8,128)(2,1)S(1)}, bf16[128,2048]{1,0:T(8,128)(2,1)S(1)}, u32[]{:S(2)}, u32[]{:S(2)}) collective-permute-start(bf16[128,2048]{1,0:T(8,128)(2,1)S(1)} %collective-permute-done.14.refs_2_), channel_id=1, source_target_pairs={{0,16},{1,17},{2,18},{3,19},{4,20},{5,21},{6,22},{7,23},{8,24},{9,... | collective-permute-start | bytes 1572872 | tf_op jit(solution)/shard_map/ppermute | solution.py:30
  96.3 0.8 copy-start.3
  97.1 26.0 %collective-permute-start.17 = (bf16[128,2048]{1,0:T(8,128)(2,1)S(1)}, bf16[128,2048]{1,0:T(8,128)(2,1)S(1)}, u32[]{:S(2)}, u32[]{:S(2)}) collective-permute-start(bf16[128,2048]{1,0:T(8,128)(2,1)S(1)} %collective-permute-done.16.refs_4_), channel_id=1, source_target_pairs={{0,16},{1,17},{2,18},{3,19},{4,20},{5,21},{6,22},{7,23},{8,24},{9,... | collective-permute-start | bytes 1572872 | tf_op jit(solution)/shard_map/ppermute | solution.py:30
  100.3 0.8 copy-start.5
  101.1 22.8 %collective-permute-start.19 = (bf16[128,2048]{1,0:T(8,128)(2,1)S(1)}, bf16[128,2048]{1,0:T(8,128)(2,1)S(1)}, u32[]{:S(2)}, u32[]{:S(2)}) collective-permute-start(bf16[128,2048]{1,0:T(8,128)(2,1)S(1)} %collective-permute-done.18.refs_6_), channel_id=1, source_target_pairs={{0,16},{1,17},{2,18},{3,19},{4,20},{5,21},{6,22},{7,23},{8,24},{9,... | collective-permute-start | bytes 1572872 | tf_op jit(solution)/shard_map/ppermute | solution.py:30
  101.9 1.0 copy-start.12
  102.9 1.0 copy-start.13
  104.0 1.0 copy-start.14
  108.6 0.8 copy-start.7
  123.9 0.8 copy-start.30
  124.7 69.8 %all-to-all-start.1 = ((bf16[16,3,2,64,128]{4,3,2,1,0:T(8,128)(2,1)}), bf16[16,3,2,64,128]{4,3,2,1,0:T(8,128)(2,1)}, u32[]{:S(2)}, u32[]{:S(2)}) async-start(bf16[16,3,2,64,128]{4,3,2,1,0:T(8,128)(2,1)} %bitcast.12), calls=%async_computation.1 | async-start | bytes 3145728 | tf_op jit(solution)/shard_map/all_to_all | solution.py:216
  130.7 1.0 copy-start.15
  131.7 1.0 copy-start.17
  132.8 1.0 copy-start.19
  133.8 1.0 copy-start.21
  134.9 1.0 copy-start.23
  135.9 1.0 copy-start.25
  136.9 1.0 copy-start.27
  138.0 1.0 copy-start.29
  139.0 1.0 copy-start.31
  140.1 9.0 %copy-start.4 = (bf16[128,2048]{1,0:T(8,128)(2,1)S(1)}, bf16[128,2048]{1,0:T(8,128)(2,1)}, u32[]{:S(2)}) copy-start(bf16[128,2048]{1,0:T(8,128)(2,1)} %copy-done.3) | copy-start | bytes 1572868
  140.1 9.0 %copy-start.6 = (bf16[128,2048]{1,0:T(8,128)(2,1)S(1)}, bf16[128,2048]{1,0:T(8,128)(2,1)}, u32[]{:S(2)}) copy-start(bf16[128,2048]{1,0:T(8,128)(2,1)} %copy-done.5) | copy-start | bytes 1572868
  140.1 9.0 %copy-start.8 = (bf16[128,2048]{1,0:T(8,128)(2,1)S(1)}, bf16[128,2048]{1,0:T(8,128)(2,1)}, u32[]{:S(2)}) copy-start(bf16[128,2048]{1,0:T(8,128)(2,1)} %copy-done.7) | copy-start | bytes 1572868
  140.1 9.0 %copy-start.33 = (bf16[3,16,2048]{2,1,0:T(8,128)(2,1)S(1)}, bf16[3,16,2048]{2,1,0:T(8,128)(2,1)}, u32[]{:S(2)}) copy-start(bf16[3,16,2048]{2,1,0:T(8,128)(2,1)} %copy-done.32) | copy-start | bytes 589828
  140.1 9.0 %copy-start.35 = (bf16[3,16,2048]{2,1,0:T(8,128)(2,1)S(1)}, bf16[3,16,2048]{2,1,0:T(8,128)(2,1)}, u32[]{:S(2)}) copy-start(bf16[3,16,2048]{2,1,0:T(8,128)(2,1)} %copy-done.34) | copy-start | bytes 589828
  140.1 9.0 %copy-start.37 = (bf16[3,16,2048]{2,1,0:T(8,128)(2,1)S(1)}, bf16[3,16,2048]{2,1,0:T(8,128)(2,1)}, u32[]{:S(2)}) copy-start(bf16[3,16,2048]{2,1,0:T(8,128)(2,1)} %copy-done.36) | copy-start | bytes 589828
  140.1 9.0 %copy-start.39 = (bf16[3,16,2048]{2,1,0:T(8,128)(2,1)S(1)}, bf16[3,16,2048]{2,1,0:T(8,128)(2,1)}, u32[]{:S(2)}) copy-start(bf16[3,16,2048]{2,1,0:T(8,128)(2,1)} %copy-done.38) | copy-start | bytes 589828
  140.1 9.0 %copy-start.41 = (bf16[3,16,2048]{2,1,0:T(8,128)(2,1)S(1)}, bf16[3,16,2048]{2,1,0:T(8,128)(2,1)}, u32[]{:S(2)}) copy-start(bf16[3,16,2048]{2,1,0:T(8,128)(2,1)} %copy-done.40) | copy-start | bytes 589828
  140.1 9.0 %copy-start.43 = (bf16[3,16,2048]{2,1,0:T(8,128)(2,1)S(1)}, bf16[3,16,2048]{2,1,0:T(8,128)(2,1)}, u32[]{:S(2)}) copy-start(bf16[3,16,2048]{2,1,0:T(8,128)(2,1)} %copy-done.42) | copy-start | bytes 589828
  143.6 9.8 %copy-start.44 = (bf16[8,128,128]{2,1,0:T(8,128)(2,1)}, bf16[8,128,128]{2,1,0:T(8,128)(2,1)S(1)}, u32[]{:S(2)}) copy-start(bf16[8,128,128]{2,1,0:T(8,128)(2,1)S(1)} %get-tuple-element.78) | copy-start | bytes 786436
  143.6 50.9 %collective-permute-start.21 = (bf16[8,128,128]{2,1,0:T(8,128)(2,1)}, bf16[8,128,128]{2,1,0:T(8,128)(2,1)S(1)}, u32[]{:S(2)}, u32[]{:S(2)}) collective-permute-start(bf16[8,128,128]{2,1,0:T(8,128)(2,1)} %get-tuple-element.58), channel_id=1, source_target_pairs={{0,128},{1,129},{2,130},{3,131},{4,132},{5,133},{6,134},{7,135},{8... | collective-permute-start | bytes 786440 | tf_op jit(solution)/shard_map/ppermute | solution.py:30
  153.5 27.5 %collective-permute-start.22 = (bf16[4,128,128]{2,1,0:T(8,128)(2,1)}, bf16[4,128,128]{2,1,0:T(8,128)(2,1)S(1)}, u32[]{:S(2)}, u32[]{:S(2)}) collective-permute-start(bf16[4,128,128]{2,1,0:T(8,128)(2,1)} %get-tuple-element.73), channel_id=1, source_target_pairs={{0,4},{1,5},{2,6},{3,7},{4,8},{5,9},{6,10},{7,11},{8,12},{9,13},{1... | collective-permute-start | bytes 393224 | tf_op jit(solution)/shard_map/ppermute | solution.py:268
  154.3 33.4 %collective-permute-start.23 = (bf16[4,128,128]{2,1,0:T(8,128)(2,1)}, bf16[4,128,128]{2,1,0:T(8,128)(2,1)S(1)}, u32[]{:S(2)}, u32[]{:S(2)}) collective-permute-start(bf16[4,128,128]{2,1,0:T(8,128)(2,1)} %get-tuple-element.74), channel_id=1, source_target_pairs={{0,8},{1,9},{2,10},{3,11},{4,12},{5,13},{6,14},{7,15},{8,0},{9,1},... | collective-permute-start | bytes 393224 | tf_op jit(solution)/shard_map/ppermute | solution.py:268
  155.3 34.0 %collective-permute-start.24 = (bf16[4,128,128]{2,1,0:T(8,128)(2,1)S(1)}, bf16[4,128,128]{2,1,0:T(8,128)(2,1)S(1)}, u32[]{:S(2)}, u32[]{:S(2)}) collective-permute-start(bf16[4,128,128]{2,1,0:T(8,128)(2,1)S(1)} %get-tuple-element.75), channel_id=1, source_target_pairs={{0,12},{1,13},{2,14},{3,15},{4,0},{5,1},{6,2},{7,3},{8,4},{9,5},{1... | collective-permute-start | bytes 393224 | tf_op jit(solution)/shard_map/ppermute | solution.py:268
  194.6 7.2 %copy-start.45 = (bf16[8,128,128]{2,1,0:T(8,128)(2,1)S(1)}, bf16[8,128,128]{2,1,0:T(8,128)(2,1)}, u32[]{:S(2)}) copy-start(bf16[8,128,128]{2,1,0:T(8,128)(2,1)} %copy-done.44) | copy-start | bytes 786436
  194.6 44.0 %all-to-all-start.2 = ((bf16[16,3,2,64,128]{4,3,2,1,0:T(8,128)(2,1)}), bf16[16,3,2,64,128]{4,3,2,1,0:T(8,128)(2,1)S(1)}, u32[]{:S(2)}, u32[]{:S(2)}) async-start(bf16[16,3,2,64,128]{4,3,2,1,0:T(8,128)(2,1)} %shard_map.149), calls=%async_computation.2 | async-start | bytes 3145728 | tf_op jit(solution)/shard_map/all_to_all | solution.py:216
  212.7 1.2 copy-start.1
  238.6 51.3 %all-to-all-start.3 = ((bf16[16,3,2,64,128]{4,3,2,1,0:T(8,128)(2,1)}), bf16[16,3,2,64,128]{4,3,2,1,0:T(8,128)(2,1)S(1)}, u32[]{:S(2)}, u32[]{:S(2)}) async-start(bf16[16,3,2,64,128]{4,3,2,1,0:T(8,128)(2,1)} %copy-done.1), calls=%async_computation.3 | async-start | bytes 3145728 | tf_op jit(solution)/shard_map/all_to_all | solution.py:216
  (11 other events, 8.3 us)
where the time goes:
time: 293 us; the launch traced here: 291 us
  waiting for transfers between devices  170 us (58%)
  starting transfers between devices  60.5 us (21%)
  Pallas kernels  30 us (10%)
  local copies, waits for them, and re-layouts  28.4 us (10%)
    ppermute x22, waiting for transfers between devices, send(): return lax.ppermute(array, ('space', 'tm'), permutation(move))  71 us
    all_to_all x4, waiting for transfers between devices, exchange(): return lax.all_to_all(array, axis, split_axis=0, concat_axis=0, tiled=True)  66 us
    ppermute x3, waiting for transfers between devices, on_device(): lax.ppermute(outs[k], 'tm', [(t, (t // 4 + k) % 4 * 4 + t % 4) for t in r...  33.4 us
    all_to_all x4, starting transfers between devices, exchange(): return lax.all_to_all(array, axis, split_axis=0, concat_axis=0, tiled=True)  30.4 us
    unnamed x92, local copies, waits for them, and re-layouts  28.3 us
    ppermute x22, starting transfers between devices, send(): return lax.ppermute(array, ('space', 'tm'), permutation(move))  27.8 us
    pallas_call x1, Pallas kernels, space_attention(): call(space_kernel, jax.ShapeDtypeStruct((16, 3, 2, 64, 128), BF16), 5 * (...  10.9 us
  transfers between devices with their start and end apart: 29, of which 14 were waited for; matrix products, arithmetic and copies ran while one was open for 0% of the time, Pallas kernels for 9%

commit v1 on v0

--- a/solution.py
+++ b/solution.py
@@ -13,6 +13,9 @@
 VMEM = 48 * 1024 * 1024
 BF16 = jnp.bfloat16
 F32 = jnp.float32
+WHOLE = pl.BlockSpec(memory_space=pltpu.VMEM)
+SCALARS = pl.BlockSpec(memory_space=pltpu.SMEM)
+LATER = pl.BlockSpec(memory_space=pl.ANY)
 
 
 def permutation(move):
@@ -48,15 +51,22 @@
     )
 
 
-def pack_kernel(a_ref, b_ref, c_ref, out_ref):
+def pack_kernel(a_ref, b_ref, c_ref, *refs):
+    out_ref = refs[-1]
     for t, ref in enumerate((a_ref, b_ref, c_ref)):
         for h in range(16):
             out_ref[h, t] = ref[:, h * 128 : (h + 1) * 128]
 
 
-def pack(a, b, c):
+def pack(a, b, c, *after):
     flat = [v.reshape(128, 2048) for v in (a, b, c)]
-    out = call(pack_kernel, jax.ShapeDtypeStruct((16, 3, 128, 128), BF16), 0, 3 << 20)(*flat)
+    out = call(
+        pack_kernel,
+        jax.ShapeDtypeStruct((16, 3, 128, 128), BF16),
+        0,
+        3 << 20,
+        in_specs=[WHOLE] * 3 + [LATER] * len(after),
+    )(*flat, *after)
     return out.reshape(16, 3, 2, 64, 128)
 
 
@@ -72,52 +82,47 @@
     return tuple(v.reshape(2, 1, 64, 2048) for v in outs)
 
 
-def space_proj_kernel(pos_ref, *refs):
-    shards, w_own, w_other, keep, other = refs[:8], refs[8], refs[9], refs[10], refs[11]
+def space_proj_kernel(shards_ref, w_own, w_other, after_ref, keep, other):
     weight = jnp.concatenate([w_own[...], w_other[...]], axis=0)
     for i in range(8):
-        at = pos_ref[0] ^ i
-        out = nt(shards[i][...], weight).astype(BF16)
-        keep[at] = out[:, :128]
-        other[at] = out[:, 128:]
-
-
-def space_proj(pos, shards, w_own, w_other):
+        out = nt(shards_ref[i], weight).astype(BF16)
+        keep[i] = out[:, :128]
+        other[i] = out[:, 128:]
+
+
+def space_proj(shards, w_own, w_other, after):
     shape = jax.ShapeDtypeStruct((8, 128, 128), BF16)
-    vmem = pl.BlockSpec(memory_space=pltpu.VMEM)
     return call(
         space_proj_kernel,
         (shape, shape),
         1 << 30,
         6 << 20,
-        in_specs=[pl.BlockSpec(memory_space=pltpu.SMEM)] + [vmem] * 10,
-    )(pos, *shards, w_own, w_other)
-
-
-def time_proj_kernel(pos_ref, *refs):
-    shards, own, pieces, outs, weight_ref = refs[:4], refs[4], refs[5:13], refs[13:17], refs[17]
+        in_specs=[WHOLE] * 3 + [LATER],
+    )(shards, w_own, w_other, after)
+
+
+def time_proj_kernel(y_ref, *refs):
+    shards, own, pieces_ref, outs, weight_ref = refs[:4], refs[4], refs[5], refs[6:10], refs[10]
     weight_ref[:128] = own[...]
     for i in range(8):
         for k in range(3):
-            row = 128 * (k + 1) + (pos_ref[1] ^ i) * 16
-            weight_ref[pl.ds(pl.multiple_of(row, 16), 16)] = pieces[i][k]
+            weight_ref[128 * (k + 1) + 16 * i : 128 * (k + 1) + 16 * (i + 1)] = pieces_ref[i, k]
     for i in range(4):
         out = nt(shards[i][...], weight_ref[...]).astype(BF16)
         for k in range(4):
-            outs[k][pos_ref[0] ^ i] = out[:, k * 128 : (k + 1) * 128]
-
-
-def time_proj(pos, shards, own, pieces):
+            outs[k][y_ref[0] ^ i] = out[:, k * 128 : (k + 1) * 128]
+
+
+def time_proj(y, shards, own, pieces):
     shape = jax.ShapeDtypeStruct((4, 128, 128), BF16)
-    vmem = pl.BlockSpec(memory_space=pltpu.VMEM)
     return call(
         time_proj_kernel,
         (shape,) * 4,
         1 << 30,
         5 << 20,
-        in_specs=[pl.BlockSpec(memory_space=pltpu.SMEM)] + [vmem] * 13,
+        in_specs=[SCALARS] + [WHOLE] * 6,
         scratch_shapes=[pltpu.VMEM((512, 2048), BF16)],
-    )(pos, *shards, own, *pieces)
+    )(y, *shards, own, pieces)
 
 
 def attend(q, k, v, o, k_t, mask):
@@ -135,7 +140,7 @@
     return dq_t, dk, dv
 
 
-def space_kernel(pos_ref, qkv_ref, keep_ref, got_ref, out_ref, o_ref, dk_ref, dv_ref):
+def space_kernel(pos_ref, qkv_ref, keep_ref, got_ref, after_ref, out_ref, o_ref, dk_ref, dv_ref):
     z_hi = pos_ref[0]
     o_ref[pl.ds(pl.multiple_of(z_hi * 512, 512), 512), :] = keep_ref[...].reshape(512, 128)
     o_ref[pl.ds(pl.multiple_of((1 - z_hi) * 512, 512), 512), :] = got_ref[...].reshape(512, 128)
@@ -159,7 +164,7 @@
     out_ref[:, 2] = dv_ref[...].astype(BF16).reshape(16, 1, 64, 128)
 
 
-def space_attention(z_hi, qkv, keep, got):
+def space_attention(z_hi, qkv, keep, got, after):
     whole = pl.BlockSpec((16, 3, 1, 64, 128), lambda b: (0, 0, b, 0, 0))
     half = pl.BlockSpec((8, 1, 64, 128), lambda b: (0, b, 0, 0))
     return call(
@@ -168,14 +173,14 @@
         5 * (1 << 29),
         4 << 20,
         grid=(2,),
-        in_specs=[pl.BlockSpec(memory_space=pltpu.SMEM), whole, half, half],
+        in_specs=[SCALARS, whole, half, half, LATER],
         out_specs=whole,
         scratch_shapes=[
             pltpu.VMEM((1024, 128), BF16),
             pltpu.VMEM((1024, 128), F32),
             pltpu.VMEM((1024, 128), F32),
         ],
-    )(z_hi, qkv, keep, got)
+    )(z_hi, qkv, keep, got, after)
 
 
 def time_kernel(pos_ref, qkv_ref, *refs):
@@ -206,7 +211,7 @@
         5 * (1 << 27),
         4 << 20,
         grid=(2,),
-        in_specs=[pl.BlockSpec(memory_space=pltpu.SMEM), whole] + [quarter] * 4,
+        in_specs=[SCALARS, whole] + [quarter] * 4,
         out_specs=whole,
         scratch_shapes=[pltpu.VMEM((16, 64, 128), BF16)],
     )(z_lo, qkv, *parts)
@@ -232,9 +237,12 @@
     z_hi, xc = place_s // 8, place_s % 8
     z_lo, y = place_t // 4, place_t % 4
 
-    time_in = exchange(pack(query_time, key_time, value_time), "tm")
-
+    halves = [[z * 8 + i for i in range(8)] for z in range(2)]
+    shards = lax.all_gather(block_grad.reshape(128, 2048), "space", axis_index_groups=halves)
     rows = lax.dynamic_slice_in_dim(proj_time, xc * 16, 16, 0)
+    time_packed = pack(query_time, key_time, value_time, rows)
+    time_in = exchange(time_packed, "tm")
+    w_other = send(proj_space, lambda z, x, y, c: (z + (-2 if z % 4 < 2 else 2), x, y, c))
     piece = jnp.stack(
         [
             send(rows, lambda z, x, y, c: (z - 1, x, y, c)),
@@ -242,47 +250,37 @@
             send(rows, lambda z, x, y, c: (z + 1, x, y, c)),
         ]
     )
-    along_x = [piece] + [send(piece, lambda z, x, y, c, k=k: (z, x ^ k, y, c)) for k in (1, 2, 3)]
-    twins = [send(p, lambda z, x, y, c: (z, x, y, 1 - c)) for p in along_x]
-    pieces = [(along_x, twins)[i % 2][i // 2] for i in range(8)]
-
+
+    space_packed = pack(query_space, key_space, value_space, time_in, w_other)
+    space_in = exchange(space_packed, "space")
+    keep, other = space_proj(shards, proj_space, w_other, space_packed)
+    got = send(other, lambda z, x, y, c: (z + 4, x, y, c))
+    pieces = lax.all_gather(piece, "space", axis_index_groups=halves)
     cotangent = (block_grad.astype(F32) + branch_grad.astype(F32)).astype(BF16).reshape(128, 2048)
     along_y = [cotangent] + [
         send(cotangent, lambda z, x, y, c, k=k: (z, x, y ^ k, c)) for k in (1, 2, 3)
     ]
-
-    grad = block_grad.reshape(128, 2048)
-    along_x = [grad] + [send(grad, lambda z, x, y, c, k=k: (z, x ^ k, y, c)) for k in (1, 2, 3)]
-    twins = [send(g, lambda z, x, y, c: (z, x, y, 1 - c)) for g in along_x]
-    shards = [(along_x, twins)[i % 2][i // 2] for i in range(8)]
-    w_other = send(proj_space, lambda z, x, y, c: (z + (-2 if z % 4 < 2 else 2), x, y, c))
-
-    space_packed = pack(query_space, key_space, value_space)
-    time_in, pieces, along_y, shards, w_other, space_packed = lax.optimization_barrier(
-        (time_in, pieces, along_y, shards, w_other, space_packed)
-    )
-
-    space_in = exchange(space_packed, "space")
-    outs = time_proj(jnp.stack([y, xc]), along_y, proj_time, pieces)
+    outs = time_proj(y.reshape(1), along_y, proj_time, pieces)
+
     parts = [outs[0]] + [
-        lax.ppermute(
-            outs[k], "tm", [(t, (t // 4 + k) % 4 * 4 + t % 4) for t in range(16)]
-        )
+        lax.ppermute(outs[k], "tm", [(t, (t // 4 + k) % 4 * 4 + t % 4) for t in range(16)])
         for k in (1, 2, 3)
     ]
-    keep, other = space_proj(xc.reshape(1), shards, proj_space, w_other)
-    got = send(other, lambda z, x, y, c: (z + 4, x, y, c))
+    space_grads = space_attention(
+        z_hi.reshape(1),
+        space_in,
+        keep.reshape(8, 2, 64, 128),
+        got.reshape(8, 2, 64, 128),
+        outs[0],
+    )
+    space_grads, parts = lax.optimization_barrier((space_grads, parts))
+
+    space_out = exchange(space_grads, "space")
     time_grads = time_attention(
         z_lo.reshape(1), time_in, [p.reshape(4, 2, 64, 128) for p in parts]
     )
-    space_in, keep, got, time_grads = lax.optimization_barrier((space_in, keep, got, time_grads))
-
+    space_out, time_grads = lax.optimization_barrier((space_out, time_grads))
     time_out = exchange(time_grads, "tm")
-    space_grads = space_attention(
-        z_hi.reshape(1), space_in, keep.reshape(8, 2, 64, 128), got.reshape(8, 2, 64, 128)
-    )
-    time_out, space_grads = lax.optimization_barrier((time_out, space_grads))
-    space_out = exchange(space_grads, "space")
     return unpack(space_out) + unpack(time_out)
 
 

time: 293 us -> 238 us (0.81)
  waiting for transfers between devices: 170 us -> 124 us
  local copies, waits for them, and re-layouts: 28.4 us -> 12.1 us
  between operations: 0.88 us -> 14.2 us
  starting transfers between devices: 60.5 us -> 52.7 us
    ppermute x3, waiting for transfers between devices: 33.4 us -> 0.01 us  [on_device(): lax.ppermute(outs[k], 'tm', [(t, (t // 4 + k) % 4 * 4 + t % 4) for t in r...]
    ppermute x22 -> x8, waiting for transfers between devices: 71 us -> 43.6 us  [send(): return lax.ppermute(array, ('space', 'tm'), permutation(move))]
    unnamed x92 -> x32, local copies, waits for them, and re-layouts: 28.3 us -> 11.2 us
    all_to_all x4, waiting for transfers between devices: 66 us -> 77.3 us  [exchange(): return lax.all_to_all(array, axis, split_axis=0, concat_axis=0, tiled=True)]
    ppermute x22 -> x8, starting transfers between devices: 27.8 us -> 16.6 us  [send(): return lax.ppermute(array, ('space', 'tm'), permutation(move))]
    ppermute x3, starting transfers between devices: 2.34 us -> 6.08 us  [on_device(): lax.ppermute(outs[k], 'tm', [(t, (t // 4 + k) % 4 * 4 + t % 4) for t in r...]
  transfers between devices with their start and end apart: 29 -> 17, of which waited for: 14 -> 9; matrix products, arithmetic and copies ran while one was open for 0% -> 1% of each run, Pallas kernels for 9% -> 13%
where the time goes in v1:
time: 238 us; the launch traced here: 237 us
  waiting for transfers between devices  124 us (52%)
  starting transfers between devices  52.7 us (22%)
  Pallas kernels  32 us (13%)
  between operations  14.2 us (6%)
  local copies, waits for them, and re-layouts  12.1 us (5%)
    all_to_all x4, waiting for transfers between devices, exchange(): return lax.all_to_all(array, axis, split_axis=0, concat_axis=0, tiled=True)  77.3 us
    ppermute x8, waiting for transfers between devices, send(): return lax.ppermute(array, ('space', 'tm'), permutation(move))  43.6 us
    all_to_all x4, starting transfers between devices, exchange(): return lax.all_to_all(array, axis, split_axis=0, concat_axis=0, tiled=True)  29.9 us
    ppermute x8, starting transfers between devices, send(): return lax.ppermute(array, ('space', 'tm'), permutation(move))  16.6 us
    unnamed x32, local copies, waits for them, and re-layouts  11.2 us
    pallas_call x1, Pallas kernels, space_attention(): call(space_kernel, jax.ShapeDtypeStruct((16, 3, 2, 64, 128), BF16), 5 * (...  10.9 us
    ppermute x3, starting transfers between devices, on_device(): lax.ppermute(outs[k], 'tm', [(t, (t // 4 + k) % 4 * 4 + t % 4) for t in r...  6.08 us
    pallas_call x1, Pallas kernels, space_proj(): call(space_proj_kernel, (shape, shape), 1 << 30, 6 << 20, in_specs=[WHOLE...  5.68 us
  transfers between devices with their start and end apart: 17, of which 9 were waited for; matrix products, arithmetic and copies ran while one was open for 1% of the time, Pallas kernels for 13%

profile of v1, /device:TPU:38, one launch (start us, length us, event | category | flops | bytes accessed | tf_op | source)
XLA Modules:
  0.0 236.9 jit_solution(618875450714386611)
XLA Ops:
  7.2 0.0 all-gather.4.cloned.1.call-start
  7.2 0.7 all-gather.4.cloned.1.call-update
  7.9 0.8 constant_dynamic-slice_fusion.refs_0_
  8.8 1.0 copy-done.4
  9.8 1.0 copy-done.5
  10.9 1.0 copy-done.6
  11.9 1.4 shard_map.145
  13.3 8.8 %all-to-all-start = ((bf16[16,3,2,64,128]{4,3,2,1,0:T(8,128)(2,1)}), bf16[16,3,2,64,128]{4,3,2,1,0:T(8,128)(2,1)S(1)}, u32[]{:S(2)}, u32[]{:S(2)}) async-start(bf16[16,3,2,64,128]{4,3,2,1,0:T(8,128)(2,1)} %bitcast.7), calls=%async_computation | async-start | bytes 3145728 | tf_op jit(solution)/shard_map/all_to_all | solution.py:221
  22.1 4.5 %collective-permute-start = (bf16[128,2048]{1,0:T(8,128)(2,1)}, bf16[128,2048]{1,0:T(8,128)(2,1)S(1)}, u32[]{:S(2)}, u32[]{:S(2)}) collective-permute-start(bf16[128,2048]{1,0:T(8,128)(2,1)} %w_own.1), channel_id=1, source_target_pairs={{0,136},{1,137},{2,138},{3,139},{4,140},{5,141},{6,142},{7,143},{8... | collective-permute-start | bytes 1572872 | tf_op jit(solution)/shard_map/ppermute | solution.py:33
  26.6 0.0 collective-permute-start.7
  26.6 1.1 collective-permute-start.6
  27.7 1.5 collective-permute-start.5
  29.2 31.2 %collective-permute-done.refs_1_.w_other = bf16[128,2048]{1,0:T(8,128)(2,1)S(1)} collective-permute-done((bf16[128,2048]{1,0:T(8,128)(2,1)}, bf16[128,2048]{1,0:T(8,128)(2,1)S(1)}, u32[]{:S(2)}, u32[]{:S(2)}) %collective-permute-start) | collective-permute-done | bytes 524320 | tf_op jit(solution)/shard_map/ppermute | solution.py:33
  60.4 3.0 %all-to-all-done.refs_0_.qkv_ref = bf16[16,3,2,64,128]{4,3,2,1,0:T(8,128)(2,1)S(1)} async-done(((bf16[16,3,2,64,128]{4,3,2,1,0:T(8,128)(2,1)}), bf16[16,3,2,64,128]{4,3,2,1,0:T(8,128)(2,1)S(1)}, u32[]{:S(2)}, u32[]{:S(2)}) %all-to-all-start) | async-done | bytes 1572896 | tf_op jit(solution)/shard_map/all_to_all | solution.py:221
  63.4 0.0 copy-done.7
  63.4 0.0 copy-done.8
  63.4 1.0 copy-done.9
  64.4 1.4 shard_map.146
  65.9 8.8 %all-to-all-start.1 = ((bf16[16,3,2,64,128]{4,3,2,1,0:T(8,128)(2,1)}), bf16[16,3,2,64,128]{4,3,2,1,0:T(8,128)(2,1)}, u32[]{:S(2)}, u32[]{:S(2)}) async-start(bf16[16,3,2,64,128]{4,3,2,1,0:T(8,128)(2,1)} %bitcast.8.after_ref), calls=%async_computation.1 | async-start | bytes 3145728 | tf_op jit(solution)/shard_map/all_to_all | solution.py:221
  74.7 0.0 all-gather.6.cloned.1.call-start
  74.7 0.0 collective-permute-done.7
  74.8 0.0 collective-permute-done.6
  74.8 0.0 collective-permute-done.5
  74.8 0.7 pad_maximum_fusion
  75.5 0.0 all-gather.6.cloned.1.call-update
  75.5 0.0 copy-done.15
  75.5 1.2 add_convert_fusion
  76.7 0.0 copy-start.3
  76.7 0.1 collective-permute-start.4
  76.8 2.6 %collective-permute-start.3 = (bf16[128,2048]{1,0:T(8,128)(2,1)S(1)}, bf16[128,2048]{1,0:T(8,128)(2,1)}, u32[]{:S(2)}, u32[]{:S(2)}) collective-permute-start(bf16[128,2048]{1,0:T(8,128)(2,1)S(1)} %bitcast.46), channel_id=1, source_target_pairs={{0,2},{1,3},{2,0},{3,1},{4,6},{5,7},{6,4},{7,5},{8,10},{9,11},{10,... | collective-permute-start | bytes 1572872 | tf_op jit(solution)/shard_map/ppermute | solution.py:33
  79.4 1.5 collective-permute-start.2
  80.9 1.0 copy-done.10
  81.9 5.7 %shard_map.147 = (bf16[8,128,128]{2,1,0:T(8,128)(2,1)S(1)}, bf16[8,128,128]{2,1,0:T(8,128)(2,1)}) custom-call(bf16[8,128,2048]{2,1,0:T(8,128)(2,1)} %all-gather.4.cloned.1.call-done.shards_ref, bf16[128,2048]{1,0:T(8,128)(2,1)S(1)} %copy-done.10, bf16[128,2048]{1,0:T(8,128)(2,1)S(1)} %collective-permute-done.refs_1_.w_other, ...), custom_call_target="tpu_custom_call" | custom-call | flops 1073741824 | bytes 6291456 | tf_op jit(solution)/shard_map/pallas_call | solution.py:95
  87.6 0.7 copy-done.13
  88.3 5.4 %collective-permute-start.1 = (bf16[8,128,128]{2,1,0:T(8,128)(2,1)}, bf16[8,128,128]{2,1,0:T(8,128)(2,1)}, u32[]{:S(2)}, u32[]{:S(2)}) collective-permute-start(bf16[8,128,128]{2,1,0:T(8,128)(2,1)} %get-tuple-element.26), channel_id=1, source_target_pairs={{0,128},{1,129},{2,130},{3,131},{4,132},{5,133},{6,134},{7,135},{8... | collective-permute-start | bytes 786440 | tf_op jit(solution)/shard_map/ppermute | solution.py:33
  93.7 9.6 %collective-permute-done.4.refs_3_ = bf16[128,2048]{1,0:T(8,128)(2,1)} collective-permute-done((bf16[128,2048]{1,0:T(8,128)(2,1)S(1)}, bf16[128,2048]{1,0:T(8,128)(2,1)}, u32[]{:S(2)}, u32[]{:S(2)}) %collective-permute-start.4) | collective-permute-done | bytes 524320 | tf_op jit(solution)/shard_map/ppermute | solution.py:33
  103.3 0.0 collective-permute-done.3.refs_2_
  103.3 0.6 collective-permute-done.2.refs_1_
  103.9 2.6 %all-gather.6.cloned.1.call-done = bf16[24,16,2048]{2,1,0:T(8,128)(2,1)} async-done(((bf16[3,16,2048]{2,1,0:T(8,128)(2,1)}), bf16[24,16,2048]{2,1,0:T(8,128)(2,1)}) %all-gather.6.cloned.1.call-update) | async-done | bytes 1572880 | tf_op jit(solution)/shard_map/all_gather | solution.py:258
  106.5 1.4 copy-done.1
  107.9 4.9 %shard_map.148 = (bf16[4,128,128]{2,1,0:T(8,128)(2,1)S(1)}, bf16[4,128,128]{2,1,0:T(8,128)(2,1)}, bf16[4,128,128]{2,1,0:T(8,128)(2,1)}, bf16[4,128,128]{2,1,0:T(8,128)(2,1)S(1)}) custom-call(s32[1]{0:T(128)} %bitcast.12.y_ref, bf16[128,2048]{1,0:T(8,128)(2,1)S(1)} %bitcast.48, bf16[128,2048]{1,0:T(8,128)(2,1)} %collective-permute-done.2.refs_1_, ...), custom_call_target="tpu_custom_call" | custom-call | flops 1073741824 | bytes 5242880 | tf_op jit(solution)/shard_map/pallas_call | solution.py:118
  112.9 2.4 %collective-permute-start.8 = (bf16[4,128,128]{2,1,0:T(8,128)(2,1)}, bf16[4,128,128]{2,1,0:T(8,128)(2,1)S(1)}, u32[]{:S(2)}, u32[]{:S(2)}) collective-permute-start(bf16[4,128,128]{2,1,0:T(8,128)(2,1)} %get-tuple-element.28), channel_id=1, source_target_pairs={{0,4},{1,5},{2,6},{3,7},{4,8},{5,9},{6,10},{7,11},{8,12},{9,13},{1... | collective-permute-start | bytes 393224 | tf_op jit(solution)/shard_map/ppermute | solution.py:266
  115.3 1.6 collective-permute-start.9
  116.9 2.0 collective-permute-start.10
  118.9 5.0 %all-to-all-done.1.qkv_ref = bf16[16,3,2,64,128]{4,3,2,1,0:T(8,128)(2,1)} async-done(((bf16[16,3,2,64,128]{4,3,2,1,0:T(8,128)(2,1)}), bf16[16,3,2,64,128]{4,3,2,1,0:T(8,128)(2,1)}, u32[]{:S(2)}, u32[]{:S(2)}) %all-to-all-start.1) | async-done | bytes 1572896 | tf_op jit(solution)/shard_map/all_to_all | solution.py:221
  123.9 2.1 collective-permute-done.1
  126.1 0.0 copy-done.14
  126.1 10.9 %shard_map.149 = bf16[16,3,2,64,128]{4,3,2,1,0:T(8,128)(2,1)S(1)} custom-call(s32[1]{0:T(128)} %bitcast.pos_ref, bf16[16,3,2,64,128]{4,3,2,1,0:T(8,128)(2,1)} %all-to-all-done.1.qkv_ref, bf16[8,2,64,128]{3,2,1,0:T(8,128)(2,1)S(1)} %bitcast.60, bf16[8,2,64,128]{3,2,1,0:T(8,128)(2,1)} %bitcast.11.got_ref, bf16[4,128,128]{2,1,0:T(8,128)(2,1)S(1)} %get-tuple-element.32.after_ref), custom_call_target="tpu_custom_call" | custom-call | flops 2684354560 | bytes 4194304 | tf_op jit(solution)/shard_map/pallas_call | solution.py:170
  137.0 1.2 copy-done.2
  138.2 0.0 collective-permute-done.8
  138.2 0.0 collective-permute-done.9
  138.2 0.0 collective-permute-done.10
  138.2 0.0 copy-start.11
  138.2 0.6 copy-done.11
  138.9 8.5 %all-to-all-start.2 = ((bf16[16,3,2,64,128]{4,3,2,1,0:T(8,128)(2,1)}), bf16[16,3,2,64,128]{4,3,2,1,0:T(8,128)(2,1)S(1)}, u32[]{:S(2)}, u32[]{:S(2)}) async-start(bf16[16,3,2,64,128]{4,3,2,1,0:T(8,128)(2,1)} %copy-done.2), calls=%async_computation.2 | async-start | bytes 3145728 | tf_op jit(solution)/shard_map/all_to_all | solution.py:221
  147.4 0.9 copy-done.12
  148.3 4.4 %shard_map.150 = bf16[16,3,2,64,128]{4,3,2,1,0:T(8,128)(2,1)S(1)} custom-call(s32[1]{0:T(128)} %bitcast.18.pos_ref, bf16[16,3,2,64,128]{4,3,2,1,0:T(8,128)(2,1)S(1)} %all-to-all-done.refs_0_.qkv_ref, bf16[4,2,64,128]{3,2,1,0:T(8,128)(2,1)S(1)} %bitcast.56, bf16[4,2,64,128]{3,2,1,0:T(8,128)(2,1)S(1)} %bitcast.57, bf16[4,2,64,128]{3,2,1,0:T(8,128)(2,1)S(1)} %bitcast.58, ...), custom_call_target="tpu_custom_call" | custom-call | flops 671088640 | bytes 4194304 | tf_op jit(solution)/shard_map/pallas_call | solution.py:208
  152.7 0.0 copy-start
  152.7 1.1 copy-done
  153.9 33.8 %all-to-all-done.2 = bf16[16,3,2,64,128]{4,3,2,1,0:T(8,128)(2,1)S(1)} async-done(((bf16[16,3,2,64,128]{4,3,2,1,0:T(8,128)(2,1)}), bf16[16,3,2,64,128]{4,3,2,1,0:T(8,128)(2,1)S(1)}, u32[]{:S(2)}, u32[]{:S(2)}) %all-to-all-start.2) | async-done | bytes 1572896 | tf_op jit(solution)/shard_map/all_to_all | solution.py:221
  187.7 3.8 %all-to-all-start.3 = ((bf16[16,3,2,64,128]{4,3,2,1,0:T(8,128)(2,1)}), bf16[16,3,2,64,128]{4,3,2,1,0:T(8,128)(2,1)S(1)}, u32[]{:S(2)}, u32[]{:S(2)}) async-start(bf16[16,3,2,64,128]{4,3,2,1,0:T(8,128)(2,1)} %copy-done), calls=%async_computation.3 | async-start | bytes 3145728 | tf_op jit(solution)/shard_map/all_to_all | solution.py:221
  191.5 1.5 shard_map.151
  193.0 35.5 %all-to-all-done.3 = bf16[16,3,2,64,128]{4,3,2,1,0:T(8,128)(2,1)S(1)} async-done(((bf16[16,3,2,64,128]{4,3,2,1,0:T(8,128)(2,1)}), bf16[16,3,2,64,128]{4,3,2,1,0:T(8,128)(2,1)S(1)}, u32[]{:S(2)}, u32[]{:S(2)}) %all-to-all-start.3) | async-done | bytes 1572896 | tf_op jit(solution)/shard_map/all_to_all | solution.py:221
  228.6 1.5 shard_map.152
  (15 shorter events, 0.0 us)
Async XLA Ops:
  7.2 73.7 %all-gather.4.cloned.1.call-start = ((), (), s32[]{:S(2)}) async-start(), calls=%async_computation.4 | async-start | bytes 4718592 | tf_op jit(solution)/shard_map/all_gather | solution.py:241
  8.8 1.0 copy-start.4
  9.8 1.0 copy-start.5
  10.9 1.0 copy-start.6
  13.3 50.1 %copy-start.7 = (bf16[2,1,64,2048]{3,2,1,0:T(8,128)(2,1)S(1)}, bf16[2,1,64,2048]{3,2,1,0:T(8,128)(2,1)}, u32[]{:S(2)}) copy-start(bf16[2,1,64,2048]{3,2,1,0:T(8,128)(2,1)} %param.10) | copy-start | bytes 1572868
  13.3 50.1 %copy-start.8 = (bf16[2,1,64,2048]{3,2,1,0:T(8,128)(2,1)S(1)}, bf16[2,1,64,2048]{3,2,1,0:T(8,128)(2,1)}, u32[]{:S(2)}) copy-start(bf16[2,1,64,2048]{3,2,1,0:T(8,128)(2,1)} %param.11) | copy-start | bytes 1572868
  13.3 50.1 %all-to-all-start = ((bf16[16,3,2,64,128]{4,3,2,1,0:T(8,128)(2,1)}), bf16[16,3,2,64,128]{4,3,2,1,0:T(8,128)(2,1)S(1)}, u32[]{:S(2)}, u32[]{:S(2)}) async-start(bf16[16,3,2,64,128]{4,3,2,1,0:T(8,128)(2,1)} %bitcast.7), calls=%async_computation | async-start | bytes 3145728 | tf_op jit(solution)/shard_map/all_to_all | solution.py:221
  22.1 38.2 %collective-permute-start = (bf16[128,2048]{1,0:T(8,128)(2,1)}, bf16[128,2048]{1,0:T(8,128)(2,1)S(1)}, u32[]{:S(2)}, u32[]{:S(2)}) collective-permute-start(bf16[128,2048]{1,0:T(8,128)(2,1)} %w_own.1), channel_id=1, source_target_pairs={{0,136},{1,137},{2,138},{3,139},{4,140},{5,141},{6,142},{7,143},{8... | collective-permute-start | bytes 1572872 | tf_op jit(solution)/shard_map/ppermute | solution.py:33
  26.6 48.1 %collective-permute-start.7 = (bf16[16,2048]{1,0:T(8,128)(2,1)S(1)}, bf16[16,2048]{1,0:T(8,128)(2,1)S(1)}, u32[]{:S(2)}, u32[]{:S(2)}) collective-permute-start(bf16[16,2048]{1,0:T(8,128)(2,1)S(1)} %constant_dynamic-slice_fusion.refs_0_), channel_id=1, source_target_pairs={{0,4},{1,5},{2,6},{3,7},{4,8},{5,9},{6,10},{7,11},{8,12},{9,13},{1... | collective-permute-start | bytes 196616 | tf_op jit(solution)/shard_map/ppermute | solution.py:33
  26.6 48.1 %collective-permute-start.6 = (bf16[16,2048]{1,0:T(8,128)(2,1)S(1)}, bf16[16,2048]{1,0:T(8,128)(2,1)S(1)}, u32[]{:S(2)}, u32[]{:S(2)}) collective-permute-start(bf16[16,2048]{1,0:T(8,128)(2,1)S(1)} %constant_dynamic-slice_fusion.refs_0_), channel_id=1, source_target_pairs={{0,8},{1,9},{2,10},{3,11},{4,12},{5,13},{6,14},{7,15},{8,128},{9,1... | collective-permute-start | bytes 196616 | tf_op jit(solution)/shard_map/ppermute | solution.py:33
  27.7 47.0 %collective-permute-start.5 = (bf16[16,2048]{1,0:T(8,128)(2,1)S(1)}, bf16[16,2048]{1,0:T(8,128)(2,1)S(1)}, u32[]{:S(2)}, u32[]{:S(2)}) collective-permute-start(bf16[16,2048]{1,0:T(8,128)(2,1)S(1)} %constant_dynamic-slice_fusion.refs_0_), channel_id=1, source_target_pairs={{0,140},{1,141},{2,142},{3,143},{4,0},{5,1},{6,2},{7,3},{8,4},{9,5... | collective-permute-start | bytes 196616 | tf_op jit(solution)/shard_map/ppermute | solution.py:33
  63.4 1.0 copy-start.9
  65.9 9.6 %copy-start.15 = (bf16[2,1,64,2048]{3,2,1,0:T(8,128)(2,1)S(1)}, bf16[2,1,64,2048]{3,2,1,0:T(8,128)(2,1)}, u32[]{:S(2)}) copy-start(bf16[2,1,64,2048]{3,2,1,0:T(8,128)(2,1)} %param.16) | copy-start | bytes 1572868
  65.9 58.1 %all-to-all-start.1 = ((bf16[16,3,2,64,128]{4,3,2,1,0:T(8,128)(2,1)}), bf16[16,3,2,64,128]{4,3,2,1,0:T(8,128)(2,1)}, u32[]{:S(2)}, u32[]{:S(2)}) async-start(bf16[16,3,2,64,128]{4,3,2,1,0:T(8,128)(2,1)} %bitcast.8.after_ref), calls=%async_computation.1 | async-start | bytes 3145728 | tf_op jit(solution)/shard_map/all_to_all | solution.py:221
  74.7 31.8 %all-gather.6.cloned.1.call-start = ((), (), s32[]{:S(2)}) async-start(), calls=%async_computation.5 | async-start | bytes 1769472 | tf_op jit(solution)/shard_map/all_gather | solution.py:258
  76.7 29.8 %copy-start.3 = (bf16[128,2048]{1,0:T(8,128)(2,1)S(1)}, bf16[128,2048]{1,0:T(8,128)(2,1)}, u32[]{:S(2)}) copy-start(bf16[128,2048]{1,0:T(8,128)(2,1)} %refs_4_.1) | copy-start | bytes 1572868
  76.7 26.6 %collective-permute-start.4 = (bf16[128,2048]{1,0:T(8,128)(2,1)S(1)}, bf16[128,2048]{1,0:T(8,128)(2,1)}, u32[]{:S(2)}, u32[]{:S(2)}) collective-permute-start(bf16[128,2048]{1,0:T(8,128)(2,1)S(1)} %bitcast.45), channel_id=1, source_target_pairs={{0,3},{1,2},{2,1},{3,0},{4,7},{5,6},{6,5},{7,4},{8,11},{9,10},{10,... | collective-permute-start | bytes 1572872 | tf_op jit(solution)/shard_map/ppermute | solution.py:33
  76.8 26.5 %collective-permute-start.3 = (bf16[128,2048]{1,0:T(8,128)(2,1)S(1)}, bf16[128,2048]{1,0:T(8,128)(2,1)}, u32[]{:S(2)}, u32[]{:S(2)}) collective-permute-start(bf16[128,2048]{1,0:T(8,128)(2,1)S(1)} %bitcast.46), channel_id=1, source_target_pairs={{0,2},{1,3},{2,0},{3,1},{4,6},{5,7},{6,4},{7,5},{8,10},{9,11},{10,... | collective-permute-start | bytes 1572872 | tf_op jit(solution)/shard_map/ppermute | solution.py:33
  79.4 24.5 %collective-permute-start.2 = (bf16[128,2048]{1,0:T(8,128)(2,1)S(1)}, bf16[128,2048]{1,0:T(8,128)(2,1)}, u32[]{:S(2)}, u32[]{:S(2)}) collective-permute-start(bf16[128,2048]{1,0:T(8,128)(2,1)S(1)} %bitcast.47), channel_id=1, source_target_pairs={{0,1},{1,0},{2,3},{3,2},{4,5},{5,4},{6,7},{7,6},{8,9},{9,8},{10,11... | collective-permute-start | bytes 1572872 | tf_op jit(solution)/shard_map/ppermute | solution.py:33
  80.9 1.0 copy-start.10
  87.6 0.7 copy-start.13
  88.3 37.8 %collective-permute-start.1 = (bf16[8,128,128]{2,1,0:T(8,128)(2,1)}, bf16[8,128,128]{2,1,0:T(8,128)(2,1)}, u32[]{:S(2)}, u32[]{:S(2)}) collective-permute-start(bf16[8,128,128]{2,1,0:T(8,128)(2,1)} %get-tuple-element.26), channel_id=1, source_target_pairs={{0,128},{1,129},{2,130},{3,131},{4,132},{5,133},{6,134},{7,135},{8... | collective-permute-start | bytes 786440 | tf_op jit(solution)/shard_map/ppermute | solution.py:33
  106.5 1.4 copy-start.1
  107.9 18.2 %copy-start.14 = (bf16[8,128,128]{2,1,0:T(8,128)(2,1)S(1)}, bf16[8,128,128]{2,1,0:T(8,128)(2,1)}, u32[]{:S(2)}) copy-start(bf16[8,128,128]{2,1,0:T(8,128)(2,1)} %copy-done.13) | copy-start | bytes 786436
  112.9 25.4 %collective-permute-start.8 = (bf16[4,128,128]{2,1,0:T(8,128)(2,1)}, bf16[4,128,128]{2,1,0:T(8,128)(2,1)S(1)}, u32[]{:S(2)}, u32[]{:S(2)}) collective-permute-start(bf16[4,128,128]{2,1,0:T(8,128)(2,1)} %get-tuple-element.28), channel_id=1, source_target_pairs={{0,4},{1,5},{2,6},{3,7},{4,8},{5,9},{6,10},{7,11},{8,12},{9,13},{1... | collective-permute-start | bytes 393224 | tf_op jit(solution)/shard_map/ppermute | solution.py:266
  115.3 22.9 %collective-permute-start.9 = (bf16[4,128,128]{2,1,0:T(8,128)(2,1)}, bf16[4,128,128]{2,1,0:T(8,128)(2,1)S(1)}, u32[]{:S(2)}, u32[]{:S(2)}) collective-permute-start(bf16[4,128,128]{2,1,0:T(8,128)(2,1)} %get-tuple-element.29), channel_id=1, source_target_pairs={{0,8},{1,9},{2,10},{3,11},{4,12},{5,13},{6,14},{7,15},{8,0},{9,1},... | collective-permute-start | bytes 393224 | tf_op jit(solution)/shard_map/ppermute | solution.py:266
  116.9 21.3 %collective-permute-start.10 = (bf16[4,128,128]{2,1,0:T(8,128)(2,1)S(1)}, bf16[4,128,128]{2,1,0:T(8,128)(2,1)S(1)}, u32[]{:S(2)}, u32[]{:S(2)}) collective-permute-start(bf16[4,128,128]{2,1,0:T(8,128)(2,1)S(1)} %get-tuple-element.30), channel_id=1, source_target_pairs={{0,12},{1,13},{2,14},{3,15},{4,0},{5,1},{6,2},{7,3},{8,4},{9,5},{1... | collective-permute-start | bytes 393224 | tf_op jit(solution)/shard_map/ppermute | solution.py:266
  137.0 1.2 copy-start.2
  138.2 0.7 copy-start.11
  138.9 48.8 %all-to-all-start.2 = ((bf16[16,3,2,64,128]{4,3,2,1,0:T(8,128)(2,1)}), bf16[16,3,2,64,128]{4,3,2,1,0:T(8,128)(2,1)S(1)}, u32[]{:S(2)}, u32[]{:S(2)}) async-start(bf16[16,3,2,64,128]{4,3,2,1,0:T(8,128)(2,1)} %copy-done.2), calls=%async_computation.2 | async-start | bytes 3145728 | tf_op jit(solution)/shard_map/all_to_all | solution.py:221
  147.4 0.9 copy-start.12
  152.7 1.2 copy-start
  187.7 40.9 %all-to-all-start.3 = ((bf16[16,3,2,64,128]{4,3,2,1,0:T(8,128)(2,1)}), bf16[16,3,2,64,128]{4,3,2,1,0:T(8,128)(2,1)S(1)}, u32[]{:S(2)}, u32[]{:S(2)}) async-start(bf16[16,3,2,64,128]{4,3,2,1,0:T(8,128)(2,1)} %copy-done), calls=%async_computation.3 | async-start | bytes 3145728 | tf_op jit(solution)/shard_map/all_to_all | solution.py:221
Sparse Core Ops, SparseCore 0:
  9.9 35.3 all-gather.3
  77.9 28.5 all-gather.5

commit v2 on v1

--- a/solution.py
+++ b/solution.py
@@ -16,6 +16,7 @@
 WHOLE = pl.BlockSpec(memory_space=pltpu.VMEM)
 SCALARS = pl.BlockSpec(memory_space=pltpu.SMEM)
 LATER = pl.BlockSpec(memory_space=pl.ANY)
+IN_HBM = pl.BlockSpec(memory_space=pltpu.HBM)
 
 
 def permutation(move):
@@ -33,6 +34,10 @@
     return lax.ppermute(array, ("space", "tm"), permutation(move))
 
 
+def twin(array):
+    return send(array, lambda z, x, y, c: (z, x, y, 1 - c))
+
+
 def nt(a, b):
     return lax.dot_general(a, b, (((1,), (1,)), ((), ())), preferred_element_type=F32)
 
@@ -52,10 +57,16 @@
 
 
 def pack_kernel(a_ref, b_ref, c_ref, *refs):
-    out_ref = refs[-1]
-    for t, ref in enumerate((a_ref, b_ref, c_ref)):
-        for h in range(16):
-            out_ref[h, t] = ref[:, h * 128 : (h + 1) * 128]
+    out_ref, sems = refs[-2:]
+    copies = [
+        pltpu.make_async_copy(ref.at[:, h * 128 : (h + 1) * 128], out_ref.at[h, t], sems.at[t, h])
+        for h in range(16)
+        for t, ref in enumerate((a_ref, b_ref, c_ref))
+    ]
+    for copy in copies:
+        copy.start()
+    for copy in copies:
+        copy.wait()
 
 
 def pack(a, b, c, *after):
@@ -65,7 +76,9 @@
         jax.ShapeDtypeStruct((16, 3, 128, 128), BF16),
         0,
         3 << 20,
-        in_specs=[WHOLE] * 3 + [LATER] * len(after),
+        in_specs=[IN_HBM] * 3 + [WHOLE] * len(after),
+        out_specs=WHOLE,
+        scratch_shapes=[pltpu.SemaphoreType.DMA((3, 16))],
     )(*flat, *after)
     return out.reshape(16, 3, 2, 64, 128)
 
@@ -82,47 +95,123 @@
     return tuple(v.reshape(2, 1, 64, 2048) for v in outs)
 
 
-def space_proj_kernel(shards_ref, w_own, w_other, after_ref, keep, other):
-    weight = jnp.concatenate([w_own[...], w_other[...]], axis=0)
+def rows_kernel(at_ref, space_ref, time_ref, rows_ref, both_ref, sems):
+    half = space_ref.at[pl.ds(pl.multiple_of(at_ref[0] * 64, 64), 64), :]
+    rows = time_ref.at[pl.ds(pl.multiple_of(at_ref[1] * 64, 64), 64), :]
+    quarter = time_ref.at[pl.ds(pl.multiple_of(at_ref[2] * 32, 32), 32), :]
+    copies = [
+        pltpu.make_async_copy(rows, rows_ref, sems.at[0]),
+        pltpu.make_async_copy(half, both_ref.at[:64], sems.at[1]),
+        pltpu.make_async_copy(quarter, both_ref.at[64:], sems.at[2]),
+    ]
+    for copy in copies:
+        copy.start()
+    for copy in copies:
+        copy.wait()
+
+
+def rows_to_send(at, proj_space, proj_time):
+    return call(
+        rows_kernel,
+        (jax.ShapeDtypeStruct((64, 2048), BF16), jax.ShapeDtypeStruct((96, 2048), BF16)),
+        0,
+        1 << 20,
+        in_specs=[SCALARS] + [IN_HBM] * 2,
+        out_specs=(WHOLE, WHOLE),
+        scratch_shapes=[pltpu.SemaphoreType.DMA((3,))],
+    )(at, proj_space, proj_time)
+
+
+def gathered_kernel(both_ref, rows_ref, half_ref, along_z_ref):
+    half_ref[...] = both_ref[:64]
+    along_z_ref[:64] = rows_ref[...]
+    along_z_ref[64:] = both_ref[64:]
+
+
+def gathered(both, rows):
+    return call(
+        gathered_kernel,
+        (jax.ShapeDtypeStruct((64, 2048), BF16), jax.ShapeDtypeStruct((96, 2048), BF16)),
+        0,
+        1 << 20,
+        in_specs=[WHOLE] * 2,
+    )(both, rows)
+
+
+def pair_kernel(a_ref, b_ref, *refs):
+    out_ref = refs[-1]
+    out_ref[0] = a_ref[...]
+    out_ref[1] = b_ref[...]
+
+
+def pair(a, b, *after):
+    shape = jax.ShapeDtypeStruct((2, 96, 2048), BF16)
+    return call(pair_kernel, shape, 0, 1 << 20, in_specs=[WHOLE] * (2 + len(after)))(a, b, *after)
+
+
+def stack_kernel(a_ref, b_ref, c_ref, d_ref, out_ref):
+    for i, ref in enumerate((a_ref, b_ref, c_ref, d_ref)):
+        out_ref[i] = ref[...]
+
+
+def stacked(shards):
+    shape = jax.ShapeDtypeStruct((4, 128, 2048), BF16)
+    return call(stack_kernel, shape, 0, 4 << 20, in_specs=[WHOLE] * 4)(*shards)
+
+
+def space_proj_kernel(at_ref, *refs):
+    own_ref, twin_ref, w_own, w_half, w_rest = refs[:5]
+    keep, other, weight_ref = refs[-3:]
+    weight_ref[:128] = w_own[...]
+    first = 128 + at_ref[1] * 64
+    rest = 128 + (1 - at_ref[1]) * 64
+    weight_ref[pl.ds(pl.multiple_of(first, 64), 64)] = w_half[...]
+    weight_ref[pl.ds(pl.multiple_of(rest, 64), 64)] = w_rest[...]
     for i in range(8):
-        out = nt(shards_ref[i], weight).astype(BF16)
-        keep[i] = out[:, :128]
-        other[i] = out[:, 128:]
-
-
-def space_proj(shards, w_own, w_other, after):
+        at = at_ref[0] ^ i
+        out = nt((own_ref, twin_ref)[i % 2][i // 2], weight_ref[...]).astype(BF16)
+        keep[at] = out[:, :128]
+        other[at] = out[:, 128:]
+
+
+def space_proj(at, own, twins, w_own, w_half, w_rest, *after):
     shape = jax.ShapeDtypeStruct((8, 128, 128), BF16)
     return call(
         space_proj_kernel,
         (shape, shape),
         1 << 30,
         6 << 20,
-        in_specs=[WHOLE] * 3 + [LATER],
-    )(shards, w_own, w_other, after)
-
-
-def time_proj_kernel(y_ref, *refs):
-    shards, own, pieces_ref, outs, weight_ref = refs[:4], refs[4], refs[5], refs[6:10], refs[10]
+        in_specs=[SCALARS] + [WHOLE] * (5 + len(after)),
+        scratch_shapes=[pltpu.VMEM((256, 2048), BF16)],
+    )(at, own, twins, w_own, w_half, w_rest, *after)
+
+
+def time_proj_kernel(at_ref, *refs):
+    shards, own, pieces, outs, weight_ref = refs[:4], refs[4], refs[5:7], refs[7:11], refs[11]
     weight_ref[:128] = own[...]
-    for i in range(8):
-        for k in range(3):
-            weight_ref[128 * (k + 1) + 16 * i : 128 * (k + 1) + 16 * (i + 1)] = pieces_ref[i, k]
+    for i in range(4):
+        quarter = at_ref[1] ^ i
+        core, half = quarter & 1, quarter >> 1
+        row = 128 * (3 - 2 * core) + 64 * half
+        weight_ref[pl.ds(pl.multiple_of(row, 64), 64)] = pieces[i % 2][i // 2, :64]
+        row = 256 + 32 * quarter
+        weight_ref[pl.ds(pl.multiple_of(row, 32), 32)] = pieces[i % 2][i // 2, 64:]
     for i in range(4):
         out = nt(shards[i][...], weight_ref[...]).astype(BF16)
         for k in range(4):
-            outs[k][y_ref[0] ^ i] = out[:, k * 128 : (k + 1) * 128]
-
-
-def time_proj(y, shards, own, pieces):
+            outs[k][at_ref[0] ^ i] = out[:, k * 128 : (k + 1) * 128]
+
+
+def time_proj(at, shards, own, rows, twin_rows):
     shape = jax.ShapeDtypeStruct((4, 128, 128), BF16)
     return call(
         time_proj_kernel,
         (shape,) * 4,
         1 << 30,
         5 << 20,
-        in_specs=[SCALARS] + [WHOLE] * 6,
+        in_specs=[SCALARS] + [WHOLE] * 7,
         scratch_shapes=[pltpu.VMEM((512, 2048), BF16)],
-    )(y, *shards, own, pieces)
+    )(at, *shards, own, rows, twin_rows)
 
 
 def attend(q, k, v, o, k_t, mask):
@@ -237,30 +326,40 @@
     z_hi, xc = place_s // 8, place_s % 8
     z_lo, y = place_t // 4, place_t % 4
 
-    halves = [[z * 8 + i for i in range(8)] for z in range(2)]
-    shards = lax.all_gather(block_grad.reshape(128, 2048), "space", axis_index_groups=halves)
-    rows = lax.dynamic_slice_in_dim(proj_time, xc * 16, 16, 0)
-    time_packed = pack(query_time, key_time, value_time, rows)
-    time_in = exchange(time_packed, "tm")
-    w_other = send(proj_space, lambda z, x, y, c: (z + (-2 if z % 4 < 2 else 2), x, y, c))
-    piece = jnp.stack(
-        [
-            send(rows, lambda z, x, y, c: (z - 1, x, y, c)),
-            send(rows, lambda z, x, y, c: (z + 2 - 4 * c, x, y, c)),
-            send(rows, lambda z, x, y, c: (z + 1, x, y, c)),
-        ]
-    )
-
-    space_packed = pack(query_space, key_space, value_space, time_in, w_other)
-    space_in = exchange(space_packed, "space")
-    keep, other = space_proj(shards, proj_space, w_other, space_packed)
-    got = send(other, lambda z, x, y, c: (z + 4, x, y, c))
-    pieces = lax.all_gather(piece, "space", axis_index_groups=halves)
+    time_in = exchange(pack(query_time, key_time, value_time), "tm")
+    grad = block_grad.reshape(128, 2048)
+    along_x = stacked(
+        [grad] + [send(grad, lambda z, x, y, c, k=k: (z, x ^ k, y, c)) for k in (1, 2, 3)]
+    )
+    half = xc // 2 % 2
+    rows, both = rows_to_send(jnp.stack([y % 2, half, xc % 4]), proj_space, proj_time)
+    both = send(both, lambda z, x, y, c: (z + (-2 if z % 4 < 2 else 2), x, y, c))
+    rows = send(rows, lambda z, x, y, c: (z + 1 - 2 * c, x, y, c))
+    w_half, along_z = gathered(both, rows)
     cotangent = (block_grad.astype(F32) + branch_grad.astype(F32)).astype(BF16).reshape(128, 2048)
     along_y = [cotangent] + [
         send(cotangent, lambda z, x, y, c, k=k: (z, x, y ^ k, c)) for k in (1, 2, 3)
     ]
-    outs = time_proj(y.reshape(1), along_y, proj_time, pieces)
+
+    space_packed = pack(
+        query_space, key_space, value_space, along_x, w_half, along_z, along_y[1]
+    )
+    space_packed, time_in = lax.optimization_barrier((space_packed, time_in))
+    space_in = exchange(space_packed, "space")
+    w_rest = send(w_half, lambda z, x, y, c: (z, x, y ^ 1, c))
+    along_z2 = send(along_z, lambda z, x, y, c: (z, x ^ 1, y, c))
+    keep, other = space_proj(
+        jnp.stack([xc, y % 2]),
+        along_x,
+        twin(along_x),
+        proj_space,
+        w_half,
+        w_rest,
+        along_y[2],
+    )
+    got = send(other, lambda z, x, y, c: (z + 4, x, y, c))
+    pieces = pair(along_z, along_z2, keep, along_y[3])
+    outs = time_proj(jnp.stack([y, xc % 4]), along_y, proj_time, pieces, twin(pieces))
 
     parts = [outs[0]] + [
         lax.ppermute(outs[k], "tm", [(t, (t // 4 + k) % 4 * 4 + t % 4) for t in range(16)])

time: 238 us -> 223 us (0.937)
  waiting for transfers between devices: 124 us -> 94.2 us
  starting transfers between devices: 52.7 us -> 71.1 us
  between operations: 14.2 us -> 0.84 us
  Pallas kernels: 32 us -> 39 us
  local copies, waits for them, and re-layouts: 12.1 us -> 15.2 us
    all_to_all x4, waiting for transfers between devices: 77.3 us -> 56.5 us  [exchange(): return lax.all_to_all(array, axis, split_axis=0, concat_axis=0, tiled=True)]
    all_to_all x4, starting transfers between devices: 29.9 us -> 44.3 us  [exchange(): return lax.all_to_all(array, axis, split_axis=0, concat_axis=0, tiled=True)]
    ppermute x8 -> x13, waiting for transfers between devices: 43.6 us -> 36.6 us  [send(): return lax.ppermute(array, ('space', 'tm'), permutation(move))]
    ppermute x8 -> x13, starting transfers between devices: 16.6 us -> 22.8 us  [send(): return lax.ppermute(array, ('space', 'tm'), permutation(move))]
    pallas_call x1 -> x5, Pallas kernels: 5.68 us -> 9.7 us  [the longest x1 5.84 us: space_proj(): call(space_proj_kernel, (shape, shape), 1 << 30, 6 << 20, in_specs=[SCALA...]
    unnamed x32 -> x48, local copies, waits for them, and re-layouts: 11.2 us -> 15.2 us
    pallas_call x2, Pallas kernels: 2.86 us -> 5.91 us  [pack(): call(pack_kernel, jax.ShapeDtypeStruct((16, 3, 128, 128), BF16), 0, 3 <<...]
    all_gather x2 -> x0, waiting for transfers between devices: 2.57 us -> none  [the longest x1 2.57 us: on_device(): pieces = lax.all_gather(piece, 'space', axis_index_groups=halves)]
  transfers between devices with their start and end apart: 17 -> 20, of which waited for: 9 -> 10; matrix products, arithmetic and copies ran while one was open for 1% -> 1% of each run, Pallas kernels for 13% -> 16%
where the time goes in v2:
time: 223 us; the launch traced here: 222 us
  waiting for transfers between devices  94.2 us (42%)
  starting transfers between devices  71.1 us (32%)
  Pallas kernels  39 us (17%)
  local copies, waits for them, and re-layouts  15.2 us (7%)
    all_to_all x4, waiting for transfers between devices, exchange(): return lax.all_to_all(array, axis, split_axis=0, concat_axis=0, tiled=True)  56.5 us
    all_to_all x4, starting transfers between devices, exchange(): return lax.all_to_all(array, axis, split_axis=0, concat_axis=0, tiled=True)  44.3 us
    ppermute x13, waiting for transfers between devices, send(): return lax.ppermute(array, ('space', 'tm'), permutation(move))  36.6 us
    ppermute x13, starting transfers between devices, send(): return lax.ppermute(array, ('space', 'tm'), permutation(move))  22.8 us
    unnamed x48, local copies, waits for them, and re-layouts  15.2 us
    pallas_call x1, Pallas kernels, space_attention(): call(space_kernel, jax.ShapeDtypeStruct((16, 3, 2, 64, 128), BF16), 5 * (...  10.9 us
    pallas_call x2, Pallas kernels, pack(): call(pack_kernel, jax.ShapeDtypeStruct((16, 3, 128, 128), BF16), 0, 3 <<...  5.91 us
    pallas_call x1, Pallas kernels, space_proj(): call(space_proj_kernel, (shape, shape), 1 << 30, 6 << 20, in_specs=[SCALA...  5.84 us
  transfers between devices with their start and end apart: 20, of which 10 were waited for; matrix products, arithmetic and copies ran while one was open for 1% of the time, Pallas kernels for 16%

profile of v2, /device:TPU:38, one launch (start us, length us, event | category | flops | bytes accessed | tf_op | source)
XLA Modules:
  0.0 221.7 jit_solution(18347862670829976356)
XLA Ops:
  0.6 1.0 copy-done.16
  1.7 1.0 copy-done.17
  2.7 1.0 copy-done.18
  3.8 2.1 shard_map.149
  5.9 0.0 copy-start.23
  5.9 8.8 %all-to-all-start = ((bf16[16,3,2,64,128]{4,3,2,1,0:T(8,128)(2,1)}), bf16[16,3,2,64,128]{4,3,2,1,0:T(8,128)(2,1)S(1)}, u32[]{:S(2)}, u32[]{:S(2)}) async-start(bf16[16,3,2,64,128]{4,3,2,1,0:T(8,128)(2,1)} %bitcast.13), calls=%async_computation | async-start | bytes 3145728 | tf_op jit(solution)/shard_map/all_to_all | solution.py:310
  14.7 0.9 collective-permute-start
  15.6 1.1 collective-permute-start.1
  16.7 2.8 %collective-permute-start.2 = (bf16[128,2048]{1,0:T(8,128)(2,1)}, bf16[128,2048]{1,0:T(8,128)(2,1)}, u32[]{:S(2)}, u32[]{:S(2)}) collective-permute-start(bf16[128,2048]{1,0:T(8,128)(2,1)} %bitcast.4.a_ref), channel_id=1, source_target_pairs={{0,96},{1,97},{2,98},{3,99},{4,100},{5,101},{6,102},{7,103},{8,104... | collective-permute-start | bytes 1572872 | tf_op jit(solution)/shard_map/ppermute | solution.py:34
  19.5 1.2 add_convert_fusion
  20.7 1.6 collective-permute-start.5
  22.3 0.1 pad_add_fusion.at_ref
  22.3 1.0 copy-done.4
  23.4 0.8 shard_map.146
  24.2 4.6 %collective-permute-start.3 = (bf16[96,2048]{1,0:T(8,128)(2,1)S(1)}, bf16[96,2048]{1,0:T(8,128)(2,1)S(1)}, u32[]{:S(2)}, u32[]{:S(2)}) collective-permute-start(bf16[96,2048]{1,0:T(8,128)(2,1)S(1)} %get-tuple-element.31), channel_id=1, source_target_pairs={{0,136},{1,137},{2,138},{3,139},{4,140},{5,141},{6,142},{7,143},{8... | collective-permute-start | bytes 1179656 | tf_op jit(solution)/shard_map/ppermute | solution.py:34
  28.8 1.2 collective-permute-done.b_ref
  30.0 1.5 collective-permute-start.4
  31.5 8.0 %collective-permute-done.1.c_ref = bf16[128,2048]{1,0:T(8,128)(2,1)} collective-permute-done((bf16[128,2048]{1,0:T(8,128)(2,1)}, bf16[128,2048]{1,0:T(8,128)(2,1)}, u32[]{:S(2)}, u32[]{:S(2)}) %collective-permute-start.1) | collective-permute-done | bytes 524320 | tf_op jit(solution)/shard_map/ppermute | solution.py:34
  39.5 2.6 %collective-permute-done.2.d_ref = bf16[128,2048]{1,0:T(8,128)(2,1)} collective-permute-done((bf16[128,2048]{1,0:T(8,128)(2,1)}, bf16[128,2048]{1,0:T(8,128)(2,1)}, u32[]{:S(2)}, u32[]{:S(2)}) %collective-permute-start.2) | collective-permute-done | bytes 524320 | tf_op jit(solution)/shard_map/ppermute | solution.py:34
  42.0 3.0 %shard_map.145.refs_0_ = bf16[4,128,2048]{2,1,0:T(8,128)(2,1)} custom-call(bf16[128,2048]{1,0:T(8,128)(2,1)} %bitcast.4.a_ref, bf16[128,2048]{1,0:T(8,128)(2,1)} %collective-permute-done.b_ref, bf16[128,2048]{1,0:T(8,128)(2,1)} %collective-permute-done.1.c_ref, bf16[128,2048]{1,0:T(8,128)(2,1)} %collective-permute-done.2.d_ref), custom_call_target="tpu_custom_call" | custom-call | bytes 4194304 | tf_op jit(solution)/shard_map/pallas_call | solution.py:159
  45.0 7.0 %collective-permute-done.4.rows_ref = bf16[64,2048]{1,0:T(8,128)(2,1)S(1)} collective-permute-done((bf16[64,2048]{1,0:T(8,128)(2,1)S(1)}, bf16[64,2048]{1,0:T(8,128)(2,1)S(1)}, u32[]{:S(2)}, u32[]{:S(2)}) %collective-permute-start.4) | collective-permute-done | bytes 262176 | tf_op jit(solution)/shard_map/ppermute | solution.py:34
  52.0 0.0 collective-permute-done.3.both_ref
  52.1 0.0 copy-start.8
  52.1 3.8 %shard_map.148 = bf16[16,3,128,128]{3,2,1,0:T(8,128)(2,1)} custom-call(bf16[128,2048]{1,0:T(8,128)(2,1)S(1)} %bitcast.49, bf16[128,2048]{1,0:T(8,128)(2,1)S(1)} %bitcast.50, bf16[128,2048]{1,0:T(8,128)(2,1)S(1)} %bitcast.51, bf16[4,128,2048]{2,1,0:T(8,128)(2,1)} %shard_map.145.refs_0_, bf16[64,2048]{1,0:T(8,128)(2,1)S(1)} %get-tuple-element.33.refs_1_.refs_3_, ...), custom_call_target="tpu_custom_call" | custom-call | bytes 3145728 | tf_op jit(solution)/shard_map/pallas_call | solution.py:74
  55.9 0.0 copy-start.11
  55.9 0.7 copy-done.11
  56.6 0.0 all-to-all-done.qkv_ref
  56.6 9.2 %all-to-all-start.1 = ((bf16[16,3,2,64,128]{4,3,2,1,0:T(8,128)(2,1)}), bf16[16,3,2,64,128]{4,3,2,1,0:T(8,128)(2,1)}, u32[]{:S(2)}, u32[]{:S(2)}) async-start(bf16[16,3,2,64,128]{4,3,2,1,0:T(8,128)(2,1)} %bitcast.9), calls=%async_computation.1 | async-start | bytes 3145728 | tf_op jit(solution)/shard_map/all_to_all | solution.py:310
  65.8 3.0 %collective-permute-start.8 = (bf16[128,2048]{1,0:T(8,128)(2,1)S(1)}, bf16[128,2048]{1,0:T(8,128)(2,1)S(1)}, u32[]{:S(2)}, u32[]{:S(2)}) collective-permute-start(bf16[128,2048]{1,0:T(8,128)(2,1)S(1)} %bitcast.46), channel_id=1, source_target_pairs={{0,2},{1,3},{2,0},{3,1},{4,6},{5,7},{6,4},{7,5},{8,10},{9,11},{10,... | collective-permute-start | bytes 1572872 | tf_op jit(solution)/shard_map/ppermute | solution.py:34
  68.8 1.2 collective-permute-start.10
  70.0 0.9 collective-permute-start.11
  70.8 0.1 pad_add_fusion.1.at_ref
  70.9 11.2 %collective-permute-done.8.refs_5_.refs_2_ = bf16[128,2048]{1,0:T(8,128)(2,1)S(1)} collective-permute-done((bf16[128,2048]{1,0:T(8,128)(2,1)S(1)}, bf16[128,2048]{1,0:T(8,128)(2,1)S(1)}, u32[]{:S(2)}, u32[]{:S(2)}) %collective-permute-start.8) | collective-permute-done | bytes 524320 | tf_op jit(solution)/shard_map/ppermute | solution.py:34
  82.2 4.8 %collective-permute-done.7.refs_4_ = bf16[64,2048]{1,0:T(8,128)(2,1)S(1)} collective-permute-done((bf16[64,2048]{1,0:T(8,128)(2,1)}, bf16[64,2048]{1,0:T(8,128)(2,1)S(1)}, u32[]{:S(2)}, u32[]{:S(2)}) %collective-permute-start.7) | collective-permute-done | bytes 262176 | tf_op jit(solution)/shard_map/ppermute | solution.py:34
  87.0 0.9 copy-done.12
  88.0 5.8 %shard_map.150 = (bf16[8,128,128]{2,1,0:T(8,128)(2,1)S(1)}, bf16[8,128,128]{2,1,0:T(8,128)(2,1)}) custom-call(s32[2]{0:T(128)S(1)} %pad_add_fusion.1.at_ref, bf16[4,128,2048]{2,1,0:T(8,128)(2,1)} %shard_map.145.refs_0_, bf16[4,128,2048]{2,1,0:T(8,128)(2,1)} %collective-permute-done.6.refs_1_, bf16[128,2048]{1,0:T(8,128)(2,1)S(1)} %copy-done.3, ...), custom_call_target="tpu_custom_call" | custom-call | flops 1073741824 | bytes 6291456 | tf_op jit(solution)/shard_map/pallas_call | solution.py:179
  93.8 0.1 shard_map.151.refs_5_
  93.9 0.6 copy-done.19
  94.5 0.8 copy-done.6
  95.3 5.4 %collective-permute-start.9 = (bf16[8,128,128]{2,1,0:T(8,128)(2,1)}, bf16[8,128,128]{2,1,0:T(8,128)(2,1)}, u32[]{:S(2)}, u32[]{:S(2)}) collective-permute-start(bf16[8,128,128]{2,1,0:T(8,128)(2,1)} %get-tuple-element.37), channel_id=1, source_target_pairs={{0,128},{1,129},{2,130},{3,131},{4,132},{5,133},{6,134},{7,135},{8... | collective-permute-start | bytes 786440 | tf_op jit(solution)/shard_map/ppermute | solution.py:34
  100.7 0.1 pad_add_fusion.2.at_ref
  100.8 1.0 copy-done.2
  101.8 1.0 copy-done.5
  102.8 1.0 copy-done.7
  103.9 4.9 %shard_map.152 = (bf16[4,128,128]{2,1,0:T(8,128)(2,1)S(1)}, bf16[4,128,128]{2,1,0:T(8,128)(2,1)}, bf16[4,128,128]{2,1,0:T(8,128)(2,1)}, bf16[4,128,128]{2,1,0:T(8,128)(2,1)}) custom-call(s32[2]{0:T(128)S(1)} %pad_add_fusion.2.at_ref, bf16[128,2048]{1,0:T(8,128)(2,1)S(1)} %bitcast.48, bf16[128,2048]{1,0:T(8,128)(2,1)S(1)} %collective-permute-done.5.refs_3_.refs_1_, ...), custom_call_target="tpu_custom_call" | custom-call | flops 1073741824 | bytes 5242880 | tf_op jit(solution)/shard_map/pallas_call | solution.py:207
  108.8 1.5 collective-permute-start.13
  110.3 0.8 collective-permute-start.14
  111.1 1.7 collective-permute-start.15
  112.8 1.7 collective-permute-done.9
  114.5 0.9 copy-done.20
  115.4 10.9 %shard_map.153 = bf16[16,3,2,64,128]{4,3,2,1,0:T(8,128)(2,1)S(1)} custom-call(s32[1]{0:T(128)} %bitcast.pos_ref, bf16[16,3,2,64,128]{4,3,2,1,0:T(8,128)(2,1)} %all-to-all-done.1.qkv_ref, bf16[8,2,64,128]{3,2,1,0:T(8,128)(2,1)S(1)} %bitcast.55, bf16[8,2,64,128]{3,2,1,0:T(8,128)(2,1)} %bitcast.16.got_ref, bf16[4,128,128]{2,1,0:T(8,128)(2,1)S(1)} %get-tuple-element.44.after_ref), custom_call_target="tpu_custom_call" | custom-call | flops 2684354560 | bytes 4194304 | tf_op jit(solution)/shard_map/pallas_call | solution.py:259
  126.4 1.2 copy-done.10
  127.6 0.0 collective-permute-done.14
  127.6 1.1 collective-permute-done.15
  128.6 0.7 copy-done.21
  129.3 5.3 %all-to-all-start.2 = ((bf16[16,3,2,64,128]{4,3,2,1,0:T(8,128)(2,1)}), bf16[16,3,2,64,128]{4,3,2,1,0:T(8,128)(2,1)S(1)}, u32[]{:S(2)}, u32[]{:S(2)}) async-start(bf16[16,3,2,64,128]{4,3,2,1,0:T(8,128)(2,1)} %copy-done.10), calls=%async_computation.2 | async-start | bytes 3145728 | tf_op jit(solution)/shard_map/all_to_all | solution.py:310
  134.6 0.9 copy-done.22
  135.5 4.4 %shard_map.154 = bf16[16,3,2,64,128]{4,3,2,1,0:T(8,128)(2,1)S(1)} custom-call(s32[1]{0:T(128)} %bitcast.18.pos_ref, bf16[16,3,2,64,128]{4,3,2,1,0:T(8,128)(2,1)S(1)} %all-to-all-done.qkv_ref, bf16[4,2,64,128]{3,2,1,0:T(8,128)(2,1)S(1)} %bitcast.56, bf16[4,2,64,128]{3,2,1,0:T(8,128)(2,1)S(1)} %bitcast.57, bf16[4,2,64,128]{3,2,1,0:T(8,128)(2,1)S(1)} %bitcast.58, ...), custom_call_target="tpu_custom_call" | custom-call | flops 671088640 | bytes 4194304 | tf_op jit(solution)/shard_map/pallas_call | solution.py:297
  140.0 1.1 copy-done
  141.1 21.1 %all-to-all-done.2 = bf16[16,3,2,64,128]{4,3,2,1,0:T(8,128)(2,1)S(1)} async-done(((bf16[16,3,2,64,128]{4,3,2,1,0:T(8,128)(2,1)}), bf16[16,3,2,64,128]{4,3,2,1,0:T(8,128)(2,1)S(1)}, u32[]{:S(2)}, u32[]{:S(2)}) %all-to-all-start.2) | async-done | bytes 1572896 | tf_op jit(solution)/shard_map/all_to_all | solution.py:310
  162.2 21.0 %all-to-all-start.3 = ((bf16[16,3,2,64,128]{4,3,2,1,0:T(8,128)(2,1)}), bf16[16,3,2,64,128]{4,3,2,1,0:T(8,128)(2,1)S(1)}, u32[]{:S(2)}, u32[]{:S(2)}) async-start(bf16[16,3,2,64,128]{4,3,2,1,0:T(8,128)(2,1)} %copy-done), calls=%async_computation.3 | async-start | bytes 3145728 | tf_op jit(solution)/shard_map/all_to_all | solution.py:310
  183.2 1.5 shard_map.155
  184.7 35.4 %all-to-all-done.3 = bf16[16,3,2,64,128]{4,3,2,1,0:T(8,128)(2,1)S(1)} async-done(((bf16[16,3,2,64,128]{4,3,2,1,0:T(8,128)(2,1)}), bf16[16,3,2,64,128]{4,3,2,1,0:T(8,128)(2,1)S(1)}, u32[]{:S(2)}, u32[]{:S(2)}) %all-to-all-start.3) | async-done | bytes 1572896 | tf_op jit(solution)/shard_map/all_to_all | solution.py:310
  220.1 1.5 shard_map.156
  (40 shorter events, 0.1 us)
Async XLA Ops:
  0.6 1.0 copy-start.16
  1.7 1.0 copy-start.17
  2.7 1.0 copy-start.18
  5.9 13.6 %copy-start.23 = (bf16[2,1,64,2048]{3,2,1,0:T(8,128)(2,1)S(1)}, bf16[2,1,64,2048]{3,2,1,0:T(8,128)(2,1)}, u32[]{:S(2)}) copy-start(bf16[2,1,64,2048]{3,2,1,0:T(8,128)(2,1)} %param.17) | copy-start | bytes 1572868
  5.9 50.7 %all-to-all-start = ((bf16[16,3,2,64,128]{4,3,2,1,0:T(8,128)(2,1)}), bf16[16,3,2,64,128]{4,3,2,1,0:T(8,128)(2,1)S(1)}, u32[]{:S(2)}, u32[]{:S(2)}) async-start(bf16[16,3,2,64,128]{4,3,2,1,0:T(8,128)(2,1)} %bitcast.13), calls=%async_computation | async-start | bytes 3145728 | tf_op jit(solution)/shard_map/all_to_all | solution.py:310
  14.7 7.6 %copy-start.3 = (bf16[128,2048]{1,0:T(8,128)(2,1)S(1)}, bf16[128,2048]{1,0:T(8,128)(2,1)}, u32[]{:S(2)}) copy-start(bf16[128,2048]{1,0:T(8,128)(2,1)} %refs_2_.1) | copy-start | bytes 1572868
  14.7 15.3 %collective-permute-start = (bf16[128,2048]{1,0:T(8,128)(2,1)}, bf16[128,2048]{1,0:T(8,128)(2,1)}, u32[]{:S(2)}, u32[]{:S(2)}) collective-permute-start(bf16[128,2048]{1,0:T(8,128)(2,1)} %bitcast.4.a_ref), channel_id=1, source_target_pairs={{0,32},{1,33},{2,34},{3,35},{4,36},{5,37},{6,38},{7,39},{8,40},{9,... | collective-permute-start | bytes 1572872 | tf_op jit(solution)/shard_map/ppermute | solution.py:34
  15.6 23.8 %collective-permute-start.1 = (bf16[128,2048]{1,0:T(8,128)(2,1)}, bf16[128,2048]{1,0:T(8,128)(2,1)}, u32[]{:S(2)}, u32[]{:S(2)}) collective-permute-start(bf16[128,2048]{1,0:T(8,128)(2,1)} %bitcast.4.a_ref), channel_id=1, source_target_pairs={{0,64},{1,65},{2,66},{3,67},{4,68},{5,69},{6,70},{7,71},{8,72},{9,... | collective-permute-start | bytes 1572872 | tf_op jit(solution)/shard_map/ppermute | solution.py:34
  16.7 25.3 %collective-permute-start.2 = (bf16[128,2048]{1,0:T(8,128)(2,1)}, bf16[128,2048]{1,0:T(8,128)(2,1)}, u32[]{:S(2)}, u32[]{:S(2)}) collective-permute-start(bf16[128,2048]{1,0:T(8,128)(2,1)} %bitcast.4.a_ref), channel_id=1, source_target_pairs={{0,96},{1,97},{2,98},{3,99},{4,100},{5,101},{6,102},{7,103},{8,104... | collective-permute-start | bytes 1572872 | tf_op jit(solution)/shard_map/ppermute | solution.py:34
  20.7 31.4 %collective-permute-start.5 = (bf16[128,2048]{1,0:T(8,128)(2,1)S(1)}, bf16[128,2048]{1,0:T(8,128)(2,1)S(1)}, u32[]{:S(2)}, u32[]{:S(2)}) collective-permute-start(bf16[128,2048]{1,0:T(8,128)(2,1)S(1)} %bitcast.45), channel_id=1, source_target_pairs={{0,1},{1,0},{2,3},{3,2},{4,5},{5,4},{6,7},{7,6},{8,9},{9,8},{10,11... | collective-permute-start | bytes 1572872 | tf_op jit(solution)/shard_map/ppermute | solution.py:34
  22.3 1.0 copy-start.4
  24.2 27.8 %collective-permute-start.3 = (bf16[96,2048]{1,0:T(8,128)(2,1)S(1)}, bf16[96,2048]{1,0:T(8,128)(2,1)S(1)}, u32[]{:S(2)}, u32[]{:S(2)}) collective-permute-start(bf16[96,2048]{1,0:T(8,128)(2,1)S(1)} %get-tuple-element.31), channel_id=1, source_target_pairs={{0,136},{1,137},{2,138},{3,139},{4,140},{5,141},{6,142},{7,143},{8... | collective-permute-start | bytes 1179656 | tf_op jit(solution)/shard_map/ppermute | solution.py:34
  30.0 22.1 %copy-start.13 = (bf16[2,1,64,2048]{3,2,1,0:T(8,128)(2,1)S(1)}, bf16[2,1,64,2048]{3,2,1,0:T(8,128)(2,1)}, u32[]{:S(2)}) copy-start(bf16[2,1,64,2048]{3,2,1,0:T(8,128)(2,1)} %param.10) | copy-start | bytes 1572868
  30.0 22.1 %copy-start.14 = (bf16[2,1,64,2048]{3,2,1,0:T(8,128)(2,1)S(1)}, bf16[2,1,64,2048]{3,2,1,0:T(8,128)(2,1)}, u32[]{:S(2)}) copy-start(bf16[2,1,64,2048]{3,2,1,0:T(8,128)(2,1)} %param.11) | copy-start | bytes 1572868
  30.0 22.1 %copy-start.15 = (bf16[2,1,64,2048]{3,2,1,0:T(8,128)(2,1)S(1)}, bf16[2,1,64,2048]{3,2,1,0:T(8,128)(2,1)}, u32[]{:S(2)}) copy-start(bf16[2,1,64,2048]{3,2,1,0:T(8,128)(2,1)} %param.12) | copy-start | bytes 1572868
  30.0 22.0 %collective-permute-start.4 = (bf16[64,2048]{1,0:T(8,128)(2,1)S(1)}, bf16[64,2048]{1,0:T(8,128)(2,1)S(1)}, u32[]{:S(2)}, u32[]{:S(2)}) collective-permute-start(bf16[64,2048]{1,0:T(8,128)(2,1)S(1)} %get-tuple-element.32), channel_id=1, source_target_pairs={{0,4},{1,5},{2,6},{3,7},{4,8},{5,9},{6,10},{7,11},{8,12},{9,13},{1... | collective-permute-start | bytes 786440 | tf_op jit(solution)/shard_map/ppermute | solution.py:34
  45.0 42.0 %collective-permute-start.6 = (bf16[4,128,2048]{2,1,0:T(8,128)(2,1)}, bf16[4,128,2048]{2,1,0:T(8,128)(2,1)}, u32[]{:S(2)}, u32[]{:S(2)}) collective-permute-start(bf16[4,128,2048]{2,1,0:T(8,128)(2,1)} %shard_map.145.refs_0_), channel_id=1, source_target_pairs={{0,16},{1,17},{2,18},{3,19},{4,20},{5,21},{6,22},{7,23},{8,24},{9,... | collective-permute-start | bytes 6291464 | tf_op jit(solution)/shard_map/ppermute | solution.py:34
  52.1 17.9 %copy-start.8 = (bf16[96,2048]{1,0:T(8,128)(2,1)}, bf16[96,2048]{1,0:T(8,128)(2,1)S(1)}, u32[]{:S(2)}) copy-start(bf16[96,2048]{1,0:T(8,128)(2,1)S(1)} %get-tuple-element.34.refs_2_.a_ref) | copy-start | bytes 1179652
  55.9 0.7 copy-start.11
  56.6 57.9 %all-to-all-start.1 = ((bf16[16,3,2,64,128]{4,3,2,1,0:T(8,128)(2,1)}), bf16[16,3,2,64,128]{4,3,2,1,0:T(8,128)(2,1)}, u32[]{:S(2)}, u32[]{:S(2)}) async-start(bf16[16,3,2,64,128]{4,3,2,1,0:T(8,128)(2,1)} %bitcast.9), calls=%async_computation.1 | async-start | bytes 3145728 | tf_op jit(solution)/shard_map/all_to_all | solution.py:310
  65.8 16.3 %collective-permute-start.8 = (bf16[128,2048]{1,0:T(8,128)(2,1)S(1)}, bf16[128,2048]{1,0:T(8,128)(2,1)S(1)}, u32[]{:S(2)}, u32[]{:S(2)}) collective-permute-start(bf16[128,2048]{1,0:T(8,128)(2,1)S(1)} %bitcast.46), channel_id=1, source_target_pairs={{0,2},{1,3},{2,0},{3,1},{4,6},{5,7},{6,4},{7,5},{8,10},{9,11},{10,... | collective-permute-start | bytes 1572872 | tf_op jit(solution)/shard_map/ppermute | solution.py:34
  68.8 25.0 %collective-permute-start.10 = (bf16[128,2048]{1,0:T(8,128)(2,1)S(1)}, bf16[128,2048]{1,0:T(8,128)(2,1)S(1)}, u32[]{:S(2)}, u32[]{:S(2)}) collective-permute-start(bf16[128,2048]{1,0:T(8,128)(2,1)S(1)} %bitcast.47), channel_id=1, source_target_pairs={{0,3},{1,2},{2,1},{3,0},{4,7},{5,6},{6,5},{7,4},{8,11},{9,10},{10,... | collective-permute-start | bytes 1572872 | tf_op jit(solution)/shard_map/ppermute | solution.py:34
  70.0 23.8 %collective-permute-start.11 = (bf16[96,2048]{1,0:T(8,128)(2,1)S(1)}, bf16[96,2048]{1,0:T(8,128)(2,1)S(1)}, u32[]{:S(2)}, u32[]{:S(2)}) collective-permute-start(bf16[96,2048]{1,0:T(8,128)(2,1)S(1)} %get-tuple-element.34.refs_2_.a_ref), channel_id=1, source_target_pairs={{0,32},{1,33},{2,34},{3,35},{4,36},{5,37},{6,38},{7,39},{8,40},{9,... | collective-permute-start | bytes 1179656 | tf_op jit(solution)/shard_map/ppermute | solution.py:34
  70.8 16.2 %collective-permute-start.7 = (bf16[64,2048]{1,0:T(8,128)(2,1)}, bf16[64,2048]{1,0:T(8,128)(2,1)S(1)}, u32[]{:S(2)}, u32[]{:S(2)}) collective-permute-start(bf16[64,2048]{1,0:T(8,128)(2,1)} %copy-done.11), channel_id=1, source_target_pairs={{0,1},{1,0},{2,3},{3,2},{4,5},{5,4},{6,7},{7,6},{8,9},{9,8},{10,11... | collective-permute-start | bytes 786440 | tf_op jit(solution)/shard_map/ppermute | solution.py:34
  70.9 22.9 %copy-start.9 = (bf16[96,2048]{1,0:T(8,128)(2,1)S(1)}, bf16[96,2048]{1,0:T(8,128)(2,1)}, u32[]{:S(2)}) copy-start(bf16[96,2048]{1,0:T(8,128)(2,1)} %copy-done.8) | copy-start | bytes 1179652
  82.2 11.6 %copy-start.1 = (bf16[128,2048]{1,0:T(8,128)(2,1)}, bf16[128,2048]{1,0:T(8,128)(2,1)S(1)}, u32[]{:S(2)}) copy-start(bf16[128,2048]{1,0:T(8,128)(2,1)S(1)} %collective-permute-done.8.refs_5_.refs_2_) | copy-start | bytes 1572868
  87.0 1.0 copy-start.12
  93.8 0.7 copy-start.19
  94.5 0.8 copy-start.6
  95.3 5.5 %collective-permute-start.12 = (bf16[2,96,2048]{2,1,0:T(8,128)(2,1)S(1)}, bf16[2,96,2048]{2,1,0:T(8,128)(2,1)}, u32[]{:S(2)}, u32[]{:S(2)}) collective-permute-start(bf16[2,96,2048]{2,1,0:T(8,128)(2,1)S(1)} %shard_map.151.refs_5_), channel_id=1, source_target_pairs={{0,16},{1,17},{2,18},{3,19},{4,20},{5,21},{6,22},{7,23},{8,24},{9,... | collective-permute-start | bytes 2359304 | tf_op jit(solution)/shard_map/ppermute | solution.py:34
  95.3 19.2 %collective-permute-start.9 = (bf16[8,128,128]{2,1,0:T(8,128)(2,1)}, bf16[8,128,128]{2,1,0:T(8,128)(2,1)}, u32[]{:S(2)}, u32[]{:S(2)}) collective-permute-start(bf16[8,128,128]{2,1,0:T(8,128)(2,1)} %get-tuple-element.37), channel_id=1, source_target_pairs={{0,128},{1,129},{2,130},{3,131},{4,132},{5,133},{6,134},{7,135},{8... | collective-permute-start | bytes 786440 | tf_op jit(solution)/shard_map/ppermute | solution.py:34
  100.8 1.0 copy-start.2
  101.8 1.0 copy-start.5
  102.8 1.0 copy-start.7
  108.8 18.8 %collective-permute-start.13 = (bf16[4,128,128]{2,1,0:T(8,128)(2,1)}, bf16[4,128,128]{2,1,0:T(8,128)(2,1)S(1)}, u32[]{:S(2)}, u32[]{:S(2)}) collective-permute-start(bf16[4,128,128]{2,1,0:T(8,128)(2,1)} %get-tuple-element.39), channel_id=1, source_target_pairs={{0,4},{1,5},{2,6},{3,7},{4,8},{5,9},{6,10},{7,11},{8,12},{9,13},{1... | collective-permute-start | bytes 393224 | tf_op jit(solution)/shard_map/ppermute | solution.py:365
  110.3 17.3 %collective-permute-start.14 = (bf16[4,128,128]{2,1,0:T(8,128)(2,1)}, bf16[4,128,128]{2,1,0:T(8,128)(2,1)S(1)}, u32[]{:S(2)}, u32[]{:S(2)}) collective-permute-start(bf16[4,128,128]{2,1,0:T(8,128)(2,1)} %get-tuple-element.40), channel_id=1, source_target_pairs={{0,8},{1,9},{2,10},{3,11},{4,12},{5,13},{6,14},{7,15},{8,0},{9,1},... | collective-permute-start | bytes 393224 | tf_op jit(solution)/shard_map/ppermute | solution.py:365
  111.1 17.5 %collective-permute-start.15 = (bf16[4,128,128]{2,1,0:T(8,128)(2,1)}, bf16[4,128,128]{2,1,0:T(8,128)(2,1)S(1)}, u32[]{:S(2)}, u32[]{:S(2)}) collective-permute-start(bf16[4,128,128]{2,1,0:T(8,128)(2,1)} %get-tuple-element.41), channel_id=1, source_target_pairs={{0,12},{1,13},{2,14},{3,15},{4,0},{5,1},{6,2},{7,3},{8,4},{9,5},{1... | collective-permute-start | bytes 393224 | tf_op jit(solution)/shard_map/ppermute | solution.py:365
  114.5 1.0 copy-start.20
  126.4 1.2 copy-start.10
  128.6 0.7 copy-start.21
  129.3 32.9 %all-to-all-start.2 = ((bf16[16,3,2,64,128]{4,3,2,1,0:T(8,128)(2,1)}), bf16[16,3,2,64,128]{4,3,2,1,0:T(8,128)(2,1)S(1)}, u32[]{:S(2)}, u32[]{:S(2)}) async-start(bf16[16,3,2,64,128]{4,3,2,1,0:T(8,128)(2,1)} %copy-done.10), calls=%async_computation.2 | async-start | bytes 3145728 | tf_op jit(solution)/shard_map/all_to_all | solution.py:310
  134.6 0.9 copy-start.22
  140.0 1.1 copy-start
  162.2 57.9 %all-to-all-start.3 = ((bf16[16,3,2,64,128]{4,3,2,1,0:T(8,128)(2,1)}), bf16[16,3,2,64,128]{4,3,2,1,0:T(8,128)(2,1)S(1)}, u32[]{:S(2)}, u32[]{:S(2)}) async-start(bf16[16,3,2,64,128]{4,3,2,1,0:T(8,128)(2,1)} %copy-done), calls=%async_computation.3 | async-start | bytes 3145728 | tf_op jit(solution)/shard_map/all_to_all | solution.py:310

commit v3 on v2

--- a/solution.py
+++ b/solution.py
@@ -57,16 +57,10 @@
 
 
 def pack_kernel(a_ref, b_ref, c_ref, *refs):
-    out_ref, sems = refs[-2:]
-    copies = [
-        pltpu.make_async_copy(ref.at[:, h * 128 : (h + 1) * 128], out_ref.at[h, t], sems.at[t, h])
-        for h in range(16)
-        for t, ref in enumerate((a_ref, b_ref, c_ref))
-    ]
-    for copy in copies:
-        copy.start()
-    for copy in copies:
-        copy.wait()
+    out_ref = refs[-1]
+    for t, ref in enumerate((a_ref, b_ref, c_ref)):
+        for h in range(16):
+            out_ref[h, t] = ref[:, h * 128 : (h + 1) * 128]
 
 
 def pack(a, b, c, *after):
@@ -76,9 +70,7 @@
         jax.ShapeDtypeStruct((16, 3, 128, 128), BF16),
         0,
         3 << 20,
-        in_specs=[IN_HBM] * 3 + [WHOLE] * len(after),
-        out_specs=WHOLE,
-        scratch_shapes=[pltpu.SemaphoreType.DMA((3, 16))],
+        in_specs=[WHOLE] * (3 + len(after)),
     )(*flat, *after)
     return out.reshape(16, 3, 2, 64, 128)
 
@@ -229,28 +221,15 @@
     return dq_t, dk, dv
 
 
-def space_kernel(pos_ref, qkv_ref, keep_ref, got_ref, after_ref, out_ref, o_ref, dk_ref, dv_ref):
+def space_kernel(pos_ref, qkv_ref, keep_ref, got_ref, after_ref, out_ref, o_ref):
     z_hi = pos_ref[0]
     o_ref[pl.ds(pl.multiple_of(z_hi * 512, 512), 512), :] = keep_ref[...].reshape(512, 128)
     o_ref[pl.ds(pl.multiple_of((1 - z_hi) * 512, 512), 512), :] = got_ref[...].reshape(512, 128)
-    k = qkv_ref[:, 1].reshape(1024, 128)
-    v = qkv_ref[:, 2].reshape(1024, 128)
-    k_t = k.T
-    chunk = 256
-    for j in range(1024 // chunk):
-        n = chunk // 64
-        q = qkv_ref[j * n : (j + 1) * n, 0].reshape(chunk, 128)
-        o = o_ref[j * chunk : (j + 1) * chunk, :]
-        dq_t, dk, dv = attend(q, k, v, o, k_t, None)
-        out_ref[j * n : (j + 1) * n, 0] = (dq_t * SCALE).T.astype(BF16).reshape(n, 1, 64, 128)
-        if j:
-            dk_ref[...] += dk
-            dv_ref[...] += dv
-        else:
-            dk_ref[...] = dk
-            dv_ref[...] = dv
-    out_ref[:, 1] = (dk_ref[...] * SCALE).astype(BF16).reshape(16, 1, 64, 128)
-    out_ref[:, 2] = dv_ref[...].astype(BF16).reshape(16, 1, 64, 128)
+    q, k, v = (qkv_ref[:, t].reshape(1024, 128) for t in range(3))
+    dq_t, dk, dv = attend(q, k, v, o_ref[...], k.T, None)
+    out_ref[:, 0] = (dq_t * SCALE).T.astype(BF16).reshape(16, 1, 64, 128)
+    out_ref[:, 1] = (dk * SCALE).astype(BF16).reshape(16, 1, 64, 128)
+    out_ref[:, 2] = dv.astype(BF16).reshape(16, 1, 64, 128)
 
 
 def space_attention(z_hi, qkv, keep, got, after):
@@ -264,11 +243,7 @@
         grid=(2,),
         in_specs=[SCALARS, whole, half, half, LATER],
         out_specs=whole,
-        scratch_shapes=[
-            pltpu.VMEM((1024, 128), BF16),
-            pltpu.VMEM((1024, 128), F32),
-            pltpu.VMEM((1024, 128), F32),
-        ],
+        scratch_shapes=[pltpu.VMEM((1024, 128), BF16)],
     )(z_hi, qkv, keep, got, after)
 
 

time: 223 us -> 221 us (level)
  Pallas kernels: 39 us -> 35.3 us
  waiting for transfers between devices: 94.2 us -> 96.5 us
    pallas_call x1, Pallas kernels: 10.9 us -> 8.58 us  [space_attention(): call(space_kernel, jax.ShapeDtypeStruct((16, 3, 2, 64, 128), BF16), 5 * (...]
    ppermute x3, waiting for transfers between devices: 1.08 us -> 3.44 us  [on_device(): lax.ppermute(outs[k], 'tm', [(t, (t // 4 + k) % 4 * 4 + t % 4) for t in r...]
  transfers between devices with their start and end apart: 20 -> 20, of which waited for: 10 -> 11; matrix products, arithmetic and copies ran while one was open for 1% -> 1% of each run, Pallas kernels for 16% -> 15%
where the time goes in v3:
time: 221 us; the launch traced here: 220 us
  waiting for transfers between devices  96.5 us (44%)
  starting transfers between devices  70.8 us (32%)
  Pallas kernels  35.3 us (16%)
  local copies, waits for them, and re-layouts  15.2 us (7%)
    all_to_all x4, waiting for transfers between devices, exchange(): return lax.all_to_all(array, axis, split_axis=0, concat_axis=0, tiled=True)  56.5 us
    all_to_all x4, starting transfers between devices, exchange(): return lax.all_to_all(array, axis, split_axis=0, concat_axis=0, tiled=True)  44 us
    ppermute x13, waiting for transfers between devices, send(): return lax.ppermute(array, ('space', 'tm'), permutation(move))  36.6 us
    ppermute x13, starting transfers between devices, send(): return lax.ppermute(array, ('space', 'tm'), permutation(move))  22.8 us
    unnamed x48, local copies, waits for them, and re-layouts  15.2 us
    pallas_call x1, Pallas kernels, space_attention(): call(space_kernel, jax.ShapeDtypeStruct((16, 3, 2, 64, 128), BF16), 5 * (...  8.58 us
    pallas_call x1, Pallas kernels, space_proj(): call(space_proj_kernel, (shape, shape), 1 << 30, 6 << 20, in_specs=[SCALA...  5.84 us
    pallas_call x1, Pallas kernels, time_proj(): call(time_proj_kernel, (shape,) * 4, 1 << 30, 5 << 20, in_specs=[SCALARS]...  4.92 us
  transfers between devices with their start and end apart: 20, of which 11 were waited for; matrix products, arithmetic and copies ran while one was open for 1% of the time, Pallas kernels for 15%

profile of v3, /device:TPU:38, one launch (start us, length us, event | category | flops | bytes accessed | tf_op | source)
XLA Modules:
  0.0 220.0 jit_solution(7302996287593708385)
XLA Ops:
  0.6 1.0 copy-done.16
  1.7 1.0 copy-done.17
  2.7 1.0 copy-done.18
  3.8 1.5 shard_map.149
  5.2 8.8 %all-to-all-start = ((bf16[16,3,2,64,128]{4,3,2,1,0:T(8,128)(2,1)}), bf16[16,3,2,64,128]{4,3,2,1,0:T(8,128)(2,1)S(1)}, u32[]{:S(2)}, u32[]{:S(2)}) async-start(bf16[16,3,2,64,128]{4,3,2,1,0:T(8,128)(2,1)} %bitcast.13), calls=%async_computation | async-start | bytes 3145728 | tf_op jit(solution)/shard_map/all_to_all | solution.py:285
  14.0 0.9 collective-permute-start
  14.9 1.1 collective-permute-start.1
  16.0 2.8 %collective-permute-start.2 = (bf16[128,2048]{1,0:T(8,128)(2,1)}, bf16[128,2048]{1,0:T(8,128)(2,1)}, u32[]{:S(2)}, u32[]{:S(2)}) collective-permute-start(bf16[128,2048]{1,0:T(8,128)(2,1)} %bitcast.4.a_ref), channel_id=1, source_target_pairs={{0,96},{1,97},{2,98},{3,99},{4,100},{5,101},{6,102},{7,103},{8,104... | collective-permute-start | bytes 1572872 | tf_op jit(solution)/shard_map/ppermute | solution.py:34
  18.8 1.2 add_convert_fusion
  20.0 1.6 collective-permute-start.5
  21.6 0.1 pad_add_fusion.at_ref
  21.6 1.0 copy-done.4
  22.7 0.8 shard_map.146
  23.5 4.6 %collective-permute-start.3 = (bf16[96,2048]{1,0:T(8,128)(2,1)S(1)}, bf16[96,2048]{1,0:T(8,128)(2,1)S(1)}, u32[]{:S(2)}, u32[]{:S(2)}) collective-permute-start(bf16[96,2048]{1,0:T(8,128)(2,1)S(1)} %get-tuple-element.31), channel_id=1, source_target_pairs={{0,136},{1,137},{2,138},{3,139},{4,140},{5,141},{6,142},{7,143},{8... | collective-permute-start | bytes 1179656 | tf_op jit(solution)/shard_map/ppermute | solution.py:34
  28.1 1.2 collective-permute-done.b_ref
  29.3 1.5 collective-permute-start.4
  30.8 8.0 %collective-permute-done.1.c_ref = bf16[128,2048]{1,0:T(8,128)(2,1)} collective-permute-done((bf16[128,2048]{1,0:T(8,128)(2,1)}, bf16[128,2048]{1,0:T(8,128)(2,1)}, u32[]{:S(2)}, u32[]{:S(2)}) %collective-permute-start.1) | collective-permute-done | bytes 524320 | tf_op jit(solution)/shard_map/ppermute | solution.py:34
  38.8 2.6 %collective-permute-done.2.d_ref = bf16[128,2048]{1,0:T(8,128)(2,1)} collective-permute-done((bf16[128,2048]{1,0:T(8,128)(2,1)}, bf16[128,2048]{1,0:T(8,128)(2,1)}, u32[]{:S(2)}, u32[]{:S(2)}) %collective-permute-start.2) | collective-permute-done | bytes 524320 | tf_op jit(solution)/shard_map/ppermute | solution.py:34
  41.4 3.0 %shard_map.145.refs_0_ = bf16[4,128,2048]{2,1,0:T(8,128)(2,1)} custom-call(bf16[128,2048]{1,0:T(8,128)(2,1)} %bitcast.4.a_ref, bf16[128,2048]{1,0:T(8,128)(2,1)} %collective-permute-done.b_ref, bf16[128,2048]{1,0:T(8,128)(2,1)} %collective-permute-done.1.c_ref, bf16[128,2048]{1,0:T(8,128)(2,1)} %collective-permute-done.2.d_ref), custom_call_target="tpu_custom_call" | custom-call | bytes 4194304 | tf_op jit(solution)/shard_map/pallas_call | solution.py:151
  44.3 0.0 collective-permute-start.6
  44.3 7.0 %collective-permute-done.4.rows_ref = bf16[64,2048]{1,0:T(8,128)(2,1)S(1)} collective-permute-done((bf16[64,2048]{1,0:T(8,128)(2,1)S(1)}, bf16[64,2048]{1,0:T(8,128)(2,1)S(1)}, u32[]{:S(2)}, u32[]{:S(2)}) %collective-permute-start.4) | collective-permute-done | bytes 262176 | tf_op jit(solution)/shard_map/ppermute | solution.py:34
  51.4 0.0 copy-start.8
  51.4 3.1 %shard_map.148 = bf16[16,3,128,128]{3,2,1,0:T(8,128)(2,1)} custom-call(bf16[128,2048]{1,0:T(8,128)(2,1)S(1)} %bitcast.49, bf16[128,2048]{1,0:T(8,128)(2,1)S(1)} %bitcast.50, bf16[128,2048]{1,0:T(8,128)(2,1)S(1)} %bitcast.51, bf16[4,128,2048]{2,1,0:T(8,128)(2,1)} %shard_map.145.refs_0_, bf16[64,2048]{1,0:T(8,128)(2,1)S(1)} %get-tuple-element.33.refs_1_.refs_3_, ...), custom_call_target="tpu_custom_call" | custom-call | bytes 3145728 | tf_op jit(solution)/shard_map/pallas_call | solution.py:68
  54.5 0.7 copy-done.11
  55.2 0.0 all-to-all-done.qkv_ref
  55.2 9.2 %all-to-all-start.1 = ((bf16[16,3,2,64,128]{4,3,2,1,0:T(8,128)(2,1)}), bf16[16,3,2,64,128]{4,3,2,1,0:T(8,128)(2,1)}, u32[]{:S(2)}, u32[]{:S(2)}) async-start(bf16[16,3,2,64,128]{4,3,2,1,0:T(8,128)(2,1)} %bitcast.9), calls=%async_computation.1 | async-start | bytes 3145728 | tf_op jit(solution)/shard_map/all_to_all | solution.py:285
  64.5 3.0 %collective-permute-start.8 = (bf16[128,2048]{1,0:T(8,128)(2,1)S(1)}, bf16[128,2048]{1,0:T(8,128)(2,1)S(1)}, u32[]{:S(2)}, u32[]{:S(2)}) collective-permute-start(bf16[128,2048]{1,0:T(8,128)(2,1)S(1)} %bitcast.46), channel_id=1, source_target_pairs={{0,2},{1,3},{2,0},{3,1},{4,6},{5,7},{6,4},{7,5},{8,10},{9,11},{10,... | collective-permute-start | bytes 1572872 | tf_op jit(solution)/shard_map/ppermute | solution.py:34
  67.5 1.2 collective-permute-start.10
  68.6 0.9 collective-permute-start.11
  69.5 0.0 collective-permute-start.7
  69.5 0.1 pad_add_fusion.1.at_ref
  69.6 11.2 %collective-permute-done.8.refs_5_.refs_2_ = bf16[128,2048]{1,0:T(8,128)(2,1)S(1)} collective-permute-done((bf16[128,2048]{1,0:T(8,128)(2,1)S(1)}, bf16[128,2048]{1,0:T(8,128)(2,1)S(1)}, u32[]{:S(2)}, u32[]{:S(2)}) %collective-permute-start.8) | collective-permute-done | bytes 524320 | tf_op jit(solution)/shard_map/ppermute | solution.py:34
  80.8 4.8 %collective-permute-done.7.refs_4_ = bf16[64,2048]{1,0:T(8,128)(2,1)S(1)} collective-permute-done((bf16[64,2048]{1,0:T(8,128)(2,1)}, bf16[64,2048]{1,0:T(8,128)(2,1)S(1)}, u32[]{:S(2)}, u32[]{:S(2)}) %collective-permute-start.7) | collective-permute-done | bytes 262176 | tf_op jit(solution)/shard_map/ppermute | solution.py:34
  85.6 0.0 collective-permute-done.6.refs_1_
  85.6 0.9 copy-done.12
  86.6 5.8 %shard_map.150 = (bf16[8,128,128]{2,1,0:T(8,128)(2,1)S(1)}, bf16[8,128,128]{2,1,0:T(8,128)(2,1)}) custom-call(s32[2]{0:T(128)S(1)} %pad_add_fusion.1.at_ref, bf16[4,128,2048]{2,1,0:T(8,128)(2,1)} %shard_map.145.refs_0_, bf16[4,128,2048]{2,1,0:T(8,128)(2,1)} %collective-permute-done.6.refs_1_, bf16[128,2048]{1,0:T(8,128)(2,1)S(1)} %copy-done.3, ...), custom_call_target="tpu_custom_call" | custom-call | flops 1073741824 | bytes 6291456 | tf_op jit(solution)/shard_map/pallas_call | solution.py:171
  92.5 0.1 shard_map.151.refs_5_
  92.5 0.6 copy-done.19
  93.1 0.8 copy-done.6
  93.9 5.4 %collective-permute-start.9 = (bf16[8,128,128]{2,1,0:T(8,128)(2,1)}, bf16[8,128,128]{2,1,0:T(8,128)(2,1)}, u32[]{:S(2)}, u32[]{:S(2)}) collective-permute-start(bf16[8,128,128]{2,1,0:T(8,128)(2,1)} %get-tuple-element.37), channel_id=1, source_target_pairs={{0,128},{1,129},{2,130},{3,131},{4,132},{5,133},{6,134},{7,135},{8... | collective-permute-start | bytes 786440 | tf_op jit(solution)/shard_map/ppermute | solution.py:34
  99.3 0.1 pad_add_fusion.2.at_ref
  99.4 1.0 copy-done.2
  100.4 1.0 copy-done.5
  101.5 1.0 copy-done.7
  102.5 4.9 %shard_map.152 = (bf16[4,128,128]{2,1,0:T(8,128)(2,1)S(1)}, bf16[4,128,128]{2,1,0:T(8,128)(2,1)}, bf16[4,128,128]{2,1,0:T(8,128)(2,1)}, bf16[4,128,128]{2,1,0:T(8,128)(2,1)}) custom-call(s32[2]{0:T(128)S(1)} %pad_add_fusion.2.at_ref, bf16[128,2048]{1,0:T(8,128)(2,1)S(1)} %bitcast.48, bf16[128,2048]{1,0:T(8,128)(2,1)S(1)} %collective-permute-done.5.refs_3_.refs_1_, ...), custom_call_target="tpu_custom_call" | custom-call | flops 1073741824 | bytes 5242880 | tf_op jit(solution)/shard_map/pallas_call | solution.py:199
  107.4 1.5 collective-permute-start.13
  108.9 0.8 collective-permute-start.14
  109.7 1.6 collective-permute-start.15
  111.4 1.7 collective-permute-done.9
  113.1 0.9 copy-done.20
  114.1 8.6 %shard_map.153 = bf16[16,3,2,64,128]{4,3,2,1,0:T(8,128)(2,1)S(1)} custom-call(s32[1]{0:T(128)} %bitcast.pos_ref, bf16[16,3,2,64,128]{4,3,2,1,0:T(8,128)(2,1)} %all-to-all-done.1.qkv_ref, bf16[8,2,64,128]{3,2,1,0:T(8,128)(2,1)S(1)} %bitcast.55, bf16[8,2,64,128]{3,2,1,0:T(8,128)(2,1)} %bitcast.16.got_ref, bf16[4,128,128]{2,1,0:T(8,128)(2,1)S(1)} %get-tuple-element.44.after_ref), custom_call_target="tpu_custom_call" | custom-call | flops 2684354560 | bytes 4194304 | tf_op jit(solution)/shard_map/pallas_call | solution.py:238
  122.7 1.2 copy-done.10
  123.8 2.4 %collective-permute-done.14 = bf16[4,128,128]{2,1,0:T(8,128)(2,1)S(1)} collective-permute-done((bf16[4,128,128]{2,1,0:T(8,128)(2,1)}, bf16[4,128,128]{2,1,0:T(8,128)(2,1)S(1)}, u32[]{:S(2)}, u32[]{:S(2)}) %collective-permute-start.14) | collective-permute-done | bytes 131104 | tf_op jit(solution)/shard_map/ppermute | solution.py:340
  126.2 1.1 collective-permute-done.15
  127.3 0.7 copy-done.21
  127.9 5.3 %all-to-all-start.2 = ((bf16[16,3,2,64,128]{4,3,2,1,0:T(8,128)(2,1)}), bf16[16,3,2,64,128]{4,3,2,1,0:T(8,128)(2,1)S(1)}, u32[]{:S(2)}, u32[]{:S(2)}) async-start(bf16[16,3,2,64,128]{4,3,2,1,0:T(8,128)(2,1)} %copy-done.10), calls=%async_computation.2 | async-start | bytes 3145728 | tf_op jit(solution)/shard_map/all_to_all | solution.py:285
  133.2 0.9 copy-done.22
  134.1 4.4 %shard_map.154 = bf16[16,3,2,64,128]{4,3,2,1,0:T(8,128)(2,1)S(1)} custom-call(s32[1]{0:T(128)} %bitcast.18.pos_ref, bf16[16,3,2,64,128]{4,3,2,1,0:T(8,128)(2,1)S(1)} %all-to-all-done.qkv_ref, bf16[4,2,64,128]{3,2,1,0:T(8,128)(2,1)S(1)} %bitcast.56, bf16[4,2,64,128]{3,2,1,0:T(8,128)(2,1)S(1)} %bitcast.57, bf16[4,2,64,128]{3,2,1,0:T(8,128)(2,1)S(1)} %bitcast.58, ...), custom_call_target="tpu_custom_call" | custom-call | flops 671088640 | bytes 4194304 | tf_op jit(solution)/shard_map/pallas_call | solution.py:272
  138.6 1.1 copy-done
  139.7 21.0 %all-to-all-done.2 = bf16[16,3,2,64,128]{4,3,2,1,0:T(8,128)(2,1)S(1)} async-done(((bf16[16,3,2,64,128]{4,3,2,1,0:T(8,128)(2,1)}), bf16[16,3,2,64,128]{4,3,2,1,0:T(8,128)(2,1)S(1)}, u32[]{:S(2)}, u32[]{:S(2)}) %all-to-all-start.2) | async-done | bytes 1572896 | tf_op jit(solution)/shard_map/all_to_all | solution.py:285
  160.7 20.7 %all-to-all-start.3 = ((bf16[16,3,2,64,128]{4,3,2,1,0:T(8,128)(2,1)}), bf16[16,3,2,64,128]{4,3,2,1,0:T(8,128)(2,1)S(1)}, u32[]{:S(2)}, u32[]{:S(2)}) async-start(bf16[16,3,2,64,128]{4,3,2,1,0:T(8,128)(2,1)} %copy-done), calls=%async_computation.3 | async-start | bytes 3145728 | tf_op jit(solution)/shard_map/all_to_all | solution.py:285
  181.4 1.5 shard_map.155
  183.0 35.5 %all-to-all-done.3 = bf16[16,3,2,64,128]{4,3,2,1,0:T(8,128)(2,1)S(1)} async-done(((bf16[16,3,2,64,128]{4,3,2,1,0:T(8,128)(2,1)}), bf16[16,3,2,64,128]{4,3,2,1,0:T(8,128)(2,1)S(1)}, u32[]{:S(2)}, u32[]{:S(2)}) %all-to-all-start.3) | async-done | bytes 1572896 | tf_op jit(solution)/shard_map/all_to_all | solution.py:285
  218.4 1.5 shard_map.156
  (40 shorter events, 0.1 us)
Async XLA Ops:
  0.6 1.0 copy-start.16
  1.7 1.0 copy-start.17
  2.7 1.0 copy-start.18
  5.2 13.6 %copy-start.23 = (bf16[2,1,64,2048]{3,2,1,0:T(8,128)(2,1)S(1)}, bf16[2,1,64,2048]{3,2,1,0:T(8,128)(2,1)}, u32[]{:S(2)}) copy-start(bf16[2,1,64,2048]{3,2,1,0:T(8,128)(2,1)} %param.17) | copy-start | bytes 1572868
  5.2 50.0 %all-to-all-start = ((bf16[16,3,2,64,128]{4,3,2,1,0:T(8,128)(2,1)}), bf16[16,3,2,64,128]{4,3,2,1,0:T(8,128)(2,1)S(1)}, u32[]{:S(2)}, u32[]{:S(2)}) async-start(bf16[16,3,2,64,128]{4,3,2,1,0:T(8,128)(2,1)} %bitcast.13), calls=%async_computation | async-start | bytes 3145728 | tf_op jit(solution)/shard_map/all_to_all | solution.py:285
  14.0 7.6 %copy-start.3 = (bf16[128,2048]{1,0:T(8,128)(2,1)S(1)}, bf16[128,2048]{1,0:T(8,128)(2,1)}, u32[]{:S(2)}) copy-start(bf16[128,2048]{1,0:T(8,128)(2,1)} %refs_2_.1) | copy-start | bytes 1572868
  14.0 15.3 %collective-permute-start = (bf16[128,2048]{1,0:T(8,128)(2,1)}, bf16[128,2048]{1,0:T(8,128)(2,1)}, u32[]{:S(2)}, u32[]{:S(2)}) collective-permute-start(bf16[128,2048]{1,0:T(8,128)(2,1)} %bitcast.4.a_ref), channel_id=1, source_target_pairs={{0,32},{1,33},{2,34},{3,35},{4,36},{5,37},{6,38},{7,39},{8,40},{9,... | collective-permute-start | bytes 1572872 | tf_op jit(solution)/shard_map/ppermute | solution.py:34
  14.9 23.8 %collective-permute-start.1 = (bf16[128,2048]{1,0:T(8,128)(2,1)}, bf16[128,2048]{1,0:T(8,128)(2,1)}, u32[]{:S(2)}, u32[]{:S(2)}) collective-permute-start(bf16[128,2048]{1,0:T(8,128)(2,1)} %bitcast.4.a_ref), channel_id=1, source_target_pairs={{0,64},{1,65},{2,66},{3,67},{4,68},{5,69},{6,70},{7,71},{8,72},{9,... | collective-permute-start | bytes 1572872 | tf_op jit(solution)/shard_map/ppermute | solution.py:34
  16.0 25.3 %collective-permute-start.2 = (bf16[128,2048]{1,0:T(8,128)(2,1)}, bf16[128,2048]{1,0:T(8,128)(2,1)}, u32[]{:S(2)}, u32[]{:S(2)}) collective-permute-start(bf16[128,2048]{1,0:T(8,128)(2,1)} %bitcast.4.a_ref), channel_id=1, source_target_pairs={{0,96},{1,97},{2,98},{3,99},{4,100},{5,101},{6,102},{7,103},{8,104... | collective-permute-start | bytes 1572872 | tf_op jit(solution)/shard_map/ppermute | solution.py:34
  20.0 31.4 %collective-permute-start.5 = (bf16[128,2048]{1,0:T(8,128)(2,1)S(1)}, bf16[128,2048]{1,0:T(8,128)(2,1)S(1)}, u32[]{:S(2)}, u32[]{:S(2)}) collective-permute-start(bf16[128,2048]{1,0:T(8,128)(2,1)S(1)} %bitcast.45), channel_id=1, source_target_pairs={{0,1},{1,0},{2,3},{3,2},{4,5},{5,4},{6,7},{7,6},{8,9},{9,8},{10,11... | collective-permute-start | bytes 1572872 | tf_op jit(solution)/shard_map/ppermute | solution.py:34
  21.6 1.0 copy-start.4
  23.5 27.8 %collective-permute-start.3 = (bf16[96,2048]{1,0:T(8,128)(2,1)S(1)}, bf16[96,2048]{1,0:T(8,128)(2,1)S(1)}, u32[]{:S(2)}, u32[]{:S(2)}) collective-permute-start(bf16[96,2048]{1,0:T(8,128)(2,1)S(1)} %get-tuple-element.31), channel_id=1, source_target_pairs={{0,136},{1,137},{2,138},{3,139},{4,140},{5,141},{6,142},{7,143},{8... | collective-permute-start | bytes 1179656 | tf_op jit(solution)/shard_map/ppermute | solution.py:34
  29.3 22.1 %copy-start.13 = (bf16[2,1,64,2048]{3,2,1,0:T(8,128)(2,1)S(1)}, bf16[2,1,64,2048]{3,2,1,0:T(8,128)(2,1)}, u32[]{:S(2)}) copy-start(bf16[2,1,64,2048]{3,2,1,0:T(8,128)(2,1)} %param.10) | copy-start | bytes 1572868
  29.3 22.1 %copy-start.14 = (bf16[2,1,64,2048]{3,2,1,0:T(8,128)(2,1)S(1)}, bf16[2,1,64,2048]{3,2,1,0:T(8,128)(2,1)}, u32[]{:S(2)}) copy-start(bf16[2,1,64,2048]{3,2,1,0:T(8,128)(2,1)} %param.11) | copy-start | bytes 1572868
  29.3 22.1 %copy-start.15 = (bf16[2,1,64,2048]{3,2,1,0:T(8,128)(2,1)S(1)}, bf16[2,1,64,2048]{3,2,1,0:T(8,128)(2,1)}, u32[]{:S(2)}) copy-start(bf16[2,1,64,2048]{3,2,1,0:T(8,128)(2,1)} %param.12) | copy-start | bytes 1572868
  29.3 22.0 %collective-permute-start.4 = (bf16[64,2048]{1,0:T(8,128)(2,1)S(1)}, bf16[64,2048]{1,0:T(8,128)(2,1)S(1)}, u32[]{:S(2)}, u32[]{:S(2)}) collective-permute-start(bf16[64,2048]{1,0:T(8,128)(2,1)S(1)} %get-tuple-element.32), channel_id=1, source_target_pairs={{0,4},{1,5},{2,6},{3,7},{4,8},{5,9},{6,10},{7,11},{8,12},{9,13},{1... | collective-permute-start | bytes 786440 | tf_op jit(solution)/shard_map/ppermute | solution.py:34
  44.3 41.3 %collective-permute-start.6 = (bf16[4,128,2048]{2,1,0:T(8,128)(2,1)}, bf16[4,128,2048]{2,1,0:T(8,128)(2,1)}, u32[]{:S(2)}, u32[]{:S(2)}) collective-permute-start(bf16[4,128,2048]{2,1,0:T(8,128)(2,1)} %shard_map.145.refs_0_), channel_id=1, source_target_pairs={{0,16},{1,17},{2,18},{3,19},{4,20},{5,21},{6,22},{7,23},{8,24},{9,... | collective-permute-start | bytes 6291464 | tf_op jit(solution)/shard_map/ppermute | solution.py:34
  51.4 17.3 %copy-start.8 = (bf16[96,2048]{1,0:T(8,128)(2,1)}, bf16[96,2048]{1,0:T(8,128)(2,1)S(1)}, u32[]{:S(2)}) copy-start(bf16[96,2048]{1,0:T(8,128)(2,1)S(1)} %get-tuple-element.34.refs_2_.a_ref) | copy-start | bytes 1179652
  54.5 0.7 copy-start.11
  55.2 57.9 %all-to-all-start.1 = ((bf16[16,3,2,64,128]{4,3,2,1,0:T(8,128)(2,1)}), bf16[16,3,2,64,128]{4,3,2,1,0:T(8,128)(2,1)}, u32[]{:S(2)}, u32[]{:S(2)}) async-start(bf16[16,3,2,64,128]{4,3,2,1,0:T(8,128)(2,1)} %bitcast.9), calls=%async_computation.1 | async-start | bytes 3145728 | tf_op jit(solution)/shard_map/all_to_all | solution.py:285
  64.5 16.3 %collective-permute-start.8 = (bf16[128,2048]{1,0:T(8,128)(2,1)S(1)}, bf16[128,2048]{1,0:T(8,128)(2,1)S(1)}, u32[]{:S(2)}, u32[]{:S(2)}) collective-permute-start(bf16[128,2048]{1,0:T(8,128)(2,1)S(1)} %bitcast.46), channel_id=1, source_target_pairs={{0,2},{1,3},{2,0},{3,1},{4,6},{5,7},{6,4},{7,5},{8,10},{9,11},{10,... | collective-permute-start | bytes 1572872 | tf_op jit(solution)/shard_map/ppermute | solution.py:34
  67.5 25.0 %collective-permute-start.10 = (bf16[128,2048]{1,0:T(8,128)(2,1)S(1)}, bf16[128,2048]{1,0:T(8,128)(2,1)S(1)}, u32[]{:S(2)}, u32[]{:S(2)}) collective-permute-start(bf16[128,2048]{1,0:T(8,128)(2,1)S(1)} %bitcast.47), channel_id=1, source_target_pairs={{0,3},{1,2},{2,1},{3,0},{4,7},{5,6},{6,5},{7,4},{8,11},{9,10},{10,... | collective-permute-start | bytes 1572872 | tf_op jit(solution)/shard_map/ppermute | solution.py:34
  68.6 23.8 %collective-permute-start.11 = (bf16[96,2048]{1,0:T(8,128)(2,1)S(1)}, bf16[96,2048]{1,0:T(8,128)(2,1)S(1)}, u32[]{:S(2)}, u32[]{:S(2)}) collective-permute-start(bf16[96,2048]{1,0:T(8,128)(2,1)S(1)} %get-tuple-element.34.refs_2_.a_ref), channel_id=1, source_target_pairs={{0,32},{1,33},{2,34},{3,35},{4,36},{5,37},{6,38},{7,39},{8,40},{9,... | collective-permute-start | bytes 1179656 | tf_op jit(solution)/shard_map/ppermute | solution.py:34
  69.5 16.2 %collective-permute-start.7 = (bf16[64,2048]{1,0:T(8,128)(2,1)}, bf16[64,2048]{1,0:T(8,128)(2,1)S(1)}, u32[]{:S(2)}, u32[]{:S(2)}) collective-permute-start(bf16[64,2048]{1,0:T(8,128)(2,1)} %copy-done.11), channel_id=1, source_target_pairs={{0,1},{1,0},{2,3},{3,2},{4,5},{5,4},{6,7},{7,6},{8,9},{9,8},{10,11... | collective-permute-start | bytes 786440 | tf_op jit(solution)/shard_map/ppermute | solution.py:34
  69.6 22.9 %copy-start.9 = (bf16[96,2048]{1,0:T(8,128)(2,1)S(1)}, bf16[96,2048]{1,0:T(8,128)(2,1)}, u32[]{:S(2)}) copy-start(bf16[96,2048]{1,0:T(8,128)(2,1)} %copy-done.8) | copy-start | bytes 1179652
  80.8 11.6 %copy-start.1 = (bf16[128,2048]{1,0:T(8,128)(2,1)}, bf16[128,2048]{1,0:T(8,128)(2,1)S(1)}, u32[]{:S(2)}) copy-start(bf16[128,2048]{1,0:T(8,128)(2,1)S(1)} %collective-permute-done.8.refs_5_.refs_2_) | copy-start | bytes 1572868
  85.6 1.0 copy-start.12
  92.4 0.7 copy-start.19
  93.1 0.8 copy-start.6
  93.9 5.5 %collective-permute-start.12 = (bf16[2,96,2048]{2,1,0:T(8,128)(2,1)S(1)}, bf16[2,96,2048]{2,1,0:T(8,128)(2,1)}, u32[]{:S(2)}, u32[]{:S(2)}) collective-permute-start(bf16[2,96,2048]{2,1,0:T(8,128)(2,1)S(1)} %shard_map.151.refs_5_), channel_id=1, source_target_pairs={{0,16},{1,17},{2,18},{3,19},{4,20},{5,21},{6,22},{7,23},{8,24},{9,... | collective-permute-start | bytes 2359304 | tf_op jit(solution)/shard_map/ppermute | solution.py:34
  93.9 19.2 %collective-permute-start.9 = (bf16[8,128,128]{2,1,0:T(8,128)(2,1)}, bf16[8,128,128]{2,1,0:T(8,128)(2,1)}, u32[]{:S(2)}, u32[]{:S(2)}) collective-permute-start(bf16[8,128,128]{2,1,0:T(8,128)(2,1)} %get-tuple-element.37), channel_id=1, source_target_pairs={{0,128},{1,129},{2,130},{3,131},{4,132},{5,133},{6,134},{7,135},{8... | collective-permute-start | bytes 786440 | tf_op jit(solution)/shard_map/ppermute | solution.py:34
  99.4 1.0 copy-start.2
  100.4 1.0 copy-start.5
  101.5 1.0 copy-start.7
  107.4 16.4 %collective-permute-start.13 = (bf16[4,128,128]{2,1,0:T(8,128)(2,1)}, bf16[4,128,128]{2,1,0:T(8,128)(2,1)S(1)}, u32[]{:S(2)}, u32[]{:S(2)}) collective-permute-start(bf16[4,128,128]{2,1,0:T(8,128)(2,1)} %get-tuple-element.39), channel_id=1, source_target_pairs={{0,4},{1,5},{2,6},{3,7},{4,8},{5,9},{6,10},{7,11},{8,12},{9,13},{1... | collective-permute-start | bytes 393224 | tf_op jit(solution)/shard_map/ppermute | solution.py:340
  108.9 17.3 %collective-permute-start.14 = (bf16[4,128,128]{2,1,0:T(8,128)(2,1)}, bf16[4,128,128]{2,1,0:T(8,128)(2,1)S(1)}, u32[]{:S(2)}, u32[]{:S(2)}) collective-permute-start(bf16[4,128,128]{2,1,0:T(8,128)(2,1)} %get-tuple-element.40), channel_id=1, source_target_pairs={{0,8},{1,9},{2,10},{3,11},{4,12},{5,13},{6,14},{7,15},{8,0},{9,1},... | collective-permute-start | bytes 393224 | tf_op jit(solution)/shard_map/ppermute | solution.py:340
  109.7 17.5 %collective-permute-start.15 = (bf16[4,128,128]{2,1,0:T(8,128)(2,1)}, bf16[4,128,128]{2,1,0:T(8,128)(2,1)S(1)}, u32[]{:S(2)}, u32[]{:S(2)}) collective-permute-start(bf16[4,128,128]{2,1,0:T(8,128)(2,1)} %get-tuple-element.41), channel_id=1, source_target_pairs={{0,12},{1,13},{2,14},{3,15},{4,0},{5,1},{6,2},{7,3},{8,4},{9,5},{1... | collective-permute-start | bytes 393224 | tf_op jit(solution)/shard_map/ppermute | solution.py:340
  113.1 1.0 copy-start.20
  122.7 1.2 copy-start.10
  127.3 0.7 copy-start.21
  127.9 32.8 %all-to-all-start.2 = ((bf16[16,3,2,64,128]{4,3,2,1,0:T(8,128)(2,1)}), bf16[16,3,2,64,128]{4,3,2,1,0:T(8,128)(2,1)S(1)}, u32[]{:S(2)}, u32[]{:S(2)}) async-start(bf16[16,3,2,64,128]{4,3,2,1,0:T(8,128)(2,1)} %copy-done.10), calls=%async_computation.2 | async-start | bytes 3145728 | tf_op jit(solution)/shard_map/all_to_all | solution.py:285
  133.2 0.9 copy-start.22
  138.6 1.1 copy-start
  160.7 57.7 %all-to-all-start.3 = ((bf16[16,3,2,64,128]{4,3,2,1,0:T(8,128)(2,1)}), bf16[16,3,2,64,128]{4,3,2,1,0:T(8,128)(2,1)S(1)}, u32[]{:S(2)}, u32[]{:S(2)}) async-start(bf16[16,3,2,64,128]{4,3,2,1,0:T(8,128)(2,1)} %copy-done), calls=%async_computation.3 | async-start | bytes 3145728 | tf_op jit(solution)/shard_map/all_to_all | solution.py:285

commit v4 on v3

--- a/solution.py
+++ b/solution.py
@@ -72,6 +72,20 @@
         3 << 20,
         in_specs=[WHOLE] * (3 + len(after)),
     )(*flat, *after)
+    return out.reshape(16, 3, 2, 64, 128)
+
+
+def pack_now(a, b, c):
+    flat = [v.reshape(128, 2048) for v in (a, b, c)]
+    out = pl.pallas_call(
+        pack_kernel,
+        out_shape=jax.ShapeDtypeStruct((16, 3, 128, 128), BF16),
+        grid=(4,),
+        in_specs=[pl.BlockSpec((32, 2048), lambda i: (i, 0))] * 3,
+        out_specs=pl.BlockSpec((16, 3, 32, 128), lambda i: (0, 0, i, 0)),
+        compiler_params=pltpu.CompilerParams(vmem_limit_bytes=62 * 1024 * 1024),
+        cost_estimate=pl.CostEstimate(flops=0, bytes_accessed=3 << 20, transcendentals=0),
+    )(*flat)
     return out.reshape(16, 3, 2, 64, 128)
 
 
@@ -128,6 +142,15 @@
         1 << 20,
         in_specs=[WHOLE] * 2,
     )(both, rows)
+
+
+def ready_kernel(a_ref, *refs):
+    refs[-1][...] = a_ref[:16, :128]
+
+
+def ready(*arrays):
+    shape = jax.ShapeDtypeStruct((16, 128), BF16)
+    return call(ready_kernel, shape, 0, 1 << 12, in_specs=[WHOLE] * len(arrays))(*arrays)
 
 
 def pair_kernel(a_ref, b_ref, *refs):
@@ -301,7 +324,7 @@
     z_hi, xc = place_s // 8, place_s % 8
     z_lo, y = place_t // 4, place_t % 4
 
-    time_in = exchange(pack(query_time, key_time, value_time), "tm")
+    time_in = exchange(pack_now(query_time, key_time, value_time), "tm")
     grad = block_grad.reshape(128, 2048)
     along_x = stacked(
         [grad] + [send(grad, lambda z, x, y, c, k=k: (z, x ^ k, y, c)) for k in (1, 2, 3)]
@@ -316,10 +339,9 @@
         send(cotangent, lambda z, x, y, c, k=k: (z, x, y ^ k, c)) for k in (1, 2, 3)
     ]
 
-    space_packed = pack(
-        query_space, key_space, value_space, along_x, w_half, along_z, along_y[1]
-    )
-    space_packed, time_in = lax.optimization_barrier((space_packed, time_in))
+    space_packed = pack(query_space, key_space, value_space)
+    first = ready(w_half, along_x, along_z, along_y[1])
+    space_packed, time_in, first = lax.optimization_barrier((space_packed, time_in, first))
     space_in = exchange(space_packed, "space")
     w_rest = send(w_half, lambda z, x, y, c: (z, x, y ^ 1, c))
     along_z2 = send(along_z, lambda z, x, y, c: (z, x ^ 1, y, c))
@@ -331,6 +353,7 @@
         w_half,
         w_rest,
         along_y[2],
+        first,
     )
     got = send(other, lambda z, x, y, c: (z + 4, x, y, c))
     pieces = pair(along_z, along_z2, keep, along_y[3])

time: 221 us -> 216 us (0.977)
  waiting for transfers between devices: 96.5 us -> 114 us
  starting transfers between devices: 70.8 us -> 55.3 us
  local copies, waits for them, and re-layouts: 15.2 us -> 10.4 us
    all_to_all x4, starting transfers between devices: 44 us -> 28.4 us  [exchange(): return lax.all_to_all(array, axis, split_axis=0, concat_axis=0, tiled=True)]
    all_to_all x4, waiting for transfers between devices: 56.5 us -> 70.6 us  [exchange(): return lax.all_to_all(array, axis, split_axis=0, concat_axis=0, tiled=True)]
    ppermute x13, waiting for transfers between devices: 36.6 us -> 43.5 us  [send(): return lax.ppermute(array, ('space', 'tm'), permutation(move))]
    unnamed x48 -> x44, local copies, waits for them, and re-layouts: 15.2 us -> 10.4 us
    pallas_call x2 -> x1, Pallas kernels: 4.58 us -> 0.27 us  [pack(): call(pack_kernel, jax.ShapeDtypeStruct((16, 3, 128, 128), BF16), 0, 3 <<...]
    pallas_call x0 -> x2, Pallas kernels: none -> 3.8 us  [the longest x1 3.8 us: pack_now(): pl.pallas_call(pack_kernel, out_shape=jax.ShapeDtypeStruct((16, 3, 128, 1...]
    ppermute x3, waiting for transfers between devices: 3.44 us -> 0.01 us  [on_device(): lax.ppermute(outs[k], 'tm', [(t, (t // 4 + k) % 4 * 4 + t % 4) for t in r...]
  transfers between devices with their start and end apart: 20 -> 20, of which waited for: 11 -> 9; matrix products, arithmetic and copies ran while one was open for 1% -> 0% of each run, Pallas kernels for 15% -> 14%
where the time goes in v4:
time: 216 us
  waiting for transfers between devices  114 us (53%)
  starting transfers between devices  55.3 us (26%)
  Pallas kernels  34.5 us (16%)
  local copies, waits for them, and re-layouts  10.4 us (5%)
    all_to_all x4, waiting for transfers between devices, exchange(): return lax.all_to_all(array, axis, split_axis=0, concat_axis=0, tiled=True)  70.6 us
    ppermute x13, waiting for transfers between devices, send(): return lax.ppermute(array, ('space', 'tm'), permutation(move))  43.5 us
    all_to_all x4, starting transfers between devices, exchange(): return lax.all_to_all(array, axis, split_axis=0, concat_axis=0, tiled=True)  28.4 us
    ppermute x13, starting transfers between devices, send(): return lax.ppermute(array, ('space', 'tm'), permutation(move))  22.9 us
    unnamed x44, local copies, waits for them, and re-layouts  10.4 us
    pallas_call x1, Pallas kernels, space_attention(): call(space_kernel, jax.ShapeDtypeStruct((16, 3, 2, 64, 128), BF16), 5 * (...  9.37 us
    pallas_call x1, Pallas kernels, time_attention(): call(time_kernel, jax.ShapeDtypeStruct((16, 3, 2, 64, 128), BF16), 5 * (1...  5.43 us
    pallas_call x1, Pallas kernels, space_proj(): call(space_proj_kernel, (shape, shape), 1 << 30, 6 << 20, in_specs=[SCALA...  5.21 us
  transfers between devices with their start and end apart: 20, of which 9 were waited for; matrix products, arithmetic and copies ran while one was open for 0% of the time, Pallas kernels for 14%

profile of v4, /device:TPU:38, one launch (start us, length us, event | category | flops | bytes accessed | tf_op | source)
XLA Modules:
  0.0 215.5 jit_solution(1298072293035957271)
XLA Ops:
  0.6 3.8 %shard_map.146 = bf16[16,3,128,128]{3,2,1,0:T(8,128)(2,1)} custom-call(bf16[128,2048]{1,0:T(8,128)(2,1)} %bitcast.64, bf16[128,2048]{1,0:T(8,128)(2,1)} %bitcast.65, bf16[128,2048]{1,0:T(8,128)(2,1)} %bitcast.66), custom_call_target="tpu_custom_call" | custom-call | bytes 3145728 | tf_op jit(solution)/shard_map/pallas_call | solution.py:80
  4.4 8.8 %all-to-all-start = ((bf16[16,3,2,64,128]{4,3,2,1,0:T(8,128)(2,1)}), bf16[16,3,2,64,128]{4,3,2,1,0:T(8,128)(2,1)}, u32[]{:S(2)}, u32[]{:S(2)}) async-start(bf16[16,3,2,64,128]{4,3,2,1,0:T(8,128)(2,1)} %bitcast.63), calls=%async_computation | async-start | bytes 3145728 | tf_op jit(solution)/shard_map/all_to_all | solution.py:308
  13.2 0.0 copy-start.10
  13.3 0.9 collective-permute-start.2
  14.2 1.1 collective-permute-start.3
  15.3 2.8 %collective-permute-start.4 = (bf16[128,2048]{1,0:T(8,128)(2,1)S(1)}, bf16[128,2048]{1,0:T(8,128)(2,1)}, u32[]{:S(2)}, u32[]{:S(2)}) collective-permute-start(bf16[128,2048]{1,0:T(8,128)(2,1)S(1)} %bitcast.52), channel_id=1, source_target_pairs={{0,96},{1,97},{2,98},{3,99},{4,100},{5,101},{6,102},{7,103},{8,104... | collective-permute-start | bytes 1572872 | tf_op jit(solution)/shard_map/ppermute | solution.py:34
  18.0 0.1 add_convert_fusion
  18.2 1.6 collective-permute-start.5
  19.7 0.1 pad_add_fusion.at_ref
  19.8 0.8 shard_map.147
  20.6 4.6 %collective-permute-start = (bf16[96,2048]{1,0:T(8,128)(2,1)S(1)}, bf16[96,2048]{1,0:T(8,128)(2,1)S(1)}, u32[]{:S(2)}, u32[]{:S(2)}) collective-permute-start(bf16[96,2048]{1,0:T(8,128)(2,1)S(1)} %get-tuple-element.32), channel_id=1, source_target_pairs={{0,136},{1,137},{2,138},{3,139},{4,140},{5,141},{6,142},{7,143},{8... | collective-permute-start | bytes 1179656 | tf_op jit(solution)/shard_map/ppermute | solution.py:34
  25.2 3.0 %collective-permute-done.2.b_ref = bf16[128,2048]{1,0:T(8,128)(2,1)S(1)} collective-permute-done((bf16[128,2048]{1,0:T(8,128)(2,1)S(1)}, bf16[128,2048]{1,0:T(8,128)(2,1)S(1)}, u32[]{:S(2)}, u32[]{:S(2)}) %collective-permute-start.2) | collective-permute-done | bytes 524320 | tf_op jit(solution)/shard_map/ppermute | solution.py:34
  28.2 0.8 copy-done.17
  29.0 1.5 collective-permute-start.1
  30.5 7.3 %collective-permute-done.3.c_ref = bf16[128,2048]{1,0:T(8,128)(2,1)} collective-permute-done((bf16[128,2048]{1,0:T(8,128)(2,1)S(1)}, bf16[128,2048]{1,0:T(8,128)(2,1)}, u32[]{:S(2)}, u32[]{:S(2)}) %collective-permute-start.3) | collective-permute-done | bytes 524320 | tf_op jit(solution)/shard_map/ppermute | solution.py:34
  37.8 2.6 %collective-permute-done.4.d_ref = bf16[128,2048]{1,0:T(8,128)(2,1)} collective-permute-done((bf16[128,2048]{1,0:T(8,128)(2,1)S(1)}, bf16[128,2048]{1,0:T(8,128)(2,1)}, u32[]{:S(2)}, u32[]{:S(2)}) %collective-permute-start.4) | collective-permute-done | bytes 524320 | tf_op jit(solution)/shard_map/ppermute | solution.py:34
  40.4 1.0 copy-done.7
  41.4 1.0 copy-done.18
  42.5 1.5 shard_map.149.refs_0_
  43.9 0.1 collective-permute-start.6
  44.0 0.1 copy-done.16
  44.1 0.3 shard_map.145
  44.4 1.2 copy-done
  45.6 4.9 %collective-permute-done.1.rows_ref = bf16[64,2048]{1,0:T(8,128)(2,1)S(1)} collective-permute-done((bf16[64,2048]{1,0:T(8,128)(2,1)S(1)}, bf16[64,2048]{1,0:T(8,128)(2,1)S(1)}, u32[]{:S(2)}, u32[]{:S(2)}) %collective-permute-start.1) | collective-permute-done | bytes 262176 | tf_op jit(solution)/shard_map/ppermute | solution.py:34
  50.5 0.0 collective-permute-done.both_ref
  50.5 0.0 copy-start.12
  50.5 0.0 collective-permute-done.5.refs_2_.refs_1_
  50.6 0.7 copy-done.12
  51.2 0.0 all-to-all-done.qkv_ref
  51.2 9.2 %all-to-all-start.1 = ((bf16[16,3,2,64,128]{4,3,2,1,0:T(8,128)(2,1)}), bf16[16,3,2,64,128]{4,3,2,1,0:T(8,128)(2,1)}, u32[]{:S(2)}, u32[]{:S(2)}) async-start(bf16[16,3,2,64,128]{4,3,2,1,0:T(8,128)(2,1)} %bitcast.43), calls=%async_computation.1 | async-start | bytes 3145728 | tf_op jit(solution)/shard_map/all_to_all | solution.py:308
  60.5 3.0 %collective-permute-start.8 = (bf16[128,2048]{1,0:T(8,128)(2,1)S(1)}, bf16[128,2048]{1,0:T(8,128)(2,1)S(1)}, u32[]{:S(2)}, u32[]{:S(2)}) collective-permute-start(bf16[128,2048]{1,0:T(8,128)(2,1)S(1)} %bitcast.47), channel_id=1, source_target_pairs={{0,2},{1,3},{2,0},{3,1},{4,6},{5,7},{6,4},{7,5},{8,10},{9,11},{10,... | collective-permute-start | bytes 1572872 | tf_op jit(solution)/shard_map/ppermute | solution.py:34
  63.5 1.2 collective-permute-start.10
  64.7 0.9 collective-permute-start.11
  65.5 0.0 collective-permute-start.7
  65.5 0.1 pad_add_fusion.1.at_ref
  65.6 11.2 %collective-permute-done.8.refs_5_.refs_2_ = bf16[128,2048]{1,0:T(8,128)(2,1)S(1)} collective-permute-done((bf16[128,2048]{1,0:T(8,128)(2,1)S(1)}, bf16[128,2048]{1,0:T(8,128)(2,1)S(1)}, u32[]{:S(2)}, u32[]{:S(2)}) %collective-permute-start.8) | collective-permute-done | bytes 524320 | tf_op jit(solution)/shard_map/ppermute | solution.py:34
  76.8 4.9 %collective-permute-done.7.refs_4_ = bf16[64,2048]{1,0:T(8,128)(2,1)S(1)} collective-permute-done((bf16[64,2048]{1,0:T(8,128)(2,1)}, bf16[64,2048]{1,0:T(8,128)(2,1)S(1)}, u32[]{:S(2)}, u32[]{:S(2)}) %collective-permute-start.7) | collective-permute-done | bytes 262176 | tf_op jit(solution)/shard_map/ppermute | solution.py:34
  81.7 1.0 copy-done.11
  82.7 0.9 copy-done.13
  83.7 5.2 %shard_map.151 = (bf16[8,128,128]{2,1,0:T(8,128)(2,1)S(1)}, bf16[8,128,128]{2,1,0:T(8,128)(2,1)}) custom-call(s32[2]{0:T(128)S(1)} %pad_add_fusion.1.at_ref, bf16[4,128,2048]{2,1,0:T(8,128)(2,1)S(1)} %shard_map.149.refs_0_, bf16[4,128,2048]{2,1,0:T(8,128)(2,1)} %collective-permute-done.6.refs_1_, bf16[128,2048]{1,0:T(8,128)(2,1)S(1)} %copy-done.11, ...), custom_call_target="tpu_custom_call" | custom-call | flops 1073741824 | bytes 6291456 | tf_op jit(solution)/shard_map/pallas_call | solution.py:194
  88.9 0.0 copy-start.9
  88.9 0.0 collective-permute-done.11.b_ref
  88.9 0.1 shard_map.152.refs_5_
  89.0 0.6 copy-done.19
  89.6 0.8 copy-done.4
  90.4 5.4 %collective-permute-start.9 = (bf16[8,128,128]{2,1,0:T(8,128)(2,1)}, bf16[8,128,128]{2,1,0:T(8,128)(2,1)S(1)}, u32[]{:S(2)}, u32[]{:S(2)}) collective-permute-start(bf16[8,128,128]{2,1,0:T(8,128)(2,1)} %get-tuple-element.39), channel_id=1, source_target_pairs={{0,128},{1,129},{2,130},{3,131},{4,132},{5,133},{6,134},{7,135},{8... | collective-permute-start | bytes 786440 | tf_op jit(solution)/shard_map/ppermute | solution.py:34
  95.8 0.1 pad_add_fusion.2.at_ref
  95.8 0.0 copy-start.5
  95.9 1.0 copy-done.5
  96.9 5.0 %shard_map.153 = (bf16[4,128,128]{2,1,0:T(8,128)(2,1)S(1)}, bf16[4,128,128]{2,1,0:T(8,128)(2,1)}, bf16[4,128,128]{2,1,0:T(8,128)(2,1)}, bf16[4,128,128]{2,1,0:T(8,128)(2,1)}) custom-call(s32[2]{0:T(128)S(1)} %pad_add_fusion.2.at_ref, bf16[128,2048]{1,0:T(8,128)(2,1)S(1)} %bitcast.49, bf16[128,2048]{1,0:T(8,128)(2,1)S(1)} %collective-permute-done.5.refs_2_.refs_1_, ...), custom_call_target="tpu_custom_call" | custom-call | flops 1073741824 | bytes 5242880 | tf_op jit(solution)/shard_map/pallas_call | solution.py:222
  101.9 1.6 collective-permute-start.13
  103.4 1.7 collective-permute-start.14
  105.1 0.7 collective-permute-start.15
  105.8 9.6 %collective-permute-done.9 = bf16[8,128,128]{2,1,0:T(8,128)(2,1)S(1)} collective-permute-done((bf16[8,128,128]{2,1,0:T(8,128)(2,1)}, bf16[8,128,128]{2,1,0:T(8,128)(2,1)S(1)}, u32[]{:S(2)}, u32[]{:S(2)}) %collective-permute-start.9) | collective-permute-done | bytes 262176 | tf_op jit(solution)/shard_map/ppermute | solution.py:34
  115.4 9.4 %shard_map.154 = bf16[16,3,2,64,128]{4,3,2,1,0:T(8,128)(2,1)} custom-call(s32[1]{0:T(128)} %bitcast.pos_ref, bf16[16,3,2,64,128]{4,3,2,1,0:T(8,128)(2,1)} %all-to-all-done.1.qkv_ref, bf16[8,2,64,128]{3,2,1,0:T(8,128)(2,1)S(1)} %bitcast.57, bf16[8,2,64,128]{3,2,1,0:T(8,128)(2,1)S(1)} %bitcast.62, bf16[4,128,128]{2,1,0:T(8,128)(2,1)S(1)} %get-tuple-element.46.after_ref), custom_call_target="tpu_custom_call" | custom-call | flops 2684354560 | bytes 4194304 | tf_op jit(solution)/shard_map/pallas_call | solution.py:261
  124.8 0.0 collective-permute-done.13
  124.8 5.0 %all-to-all-start.2 = ((bf16[16,3,2,64,128]{4,3,2,1,0:T(8,128)(2,1)}), bf16[16,3,2,64,128]{4,3,2,1,0:T(8,128)(2,1)S(1)}, u32[]{:S(2)}, u32[]{:S(2)}) async-start(bf16[16,3,2,64,128]{4,3,2,1,0:T(8,128)(2,1)} %shard_map.154), calls=%async_computation.2 | async-start | bytes 3145728 | tf_op jit(solution)/shard_map/all_to_all | solution.py:308
  129.9 5.4 %shard_map.155 = bf16[16,3,2,64,128]{4,3,2,1,0:T(8,128)(2,1)S(1)} custom-call(s32[1]{0:T(128)} %bitcast.18.pos_ref, bf16[16,3,2,64,128]{4,3,2,1,0:T(8,128)(2,1)} %all-to-all-done.qkv_ref, bf16[4,2,64,128]{3,2,1,0:T(8,128)(2,1)S(1)} %bitcast.58, bf16[4,2,64,128]{3,2,1,0:T(8,128)(2,1)S(1)} %bitcast.59, bf16[4,2,64,128]{3,2,1,0:T(8,128)(2,1)S(1)} %bitcast.60, ...), custom_call_target="tpu_custom_call" | custom-call | flops 671088640 | bytes 4194304 | tf_op jit(solution)/shard_map/pallas_call | solution.py:295
  135.3 1.1 copy-done.1
  136.5 35.2 %all-to-all-done.2 = bf16[16,3,2,64,128]{4,3,2,1,0:T(8,128)(2,1)S(1)} async-done(((bf16[16,3,2,64,128]{4,3,2,1,0:T(8,128)(2,1)}), bf16[16,3,2,64,128]{4,3,2,1,0:T(8,128)(2,1)S(1)}, u32[]{:S(2)}, u32[]{:S(2)}) %all-to-all-start.2) | async-done | bytes 1572896 | tf_op jit(solution)/shard_map/all_to_all | solution.py:308
  171.6 5.4 %all-to-all-start.3 = ((bf16[16,3,2,64,128]{4,3,2,1,0:T(8,128)(2,1)}), bf16[16,3,2,64,128]{4,3,2,1,0:T(8,128)(2,1)S(1)}, u32[]{:S(2)}, u32[]{:S(2)}) async-start(bf16[16,3,2,64,128]{4,3,2,1,0:T(8,128)(2,1)} %copy-done.1), calls=%async_computation.3 | async-start | bytes 3145728 | tf_op jit(solution)/shard_map/all_to_all | solution.py:308
  177.0 1.5 shard_map.156
  178.5 35.5 %all-to-all-done.3 = bf16[16,3,2,64,128]{4,3,2,1,0:T(8,128)(2,1)S(1)} async-done(((bf16[16,3,2,64,128]{4,3,2,1,0:T(8,128)(2,1)}), bf16[16,3,2,64,128]{4,3,2,1,0:T(8,128)(2,1)S(1)}, u32[]{:S(2)}, u32[]{:S(2)}) %all-to-all-start.3) | async-done | bytes 1572896 | tf_op jit(solution)/shard_map/all_to_all | solution.py:308
  214.0 1.5 shard_map.157
  (37 shorter events, 0.1 us)
Async XLA Ops:
  4.4 8.8 %copy-start.6 = (bf16[2,1,64,2048]{3,2,1,0:T(8,128)(2,1)S(1)}, bf16[2,1,64,2048]{3,2,1,0:T(8,128)(2,1)}, u32[]{:S(2)}) copy-start(bf16[2,1,64,2048]{3,2,1,0:T(8,128)(2,1)} %param.16) | copy-start | bytes 1572868
  4.4 13.6 %copy-start.21 = (bf16[2,1,64,2048]{3,2,1,0:T(8,128)(2,1)S(1)}, bf16[2,1,64,2048]{3,2,1,0:T(8,128)(2,1)}, u32[]{:S(2)}) copy-start(bf16[2,1,64,2048]{3,2,1,0:T(8,128)(2,1)} %param.17) | copy-start | bytes 1572868
  4.4 46.8 %all-to-all-start = ((bf16[16,3,2,64,128]{4,3,2,1,0:T(8,128)(2,1)}), bf16[16,3,2,64,128]{4,3,2,1,0:T(8,128)(2,1)}, u32[]{:S(2)}, u32[]{:S(2)}) async-start(bf16[16,3,2,64,128]{4,3,2,1,0:T(8,128)(2,1)} %bitcast.63), calls=%async_computation | async-start | bytes 3145728 | tf_op jit(solution)/shard_map/all_to_all | solution.py:308
  13.2 6.6 %copy-start.2 = (bf16[128,2048]{1,0:T(8,128)(2,1)S(1)}, bf16[128,2048]{1,0:T(8,128)(2,1)}, u32[]{:S(2)}) copy-start(bf16[128,2048]{1,0:T(8,128)(2,1)} %refs_4_.1) | copy-start | bytes 1572868
  13.2 6.6 %copy-start.10 = (bf16[128,2048]{1,0:T(8,128)(2,1)S(1)}, bf16[128,2048]{1,0:T(8,128)(2,1)}, u32[]{:S(2)}) copy-start(bf16[128,2048]{1,0:T(8,128)(2,1)} %refs_2_.1) | copy-start | bytes 1572868
  13.3 15.0 %collective-permute-start.2 = (bf16[128,2048]{1,0:T(8,128)(2,1)S(1)}, bf16[128,2048]{1,0:T(8,128)(2,1)S(1)}, u32[]{:S(2)}, u32[]{:S(2)}) collective-permute-start(bf16[128,2048]{1,0:T(8,128)(2,1)S(1)} %bitcast.50), channel_id=1, source_target_pairs={{0,32},{1,33},{2,34},{3,35},{4,36},{5,37},{6,38},{7,39},{8,40},{9,... | collective-permute-start | bytes 1572872 | tf_op jit(solution)/shard_map/ppermute | solution.py:34
  14.2 23.6 %collective-permute-start.3 = (bf16[128,2048]{1,0:T(8,128)(2,1)S(1)}, bf16[128,2048]{1,0:T(8,128)(2,1)}, u32[]{:S(2)}, u32[]{:S(2)}) collective-permute-start(bf16[128,2048]{1,0:T(8,128)(2,1)S(1)} %bitcast.51), channel_id=1, source_target_pairs={{0,64},{1,65},{2,66},{3,67},{4,68},{5,69},{6,70},{7,71},{8,72},{9,... | collective-permute-start | bytes 1572872 | tf_op jit(solution)/shard_map/ppermute | solution.py:34
  15.3 25.1 %collective-permute-start.4 = (bf16[128,2048]{1,0:T(8,128)(2,1)S(1)}, bf16[128,2048]{1,0:T(8,128)(2,1)}, u32[]{:S(2)}, u32[]{:S(2)}) collective-permute-start(bf16[128,2048]{1,0:T(8,128)(2,1)S(1)} %bitcast.52), channel_id=1, source_target_pairs={{0,96},{1,97},{2,98},{3,99},{4,100},{5,101},{6,102},{7,103},{8,104... | collective-permute-start | bytes 1572872 | tf_op jit(solution)/shard_map/ppermute | solution.py:34
  18.2 32.4 %collective-permute-start.5 = (bf16[128,2048]{1,0:T(8,128)(2,1)S(1)}, bf16[128,2048]{1,0:T(8,128)(2,1)S(1)}, u32[]{:S(2)}, u32[]{:S(2)}) collective-permute-start(bf16[128,2048]{1,0:T(8,128)(2,1)S(1)} %bitcast.46), channel_id=1, source_target_pairs={{0,1},{1,0},{2,3},{3,2},{4,5},{5,4},{6,7},{7,6},{8,9},{9,8},{10,11... | collective-permute-start | bytes 1572872 | tf_op jit(solution)/shard_map/ppermute | solution.py:34
  20.6 29.9 %collective-permute-start = (bf16[96,2048]{1,0:T(8,128)(2,1)S(1)}, bf16[96,2048]{1,0:T(8,128)(2,1)S(1)}, u32[]{:S(2)}, u32[]{:S(2)}) collective-permute-start(bf16[96,2048]{1,0:T(8,128)(2,1)S(1)} %get-tuple-element.32), channel_id=1, source_target_pairs={{0,136},{1,137},{2,138},{3,139},{4,140},{5,141},{6,142},{7,143},{8... | collective-permute-start | bytes 1179656 | tf_op jit(solution)/shard_map/ppermute | solution.py:34
  28.2 0.8 copy-start.17
  29.0 21.5 %collective-permute-start.1 = (bf16[64,2048]{1,0:T(8,128)(2,1)S(1)}, bf16[64,2048]{1,0:T(8,128)(2,1)S(1)}, u32[]{:S(2)}, u32[]{:S(2)}) collective-permute-start(bf16[64,2048]{1,0:T(8,128)(2,1)S(1)} %get-tuple-element.33), channel_id=1, source_target_pairs={{0,4},{1,5},{2,6},{3,7},{4,8},{5,9},{6,10},{7,11},{8,12},{9,13},{1... | collective-permute-start | bytes 786440 | tf_op jit(solution)/shard_map/ppermute | solution.py:34
  40.4 1.0 copy-start.7
  41.4 1.0 copy-start.18
  42.5 1.6 copy-start.14
  42.5 1.6 copy-start.15
  42.5 1.7 copy-start.16
  43.9 37.8 %collective-permute-start.6 = (bf16[4,128,2048]{2,1,0:T(8,128)(2,1)S(1)}, bf16[4,128,2048]{2,1,0:T(8,128)(2,1)}, u32[]{:S(2)}, u32[]{:S(2)}) collective-permute-start(bf16[4,128,2048]{2,1,0:T(8,128)(2,1)S(1)} %shard_map.149.refs_0_), channel_id=1, source_target_pairs={{0,16},{1,17},{2,18},{3,19},{4,20},{5,21},{6,22},{7,23},{8,24},{9,... | collective-permute-start | bytes 6291464 | tf_op jit(solution)/shard_map/ppermute | solution.py:34
  44.4 1.2 copy-start
  50.5 0.7 copy-start.12
  51.2 64.2 %all-to-all-start.1 = ((bf16[16,3,2,64,128]{4,3,2,1,0:T(8,128)(2,1)}), bf16[16,3,2,64,128]{4,3,2,1,0:T(8,128)(2,1)}, u32[]{:S(2)}, u32[]{:S(2)}) async-start(bf16[16,3,2,64,128]{4,3,2,1,0:T(8,128)(2,1)} %bitcast.43), calls=%async_computation.1 | async-start | bytes 3145728 | tf_op jit(solution)/shard_map/all_to_all | solution.py:308
  60.5 16.3 %collective-permute-start.8 = (bf16[128,2048]{1,0:T(8,128)(2,1)S(1)}, bf16[128,2048]{1,0:T(8,128)(2,1)S(1)}, u32[]{:S(2)}, u32[]{:S(2)}) collective-permute-start(bf16[128,2048]{1,0:T(8,128)(2,1)S(1)} %bitcast.47), channel_id=1, source_target_pairs={{0,2},{1,3},{2,0},{3,1},{4,6},{5,7},{6,4},{7,5},{8,10},{9,11},{10,... | collective-permute-start | bytes 1572872 | tf_op jit(solution)/shard_map/ppermute | solution.py:34
  63.5 25.4 %collective-permute-start.10 = (bf16[128,2048]{1,0:T(8,128)(2,1)S(1)}, bf16[128,2048]{1,0:T(8,128)(2,1)S(1)}, u32[]{:S(2)}, u32[]{:S(2)}) collective-permute-start(bf16[128,2048]{1,0:T(8,128)(2,1)S(1)} %bitcast.48), channel_id=1, source_target_pairs={{0,3},{1,2},{2,1},{3,0},{4,7},{5,6},{6,5},{7,4},{8,11},{9,10},{10,... | collective-permute-start | bytes 1572872 | tf_op jit(solution)/shard_map/ppermute | solution.py:34
  64.7 24.3 %collective-permute-start.11 = (bf16[96,2048]{1,0:T(8,128)(2,1)S(1)}, bf16[96,2048]{1,0:T(8,128)(2,1)S(1)}, u32[]{:S(2)}, u32[]{:S(2)}) collective-permute-start(bf16[96,2048]{1,0:T(8,128)(2,1)S(1)} %get-tuple-element.35.refs_1_.a_ref), channel_id=1, source_target_pairs={{0,32},{1,33},{2,34},{3,35},{4,36},{5,37},{6,38},{7,39},{8,40},{9,... | collective-permute-start | bytes 1179656 | tf_op jit(solution)/shard_map/ppermute | solution.py:34
  65.5 16.2 %collective-permute-start.7 = (bf16[64,2048]{1,0:T(8,128)(2,1)}, bf16[64,2048]{1,0:T(8,128)(2,1)S(1)}, u32[]{:S(2)}, u32[]{:S(2)}) collective-permute-start(bf16[64,2048]{1,0:T(8,128)(2,1)} %copy-done.12), channel_id=1, source_target_pairs={{0,1},{1,0},{2,3},{3,2},{4,5},{5,4},{6,7},{7,6},{8,9},{9,8},{10,11... | collective-permute-start | bytes 786440 | tf_op jit(solution)/shard_map/ppermute | solution.py:34
  76.8 12.1 %copy-start.8 = (bf16[128,2048]{1,0:T(8,128)(2,1)}, bf16[128,2048]{1,0:T(8,128)(2,1)S(1)}, u32[]{:S(2)}) copy-start(bf16[128,2048]{1,0:T(8,128)(2,1)S(1)} %collective-permute-done.8.refs_5_.refs_2_) | copy-start | bytes 1572868
  81.7 1.0 copy-start.11
  82.7 0.9 copy-start.13
  88.9 0.7 copy-start.19
  88.9 6.9 %copy-start.3 = (bf16[128,2048]{1,0:T(8,128)(2,1)S(1)}, bf16[128,2048]{1,0:T(8,128)(2,1)}, u32[]{:S(2)}) copy-start(bf16[128,2048]{1,0:T(8,128)(2,1)} %refs_4_.1) | copy-start | bytes 1572868
  88.9 6.9 %copy-start.9 = (bf16[128,2048]{1,0:T(8,128)(2,1)S(1)}, bf16[128,2048]{1,0:T(8,128)(2,1)}, u32[]{:S(2)}) copy-start(bf16[128,2048]{1,0:T(8,128)(2,1)} %copy-done.8) | copy-start | bytes 1572868
  89.6 0.8 copy-start.4
  90.4 5.4 %collective-permute-start.12 = (bf16[2,96,2048]{2,1,0:T(8,128)(2,1)S(1)}, bf16[2,96,2048]{2,1,0:T(8,128)(2,1)}, u32[]{:S(2)}, u32[]{:S(2)}) collective-permute-start(bf16[2,96,2048]{2,1,0:T(8,128)(2,1)S(1)} %shard_map.152.refs_5_), channel_id=1, source_target_pairs={{0,16},{1,17},{2,18},{3,19},{4,20},{5,21},{6,22},{7,23},{8,24},{9,... | collective-permute-start | bytes 2359304 | tf_op jit(solution)/shard_map/ppermute | solution.py:34
  90.4 25.0 %collective-permute-start.9 = (bf16[8,128,128]{2,1,0:T(8,128)(2,1)}, bf16[8,128,128]{2,1,0:T(8,128)(2,1)S(1)}, u32[]{:S(2)}, u32[]{:S(2)}) collective-permute-start(bf16[8,128,128]{2,1,0:T(8,128)(2,1)} %get-tuple-element.39), channel_id=1, source_target_pairs={{0,128},{1,129},{2,130},{3,131},{4,132},{5,133},{6,134},{7,135},{8... | collective-permute-start | bytes 786440 | tf_op jit(solution)/shard_map/ppermute | solution.py:34
  95.8 1.0 copy-start.5
  96.9 18.6 %copy-start.20 = (bf16[8,128,128]{2,1,0:T(8,128)(2,1)S(1)}, bf16[8,128,128]{2,1,0:T(8,128)(2,1)}, u32[]{:S(2)}) copy-start(bf16[8,128,128]{2,1,0:T(8,128)(2,1)} %copy-done.19) | copy-start | bytes 786436
  101.9 23.0 %collective-permute-start.13 = (bf16[4,128,128]{2,1,0:T(8,128)(2,1)}, bf16[4,128,128]{2,1,0:T(8,128)(2,1)S(1)}, u32[]{:S(2)}, u32[]{:S(2)}) collective-permute-start(bf16[4,128,128]{2,1,0:T(8,128)(2,1)} %get-tuple-element.41), channel_id=1, source_target_pairs={{0,4},{1,5},{2,6},{3,7},{4,8},{5,9},{6,10},{7,11},{8,12},{9,13},{1... | collective-permute-start | bytes 393224 | tf_op jit(solution)/shard_map/ppermute | solution.py:363
  103.4 21.4 %collective-permute-start.14 = (bf16[4,128,128]{2,1,0:T(8,128)(2,1)}, bf16[4,128,128]{2,1,0:T(8,128)(2,1)S(1)}, u32[]{:S(2)}, u32[]{:S(2)}) collective-permute-start(bf16[4,128,128]{2,1,0:T(8,128)(2,1)} %get-tuple-element.42), channel_id=1, source_target_pairs={{0,8},{1,9},{2,10},{3,11},{4,12},{5,13},{6,14},{7,15},{8,0},{9,1},... | collective-permute-start | bytes 393224 | tf_op jit(solution)/shard_map/ppermute | solution.py:363
  105.1 19.7 %collective-permute-start.15 = (bf16[4,128,128]{2,1,0:T(8,128)(2,1)}, bf16[4,128,128]{2,1,0:T(8,128)(2,1)S(1)}, u32[]{:S(2)}, u32[]{:S(2)}) collective-permute-start(bf16[4,128,128]{2,1,0:T(8,128)(2,1)} %get-tuple-element.43), channel_id=1, source_target_pairs={{0,12},{1,13},{2,14},{3,15},{4,0},{5,1},{6,2},{7,3},{8,4},{9,5},{1... | collective-permute-start | bytes 393224 | tf_op jit(solution)/shard_map/ppermute | solution.py:363
  124.8 46.8 %all-to-all-start.2 = ((bf16[16,3,2,64,128]{4,3,2,1,0:T(8,128)(2,1)}), bf16[16,3,2,64,128]{4,3,2,1,0:T(8,128)(2,1)S(1)}, u32[]{:S(2)}, u32[]{:S(2)}) async-start(bf16[16,3,2,64,128]{4,3,2,1,0:T(8,128)(2,1)} %shard_map.154), calls=%async_computation.2 | async-start | bytes 3145728 | tf_op jit(solution)/shard_map/all_to_all | solution.py:308
  135.3 1.1 copy-start.1
  171.6 42.4 %all-to-all-start.3 = ((bf16[16,3,2,64,128]{4,3,2,1,0:T(8,128)(2,1)}), bf16[16,3,2,64,128]{4,3,2,1,0:T(8,128)(2,1)S(1)}, u32[]{:S(2)}, u32[]{:S(2)}) async-start(bf16[16,3,2,64,128]{4,3,2,1,0:T(8,128)(2,1)} %copy-done.1), calls=%async_computation.3 | async-start | bytes 3145728 | tf_op jit(solution)/shard_map/all_to_all | solution.py:308
